TPU v7x, 128 devices: a whole 4x4x4 slice. The times are simulated.
128 devices in a mesh: grp: 4 (over z), fsdp: 32 (over y, x, core).
Axes of the slice: x: 4, y: 4, z: 4, core: 2. Of those that a mesh axis runs over, the one named last changes fastest.
Arguments:
- ids: int32 [128, 256], P(('grp', 'fsdp')), may hold values from 0 to 30719
- lengths: int32 [128], P(('grp', 'fsdp')), may hold values from 1 to 256, as said below
- picks: int32 [128, 64], P(('grp', 'fsdp')), may hold values from 0 to 255, as said below
- labels: int32 [128, 64], P(('grp', 'fsdp')), may hold values from 0 to 30719
- s_table: float32 [30720, 512], P('fsdp')
- s_pos: float32 [256, 512], P('fsdp'), may hold values from -0.25 to 0.25
- s_qkv: float32 [512, 1536], P('fsdp'), may hold values from -0.25 to 0.25
- s_out: float32 [512, 512], P('fsdp'), may hold values from -1 to 1
- s_up: float32 [512, 2048], P('fsdp'), may hold values from -0.25 to 0.25
- s_down: float32 [2048, 512], P('fsdp'), may hold values from -0.125 to 0.125
- s_norms: float32 [512, 6], P('fsdp')
- m_table: float32 [30720, 512], P('fsdp'), may hold values from -1.4305115e-06 to 1.4305115e-06
- m_pos: float32 [256, 512], P('fsdp'), may hold values from -1.4305115e-06 to 1.4305115e-06
- m_qkv: float32 [512, 1536], P('fsdp'), may hold values from -1.4305115e-06 to 1.4305115e-06
- m_out: float32 [512, 512], P('fsdp'), may hold values from -1.4305115e-06 to 1.4305115e-06
- m_up: float32 [512, 2048], P('fsdp'), may hold values from -1.4305115e-06 to 1.4305115e-06
- m_down: float32 [2048, 512], P('fsdp'), may hold values from -1.4305115e-06 to 1.4305115e-06
- m_norms: float32 [512, 6], P('fsdp'), may hold values from -5.722046e-06 to 5.722046e-06
- a_table: float32 [30720, 512], P('fsdp'), may hold values from -0.25 to 0.25
- a_pos: float32 [256, 512], P('fsdp'), may hold values from -0.25 to 0.25
- a_qkv: float32 [512, 1536], P('fsdp'), may hold values from -0.25 to 0.25
- a_out: float32 [512, 512], P('fsdp'), may hold values from -0.25 to 0.25
- a_up: float32 [512, 2048], P('fsdp'), may hold values from -0.25 to 0.25
- a_down: float32 [2048, 512], P('fsdp'), may hold values from -0.125 to 0.125
- a_norms: float32 [512, 6], P('fsdp'), may hold values from -3 to 3
- t_table: bfloat16 [4, 30720, 768], P('grp', 'fsdp')
- t_pos: bfloat16 [4, 256, 768], P('grp'), may hold values from -0.21875 to 0.21875
- t_qkv: bfloat16 [4, 768, 2304], P('grp'), may hold values from -0.21875 to 0.21875
- t_out: bfloat16 [4, 768, 768], P('grp'), may hold values from -0.875 to 0.875
- t_up: bfloat16 [4, 768, 3072], P('grp'), may hold values from -0.21875 to 0.21875
- t_down: bfloat16 [4, 3072, 768], P('grp'), may hold values from -0.109375 to 0.109375
- t_norms: bfloat16 [4, 768, 6], P('grp')
Outputs:
- loss_sum: float32 [], replicated
- count: float32 [], replicated
- clip_norm: float32 [], replicated
- new_table: float32 [30720, 512], P('fsdp')
- new_pos: float32 [256, 512], P('fsdp')
- new_qkv: float32 [512, 1536], P('fsdp')
- new_out: float32 [512, 512], P('fsdp')
- new_up: float32 [512, 2048], P('fsdp')
- new_down: float32 [2048, 512], P('fsdp')
- new_norms: float32 [512, 6], P('fsdp')
- mom_table: float32 [30720, 512], P('fsdp')
- mom_pos: float32 [256, 512], P('fsdp')
- mom_qkv: float32 [512, 1536], P('fsdp')
- mom_out: float32 [512, 512], P('fsdp')
- mom_up: float32 [512, 2048], P('fsdp')
- mom_down: float32 [2048, 512], P('fsdp')
- mom_norms: float32 [512, 6], P('fsdp')
- avg_table: float32 [30720, 512], P('fsdp')
- avg_pos: float32 [256, 512], P('fsdp')
- avg_qkv: float32 [512, 1536], P('fsdp')
- avg_out: float32 [512, 512], P('fsdp')
- avg_up: float32 [512, 2048], P('fsdp')
- avg_down: float32 [2048, 512], P('fsdp')
- avg_norms: float32 [512, 6], P('fsdp')
Inputs may be any that keep to these rules, and one draw needn't show every extreme that they name: `lengths`: real tokens of each sequence; the sequence on the last device of fsdp in each teacher group has all 256. `picks`: all different within a row; positions at or beyond the sequence's length don't count.
All inputs are finite; a program needn't handle non-finite values.
Results may differ from a plain program's by a relative error of at most 0.018.
The roundings to bfloat16 on the way count: a program that leaves them out, or rounds other values in their place, can miss the bound.
Values may be sent and summed in bfloat16 or wider, within the bound.
A program may use at most 320 MiB of HBM per device.

v0:
```python
from functools import partial
import functools
import math

import jax
import jax.numpy as jnp
from jax import lax
from jax.sharding import Mesh
from jax.sharding import PartitionSpec as P

HD = 64
FSDP = ("fsdp_0", "fsdp_1", "fsdp_2")
GRP_FSDP = ("grp", "fsdp_0", "fsdp_1", "fsdp_2")


norm_eps = 1e-12
clip_limit = 0.001
learn_rate = 100000.0
momentum_decay = 0.9
average_decay = 0.9


def for_sending(value):
    return jax.tree.map(lambda a: a.astype(jnp.bfloat16) if a.dtype == jnp.float32 else a, value)


def in_one_piece(arrays, axis, dim, along):
    columns = [a.reshape(*a.shape[:along], -1) for a in arrays]
    both = jnp.concatenate(columns, axis=along)
    out, at, finished = (lax.all_gather(both, axis, axis=dim, tiled=True), 0, [])
    for a, column in zip(arrays, columns):
        piece = out[..., at : at + column.shape[along]]
        finished.append(piece.reshape(*piece.shape[:along], *a.shape[along:]))
        at += column.shape[along]
    return tuple(finished)


def in_order(blocks, dim):
    blocks = jnp.moveaxis(blocks, 0, dim)
    dims = blocks.shape
    return blocks.reshape(*dims[:dim], dims[dim] * dims[dim + 1], *dims[dim + 2 :])


def from_everyone(value, axis):
    copies = jnp.broadcast_to(value, (lax.axis_size(axis), *value.shape))
    return lax.all_to_all(copies, axis, split_axis=0, concat_axis=0, tiled=True)


def gathered_copies(value, axis, dim):
    return in_order(from_everyone(value, axis), dim)


def side_by_side(arrays, axis, dim, along):
    widths = [math.prod(a.shape[along:]) for a in arrays]
    both = jnp.concatenate(
        [a.reshape(*a.shape[:along], w) for a, w in zip(arrays, widths)], axis=along
    )
    out = lax.psum_scatter(both, axis, scatter_dimension=dim, tiled=True)
    blocks = jnp.split(out, [sum(widths[:k]) for k in range(1, len(widths))], axis=along)
    return tuple((b.reshape(*out.shape[:along], *a.shape[along:]) for a, b in zip(arrays, blocks)))


def over_axes(value, axes):
    return functools.reduce(lax.psum, axes, value)


def of_everyone(value, axis):
    return from_everyone(value, axis).sum(axis=0)


def layer_norm(value, gain, shift):
    mean = jnp.mean(value, -1, keepdims=True)
    centred = value - mean
    var = jnp.mean(centred * centred, -1, keepdims=True)
    return centred * lax.rsqrt(var + norm_eps) * gain + shift


def norm_back(value, gain, shift, grad):
    _, pull = jax.vjp(layer_norm, value, gain, shift)
    return pull(grad)


def project(left, right):
    return jnp.einsum("blk,kn->bln", left, right, preferred_element_type=jnp.float32)


def project_back(grad, right):
    return jnp.einsum("bln,kn->blk", grad, right, preferred_element_type=jnp.float32)


def weight_grad(left, grad):
    return jnp.einsum("blk,bln->kn", left, grad, preferred_element_type=jnp.float32)


def split_heads(packed, width):
    batch, span = (packed.shape[0], packed.shape[1])
    return [
        packed[:, :, piece * width : (piece + 1) * width].reshape(batch, span, width // HD, HD)
        for piece in range(3)
    ]


def masked_scores(query, keyed, lengths):
    scores = jnp.einsum(
        "bqhd,bkhd->bhqk", query, keyed, preferred_element_type=jnp.float32
    ) * HD ** (-0.5)
    valid = jnp.arange(query.shape[1])[None, :] < lengths[:, None]
    return jnp.where(valid[:, None, None, :], scores, -1e30)


def forward(ids, lengths, weights):
    table, positions, w_qkv, w_out, w_up, w_down, norms = weights
    norms = norms.astype(jnp.float32)
    width = table.shape[1]
    embedded = (
        jnp.take(table, ids, axis=0).astype(jnp.float32) + positions.astype(jnp.float32)[None]
    )
    first = layer_norm(embedded, norms[:, 0], norms[:, 1])
    first_low = first.astype(jnp.bfloat16)
    packed = project(first_low, w_qkv).astype(jnp.bfloat16)
    query, keyed, valued = split_heads(packed, width)
    scores = masked_scores(query, keyed, lengths)
    top = jnp.max(scores, -1, keepdims=True)
    total = jnp.sum(jnp.exp(scores - top), -1, keepdims=True)
    probs = (jnp.exp(scores - top) / total).astype(jnp.bfloat16)
    context = jnp.einsum("bhqk,bkhd->bqhd", probs, valued, preferred_element_type=jnp.float32)
    context = context.reshape(first.shape).astype(jnp.bfloat16)
    joined = first + project(context, w_out)
    second = layer_norm(joined, norms[:, 2], norms[:, 3])
    second_low = second.astype(jnp.bfloat16)
    hidden_pre = project(second_low, w_up)
    active = jax.nn.gelu(hidden_pre, approximate=False).astype(jnp.bfloat16)
    summed = second + project(active, w_down)
    final = layer_norm(summed, norms[:, 4], norms[:, 5])
    saved = (
        embedded,
        first_low,
        packed,
        top,
        total,
        context,
        joined,
        second_low,
        hidden_pre,
        active,
        summed,
    )
    return (final, saved)


def backward(lengths, weights, saved, grad_final):
    table, positions, w_qkv, w_out, w_up, w_down, norms = weights
    norms = norms.astype(jnp.float32)
    (
        embedded,
        first_low,
        packed,
        top,
        total,
        context,
        joined,
        second_low,
        hidden_pre,
        active,
        summed,
    ) = saved
    width = table.shape[1]
    grad_summed, gain_c, shift_c = norm_back(summed, norms[:, 4], norms[:, 5], grad_final)
    grad_ffn = grad_summed.astype(jnp.bfloat16)
    g_down = weight_grad(active, grad_ffn)
    _, gelu_pull = jax.vjp(partial(jax.nn.gelu, approximate=False), hidden_pre)
    grad_up = gelu_pull(project_back(grad_ffn, w_down))[0].astype(jnp.bfloat16)
    g_up = weight_grad(second_low, grad_up)
    grad_second = grad_summed + project_back(grad_up, w_up)
    grad_joined, gain_b, shift_b = norm_back(joined, norms[:, 2], norms[:, 3], grad_second)
    grad_attn = grad_joined.astype(jnp.bfloat16)
    g_out = weight_grad(context, grad_attn)
    grad_context = project_back(grad_attn, w_out).astype(jnp.bfloat16)
    query, keyed, valued = split_heads(packed, width)
    scores = masked_scores(query, keyed, lengths)
    probs = jnp.exp(scores - top) / total
    grad_heads = grad_context.reshape(query.shape)
    grad_valued = jnp.einsum(
        "bhqk,bqhd->bkhd",
        probs.astype(jnp.bfloat16),
        grad_heads,
        preferred_element_type=jnp.float32,
    )
    grad_probs = jnp.einsum(
        "bqhd,bkhd->bhqk", grad_heads, valued, preferred_element_type=jnp.float32
    )
    grad_scores = (probs * (grad_probs - jnp.sum(probs * grad_probs, -1, keepdims=True))).astype(
        jnp.bfloat16
    )
    grad_query = jnp.einsum(
        "bhqk,bkhd->bqhd", grad_scores, keyed, preferred_element_type=jnp.float32
    ) * HD ** (-0.5)
    grad_keyed = jnp.einsum(
        "bhqk,bqhd->bkhd", grad_scores, query, preferred_element_type=jnp.float32
    ) * HD ** (-0.5)
    grad_packed = jnp.concatenate(
        [piece.reshape(first_low.shape) for piece in (grad_query, grad_keyed, grad_valued)], -1
    )
    grad_packed = grad_packed.astype(jnp.bfloat16)
    g_qkv = weight_grad(first_low, grad_packed)
    grad_first = grad_joined + project_back(grad_packed, w_qkv)
    grad_embedded, gain_a, shift_a = norm_back(embedded, norms[:, 0], norms[:, 1], grad_first)
    g_positions = jnp.sum(grad_embedded, 0)
    g_norms = jnp.stack([gain_a, shift_a, gain_b, shift_b, gain_c, shift_c], -1)
    return (grad_embedded, g_positions, g_qkv, g_out, g_up, g_down, g_norms)


def per_device(
    ids,
    lengths,
    picks,
    labels,
    s_table,
    s_pos,
    s_qkv,
    s_out,
    s_up,
    s_down,
    s_norms,
    m_table,
    m_pos,
    m_qkv,
    m_out,
    m_up,
    m_down,
    m_norms,
    a_table,
    a_pos,
    a_qkv,
    a_out,
    a_up,
    a_down,
    a_norms,
    t_table,
    t_pos,
    t_qkv,
    t_out,
    t_up,
    t_down,
    t_norms,
):
    masters = (s_table, s_pos, s_qkv, s_out, s_up, s_down, s_norms)
    momenta = (m_table, m_pos, m_qkv, m_out, m_up, m_down, m_norms)
    averages = (a_table, a_pos, a_qkv, a_out, a_up, a_down, a_norms)
    lowered = tuple((weight.astype(jnp.bfloat16) for weight in masters))
    student = jax.tree.map(
        lambda part, own: part.astype(own.dtype),
        lax.all_gather(for_sending(lowered), FSDP, axis=0, tiled=True),
        lowered,
    )
    group_ids, group_lengths, group_picks, group_labels = in_one_piece(
        (ids, lengths, picks, labels), "grp", 0, 1
    )
    teacher_rows = lax.all_gather(t_table, FSDP, axis=1, tiled=True)[0]
    teacher = (teacher_rows, t_pos[0], t_qkv[0], t_out[0], t_up[0], t_down[0], t_norms[0])
    teacher_final, _ = forward(group_ids, group_lengths, teacher)
    taken = jnp.take_along_axis(teacher_final, group_picks[:, :, None], axis=1).astype(jnp.bfloat16)
    teacher_logits = jnp.einsum(
        "bpd,vd->bpv", taken, teacher_rows, preferred_element_type=jnp.float32
    )
    log_probs = jax.nn.log_softmax(teacher_logits, axis=-1)
    group_counted = (group_picks < group_lengths[:, None]).astype(jnp.float32)
    label_logp = jnp.take_along_axis(log_probs, group_labels[:, :, None], axis=2)[:, :, 0]
    label_loss = -jnp.sum(group_counted * label_logp, -1) / jnp.maximum(
        jnp.sum(group_counted, -1), 1.0
    )
    all_losses = gathered_copies(label_loss[None], "grp", 0)
    blend = jax.nn.softmax(-all_losses, axis=0)
    mine = lax.dynamic_index_in_dim(blend, lax.axis_index("grp"), 0, keepdims=False)
    teacher_probs = jnp.exp(log_probs)
    share = (mine[:, None, None] * teacher_probs).astype(jnp.bfloat16)
    spread = (mine[:, None] * jnp.sum(teacher_probs * log_probs, -1)).astype(jnp.bfloat16)
    target, entropy = tuple(
        (part.astype(jnp.float32) for part in side_by_side((share, spread), "grp", 0, 2))
    )
    final, saved = forward(ids, lengths, student)
    counted = (picks < lengths[:, None]).astype(jnp.float32)
    rows_low = jnp.take_along_axis(final, picks[:, :, None], axis=1).astype(jnp.bfloat16)
    logits = jnp.einsum("bpd,vd->bpv", rows_low, student[0], preferred_element_type=jnp.float32)
    log_total = jax.scipy.special.logsumexp(logits, axis=-1)
    per_row = entropy - jnp.sum(target * logits, -1) + log_total
    loss_local = jnp.sum(counted * per_row)
    count_local = jnp.sum(counted)
    grad_logits = (counted[:, :, None] * (jnp.exp(logits - log_total[:, :, None]) - target)).astype(
        jnp.bfloat16
    )
    grad_rows = jnp.einsum(
        "bpv,vd->bpd", grad_logits, student[0], preferred_element_type=jnp.float32
    )
    grad_final = jnp.zeros(final.shape, jnp.float32).at[0, picks[0]].add(grad_rows[0])
    terms = backward(lengths, student, saved, grad_final)
    grad_embedded = terms[0]
    width = s_table.shape[1]
    head_grad = jnp.einsum("bpv,bpd->vd", grad_logits, rows_low, preferred_element_type=jnp.float32)
    g_lookup = (
        jnp.zeros((student[0].shape[0], width), jnp.float32)
        .at[ids.reshape(-1)]
        .add(grad_embedded.reshape(-1, width))
    )
    table_part = lax.psum_scatter(
        (g_lookup + head_grad).astype(jnp.bfloat16), FSDP, scatter_dimension=0, tiled=True
    ).astype(jnp.float32)
    rest = jax.tree.map(
        lambda part: part.astype(jnp.float32),
        lax.psum_scatter(for_sending(terms[1:]), FSDP, scatter_dimension=0, tiled=True),
    )
    shards = jax.tree.map(
        lambda part: part.astype(jnp.float32),
        lax.psum(for_sending((table_part,) + tuple(rest)), "grp"),
    )
    squares = sum((jnp.sum(piece * piece) for piece in shards))
    loss_sum, count = (over_axes(loss_local, GRP_FSDP), over_axes(count_local, GRP_FSDP))
    squares = of_everyone(squares, FSDP)
    clip_norm = jnp.sqrt(squares) / count
    factor = jnp.minimum(1.0, clip_limit / clip_norm) / count
    new_weights, new_moments, new_averages = ([], [], [])
    for weight, moment, average, grad in zip(masters, momenta, averages, shards):
        clipped = grad * factor
        moment_new = momentum_decay * moment + clipped
        weight_new = weight - learn_rate * (clipped + momentum_decay * moment_new)
        new_weights.append(weight_new)
        new_moments.append(moment_new)
        new_averages.append(average_decay * average + (1.0 - average_decay) * weight_new)
    return (
        (loss_sum, count, clip_norm) + tuple(new_weights) + tuple(new_moments) + tuple(new_averages)
    )


def solution(mesh):
    finer = Mesh(
        mesh.devices.reshape(mesh.shape["grp"], 4, 4, 2), ("grp", "fsdp_0", "fsdp_1", "fsdp_2")
    )
    return jax.shard_map(
        per_device,
        mesh=finer,
        in_specs=(
            P(GRP_FSDP, None),
            P(GRP_FSDP),
            P(GRP_FSDP, None),
            P(GRP_FSDP, None),
            P(FSDP, None),
            P(FSDP, None),
            P(FSDP, None),
            P(FSDP, None),
            P(FSDP, None),
            P(FSDP, None),
            P(FSDP, None),
            P(FSDP, None),
            P(FSDP, None),
            P(FSDP, None),
            P(FSDP, None),
            P(FSDP, None),
            P(FSDP, None),
            P(FSDP, None),
            P(FSDP, None),
            P(FSDP, None),
            P(FSDP, None),
            P(FSDP, None),
            P(FSDP, None),
            P(FSDP, None),
            P(FSDP, None),
            P("grp", FSDP, None),
            P("grp", None, None),
            P("grp", None, None),
            P("grp", None, None),
            P("grp", None, None),
            P("grp", None, None),
            P("grp", None, None),
        ),
        out_specs=(
            P(),
            P(),
            P(),
            P(FSDP, None),
            P(FSDP, None),
            P(FSDP, None),
            P(FSDP, None),
            P(FSDP, None),
            P(FSDP, None),
            P(FSDP, None),
            P(FSDP, None),
            P(FSDP, None),
            P(FSDP, None),
            P(FSDP, None),
            P(FSDP, None),
            P(FSDP, None),
            P(FSDP, None),
            P(FSDP, None),
            P(FSDP, None),
            P(FSDP, None),
            P(FSDP, None),
            P(FSDP, None),
            P(FSDP, None),
            P(FSDP, None),
        ),
        check_vma=False,
    )
```

profile of v0, /device:TPU:1, one launch (start us, length us, event | category | flops | bytes accessed | tf_op | source)
XLA Modules:
  0.0 1373.3 jit_solution(8588599391114457754)
XLA Ops:
  8.0 2.7 convert_element_type.270
  17.0 10.1 all-gather
  30.4 2.0 bitcast_convert_fusion
  35.7 127.4 %all-gather.8.cloned.1.call-done = bf16[1,30720,768]{2,1,0:T(8,128)(2,1)} async-done(((bf16[1,960,768]{2,1,0:T(8,128)(2,1)}), bf16[1,30720,768]{2,1,0:T(8,128)(2,1)}) %all-gather.8.cloned.1.call-update) | async-done | bytes 47185936 | tf_op jit(solution)/shard_map/all_gather | solution.py:259
  163.1 19.0 %gather_fusion = bf16[1024,768]{1,0:T(8,128)(2,1)} fusion(bf16[30720,768]{1,0:T(8,128)(2,1)} %bitcast.264, s32[1024]{0:T(1024)S(1)} %broadcast_clamp_fusion), kind=kCustom, calls=%fused_computation | custom fusion | bytes 3149824 | tf_op jit(solution)/shard_map/jit(_take)/gather | solution.py:116
  182.1 2.5 fusion.31
  184.6 2.0 multiply_reduce_fusion.2
  186.7 4.6 convolution_convert_fusion
  193.0 2.6 copy.152
  197.2 1.7 copy.151
  199.0 10.5 fusion.241
  209.6 7.0 fusion.55
  216.7 2.3 fusion.242
  219.8 12.0 fusion.33
  231.9 36.7 %fusion.243 = (f32[4,256]{1,0:T(4,128)S(1)}, f32[4,256,768]{2,1,0:T(8,128)S(1)}) fusion(bf16[1,3072,768]{2,1,0:T(8,128)(2,1)S(1)} %bitcast.319, f32[4,256,3072]{2,1,0:T(8,128)} %get-tuple-element.124, u8[256,3072]{1,0:T(8,128)(4,1)S(1)} %get-tuple-element.25, u8[256,3072]{1,0:T(8,128)(4,1)S(1)} %get-tuple-element.24, f32[768]{0:T(1024)S(1)} %copy-done.72, ...), kind=kOutput, calls=%fused_computation.388 | convolution fusion | flops 5056756736 | bytes 25184256 | tf_op jit(solution)/shard_map/blk,kn->bln/dot_general | solution.py:84
  269.7 2.4 gather_fusion.3
  272.2 31.1 %fusion.244 = (f32[4,64]{1,0:T(4,128)S(1)}, f32[4,64,30720]{2,1,0:T(8,128)}) fusion(bf16[1,30720,768]{2,1,0:T(8,128)(2,1)} %all-gather.8.cloned.1.call-done, bf16[4,64,768]{2,1,0:T(8,128)(2,1)S(1)} %bitcast.272, pred[4,64]{1,0:T(4,128)(4,1)S(1)} %copy-done.95), kind=kOutput, calls=%fused_computation.389 | convolution fusion | flops 12087656448 | bytes 79037696 | tf_op jit(solution)/shard_map/bpd,vd->bpv/dot_general | solution.py:263
  303.2 14.0 %exponential_reduce_fusion = f32[4,64]{1,0:T(4,128)S(1)} fusion(f32[4,64,30720]{2,1,0:T(8,128)} %get-tuple-element.128, f32[4,64]{1,0:T(4,128)S(1)} %get-tuple-element.127), kind=kLoop, calls=%fused_computation.15 | loop fusion | flops 15728384 | bytes 31459328 | tf_op jit(solution)/shard_map/jit(log_softmax)/reduce_sum | solution.py:266
  317.3 5.4 copy-done.2
  322.7 12.9 fusion.5
  335.6 3.7 gather_fusion.4
  340.3 8.2 all_to_all.11
  348.6 17.8 %fusion.4 = bf16[4,64,30720]{2,1,0:T(8,128)(2,1)} fusion(f32[4,64,30720]{2,1,0:T(8,128)} %get-tuple-element.88, f32[4]{0:T(128)S(1)} %dynamic-slice_bitcast_fusion), kind=kLoop, calls=%fused_computation.13 | loop fusion | flops 15728640 | bytes 47185936 | tf_op jit(solution)/shard_map/convert_element_type | solution.py:276
  366.6 13.3 pad_maximum_fusion
  380.6 25.3 %all-gather.1 = bf16[32,16,6]{1,2,0:T(8,128)(2,1)S(1)} all-gather(bf16[1,16,6]{1,2,0:T(8,128)(2,1)S(1)} %convert_bitcast_fusion), channel_id=1, replica_groups=mesh['grp'=4,'fsdp_0'=4,'fsdp_1'=4,'fsdp_2'=2] {'fsdp_0','fsdp_1','fsdp_2'}, dimensions={0}, use_global_device_ids=true | all-gather | bytes 6336 | tf_op jit(solution)/shard_map/all_gather | solution.py:253
  406.2 24.0 %all_gather.30 = bf16[256,512]{1,0:T(8,128)(2,1)S(1)} all-gather(bf16[8,512]{1,0:T(8,128)(2,1)S(1)} %convert_element_type.272), channel_id=1, replica_groups=mesh['grp'=4,'fsdp_0'=4,'fsdp_1'=4,'fsdp_2'=2] {'fsdp_0','fsdp_1','fsdp_2'}, dimensions={0}, use_global_device_ids=true | all-gather | bytes 270336 | tf_op jit(solution)/shard_map/all_gather | solution.py:253
  430.9 22.9 %all_gather.33 = bf16[512,512]{1,0:T(8,128)(2,1)S(1)} all-gather(bf16[16,512]{1,0:T(8,128)(2,1)S(1)} %convert_element_type.285), channel_id=1, replica_groups=mesh['grp'=4,'fsdp_0'=4,'fsdp_1'=4,'fsdp_2'=2] {'fsdp_0','fsdp_1','fsdp_2'}, dimensions={0}, use_global_device_ids=true | all-gather | bytes 540672 | tf_op jit(solution)/shard_map/all_gather | solution.py:253
  454.9 3.0 gather_fusion.1
  458.5 2.1 fusion.36
  461.2 2.2 fusion.237
  463.3 2.0 convolution_convert_fusion.8
  466.1 8.3 multiply_convert_fusion.1
  474.4 2.7 fusion.239
  478.4 18.6 %fusion.240 = (f32[64]{0:T(128)S(1)}, f32[64,30720]{1,0:T(8,128)}) fusion(bf16[30720,512]{1,0:T(8,128)(2,1)} %all-gather.10.cloned.1.call-done, bf16[64,512]{1,0:T(8,128)(2,1)S(1)} %gather_fusion.2, pred[64]{0:T(512)(128)(4,1)S(1)} %copy-done.90), kind=kOutput, calls=%fused_computation.385 | convolution fusion | flops 2015264768 | bytes 39387456 | tf_op jit(solution)/shard_map/bpd,vd->bpv/dot_general | solution.py:284
  497.1 4.5 exponential_reduce_fusion.1
  501.6 50.1 %reduce-scatter.11.cloned.1.call-done = bf16[1,64,30721]{2,1,0:T(8,128)(2,1)} async-done(((bf16[4,64,30721]{2,1,0:T(8,128)(2,1)}), bf16[1,64,30721]{2,1,0:T(8,128)(2,1)}) %reduce-scatter.11.cloned.1.call-update) | async-done | bytes 3932304 | tf_op jit(solution)/shard_map/reduce_scatter | solution.py:58
  551.7 6.2 fusion.28
  558.0 2.1 copy-done.3
  560.0 12.6 fusion.245
  575.3 4.2 add_convert_fusion
  581.9 2.2 multiply_reduce_fusion.3
  588.6 2.3 fusion.215
  594.8 3.2 convolution_convert_fusion.3
  598.1 2.1 convolution_convert_fusion.1
  600.3 3.4 convolution_convert_fusion.2
  604.0 24.5 %fusion.118 = f32[30720,512]{1,0:T(8,128)} fusion(bf16[64,30720]{1,0:T(8,128)(2,1)} %copy-done.3, bf16[64,512]{1,0:T(8,128)(2,1)S(1)} %gather_fusion.2, pred[64]{0:T(512)(128)(4,1)S(1)} %copy-done.91), kind=kOutput, calls=%fused_computation.217 | convolution fusion | flops 2013298688 | bytes 66912320 | tf_op jit(solution)/shard_map/bpv,bpd->vd/dot_general | solution.py:299
  628.5 30.9 %scatter_fusion = f32[30720,512]{1,0:T(8,128)} fusion(f32[30720,512]{1,0:T(8,128)} %fusion.118, s32[256]{0:T(256)S(1)} %bitcast.311, f32[256,512]{1,0:T(8,128)S(1)} %get-tuple-element.82), kind=kCustom, calls=%fused_computation.6 | custom fusion | flops 131072 | bytes 1573888 | tf_op jit(solution)/shard_map/scatter-add | solution.py:303
  659.4 31.6 %convert_element_type.300 = bf16[30720,512]{1,0:T(8,128)(2,1)} convert(f32[30720,512]{1,0:T(8,128)} %scatter_fusion) | non-fusion elementwise | flops 15728640 | bytes 94371840 | tf_op jit(solution)/shard_map/convert_element_type | solution.py:306
  692.9 49.6 %reduce-scatter.15.cloned.1.call-done = bf16[8,512]{1,0:T(8,128)(2,1)} async-done(((bf16[256,512]{1,0:T(8,128)(2,1)}), bf16[8,512]{1,0:T(8,128)(2,1)}) %reduce-scatter.15.cloned.1.call-update) | async-done | bytes 8208 | tf_op jit(solution)/shard_map/reduce_scatter | solution.py:310
  742.4 80.1 %reduce-scatter.19.cloned.1.call-done = bf16[16,512]{1,0:T(8,128)(2,1)} async-done(((bf16[512,512]{1,0:T(8,128)(2,1)}), bf16[16,512]{1,0:T(8,128)(2,1)}) %reduce-scatter.19.cloned.1.call-update) | async-done | bytes 16400 | tf_op jit(solution)/shard_map/reduce_scatter | solution.py:310
  822.6 81.4 %reduce-scatter.17.cloned.1.call-done = bf16[16,1536]{1,0:T(8,128)(2,1)} async-done(((bf16[512,1536]{1,0:T(8,128)(2,1)}), bf16[16,1536]{1,0:T(8,128)(2,1)}) %reduce-scatter.17.cloned.1.call-update) | async-done | bytes 49168 | tf_op jit(solution)/shard_map/reduce_scatter | solution.py:310
  904.1 81.6 %reduce-scatter.23.cloned.1.call-done = bf16[64,512]{1,0:T(8,128)(2,1)} async-done(((bf16[2048,512]{1,0:T(8,128)(2,1)}), bf16[64,512]{1,0:T(8,128)(2,1)}) %reduce-scatter.23.cloned.1.call-update) | async-done | bytes 65552 | tf_op jit(solution)/shard_map/reduce_scatter | solution.py:310
  985.7 81.5 %reduce-scatter.21.cloned.1.call-done = bf16[16,2048]{1,0:T(8,128)(2,1)} async-done(((bf16[512,2048]{1,0:T(8,128)(2,1)}), bf16[16,2048]{1,0:T(8,128)(2,1)}) %reduce-scatter.21.cloned.1.call-update) | async-done | bytes 65552 | tf_op jit(solution)/shard_map/reduce_scatter | solution.py:310
  1067.2 164.0 %reduce-scatter.13.cloned.1.call-done = bf16[960,512]{1,0:T(8,128)(2,1)} async-done(((bf16[30720,512]{1,0:T(8,128)(2,1)}), bf16[960,512]{1,0:T(8,128)(2,1)}) %reduce-scatter.13.cloned.1.call-update) | async-done | bytes 983056 | tf_op jit(solution)/shard_map/reduce_scatter | solution.py:305
  1232.7 9.3 all-reduce.3
  1242.0 8.9 all-reduce.2
  1250.8 7.7 all-reduce.1
  1258.5 9.2 all-reduce.4
  1267.7 4.6 all-reduce.10.cloned.1.call-done
  1277.7 45.4 %all-reduce.12.cloned.1.call-done = (bf16[960,512]{1,0:T(8,128)(2,1)}, bf16[16,2048]{1,0:T(8,128)(2,1)}, bf16[64,512]{1,0:T(8,128)(2,1)}) async-done(((bf16[960,512]{1,0:T(8,128)(2,1)}, bf16[16,2048]{1,0:T(8,128)(2,1)}, bf16[64,512]{1,0:T(8,128)(2,1)}), (bf16[960,512]{1,0:T(8,128)(2,1)}, bf16[16,2048]{1,0:T(8,128)(2,1)}, bf16[64,512]{1,0:T(8,128)(2,1)})) %all-reduce.12.cloned.1.call-update) | async-done | bytes 1114128 | tf_op jit(solution)/shard_map/psum | solution.py:314
  1323.1 2.3 fusion.53
  1333.5 8.7 all-to-all-start.1
  1342.9 6.2 all-to-all-done.1
  1359.3 6.2 multiply_add_fusion.3
  (367 shorter events, 58.7 us)
Async XLA Ops:
  7.2 179.5 %copy-start = (bf16[1,768,2304]{2,1,0:T(8,128)(2,1)S(1)}, bf16[1,768,2304]{2,1,0:T(8,128)(2,1)}, u32[]{:S(2)}) copy-start(bf16[1,768,2304]{2,1,0:T(8,128)(2,1)} %param.59) | copy-start | bytes 10616836
  7.2 9.1 copy-start.56
  7.2 155.9 %all-gather.8.cloned.1.call-start = ((), (), s32[]{:S(2)}) async-start(), calls=%async_computation.10 | async-start | bytes 48660480 | tf_op jit(solution)/shard_map/all_gather | solution.py:259
  8.0 24.4 %copy-start.50 = (bf16[1,768,6]{1,2,0:T(8,128)(2,1)S(1)}, bf16[1,768,6]{1,2,0:T(8,128)(2,1)}, u32[]{:S(2)}) copy-start(bf16[1,768,6]{1,2,0:T(8,128)(2,1)} %param.63) | copy-start | bytes 27652
  8.0 446.9 %all-gather.10.cloned.1.call-start = ((), (), s32[]{:S(2)}) async-start(), calls=%async_computation.12 | async-start | bytes 32440320 | tf_op jit(solution)/shard_map/all_gather | solution.py:253
  10.7 447.7 %all-gather.12.cloned.1.call-start = ((), (), s32[]{:S(2)}) async-start(), calls=%async_computation.13 | async-start | bytes 1622016 | tf_op jit(solution)/shard_map/all_gather | solution.py:253
  12.3 453.8 %all-gather.14.cloned.1.call-start = ((), (), s32[]{:S(2)}) async-start(), calls=%async_computation.14 | async-start | bytes 2162688 | tf_op jit(solution)/shard_map/all_gather | solution.py:253
  13.9 460.4 %all-gather.16.cloned.1.call-start = ((), (), s32[]{:S(2)}) async-start(), calls=%async_computation.15 | async-start | bytes 2162688 | tf_op jit(solution)/shard_map/all_gather | solution.py:253
  15.6 536.1 %reduce-scatter.11.cloned.1.call-start = ((), (), s32[]{:S(2)}) async-start(), calls=%async_computation.11 | async-start | bytes 19742720 | tf_op jit(solution)/shard_map/reduce_scatter | solution.py:58
  163.1 19.0 %copy-start.51 = (pred[4,256]{1,0:T(4,128)(4,1)S(1)}, pred[4,256]{1,0:T(4,128)(4,1)}, u32[]{:S(2)}) copy-start(pred[4,256]{1,0:T(4,128)(4,1)} %compare_and_fusion) | copy-start | bytes 3076
  209.5 7.1 copy-start.75
  209.5 7.1 copy-start.77
  209.5 7.1 copy-start.98
  219.0 12.8 slice-start.2
  219.8 12.1 slice-start.3
  303.2 19.4 %copy-start.2 = (f32[4,64,30720]{2,1,0:T(8,128)S(1)}, f32[4,64,30720]{2,1,0:T(8,128)}, u32[]{:S(2)}) copy-start(f32[4,64,30720]{2,1,0:T(8,128)} %get-tuple-element.128) | copy-start | bytes 94371840
  322.7 12.9 copy-start.4
  322.7 16.7 %copy-start.89 = (pred[4,64]{1,0:T(4,128)(4,1)S(1)}, pred[4,64]{1,0:T(4,128)(4,1)}, u32[]{:S(2)}) copy-start(pred[4,64]{1,0:T(4,128)(4,1)} %get-tuple-element.107) | copy-start | bytes 772
  379.9 26.3 %copy-start.32 = (f32[16,512]{1,0:T(8,128)S(1)}, f32[16,512]{1,0:T(8,128)}, u32[]{:S(2)}) copy-start(f32[16,512]{1,0:T(8,128)} %param.39) | copy-start | bytes 98308
  379.9 50.3 %copy-start.57 = (s32[1,256]{1,0:T(1,128)S(1)}, s32[1,256]{1,0:T(1,128)}, u32[]{:S(2)}) copy-start(s32[1,256]{1,0:T(1,128)} %param.32) | copy-start | bytes 3076
  379.9 50.4 %copy-start.87 = (s32[1,64]{1,0:T(1,128)S(1)}, s32[1,64]{1,0:T(1,128)}, u32[]{:S(2)}) copy-start(s32[1,64]{1,0:T(1,128)} %param.34) | copy-start | bytes 772
  380.0 311.3 %reduce-scatter.25.cloned.1.call-start = ((), (), s32[]{:S(2)}) async-start(), calls=%async_computation.22 | async-start | bytes 135168
  430.2 35.1 %copy-start.48 = (pred[256]{0:T(512)(128)(4,1)}, pred[256]{0:T(512)(128)(4,1)S(1)}, u32[]{:S(2)}) copy-start(pred[256]{0:T(512)(128)(4,1)S(1)} %get-tuple-element.91) | copy-start | bytes 772
  430.3 24.0 %copy-start.96 = (s32[64]{0:T(128)}, s32[64]{0:T(128)S(1)}, u32[]{:S(2)}) copy-start(s32[64]{0:T(128)S(1)} %fusion.153) | copy-start | bytes 772
  454.8 10.5 copy-start.86
  454.8 19.6 %copy-start.66 = (f32[512,1]{0,1:T(1,128)}, f32[512,1]{0,1:T(1,128)S(1)}, u32[]{:S(2)}) copy-start(f32[512,1]{0,1:T(1,128)S(1)} %get-tuple-element.103) | copy-start | bytes 6148
  465.3 9.0 copy-start.27
  466.0 8.3 copy-start.54
  466.1 8.4 copy-start.61
  497.1 54.7 %copy-start.94 = (f32[64]{0:T(128)S(1)}, f32[64]{0:T(128)}, u32[]{:S(2)}) copy-start(f32[64]{0:T(128)} %fusion.156) | copy-start | bytes 772
  501.6 56.3 %copy-start.84 = (f32[64]{0:T(128)}, f32[64]{0:T(128)S(1)}, u32[]{:S(2)}) copy-start(f32[64]{0:T(128)S(1)} %exponential_reduce_fusion.1) | copy-start | bytes 772
  581.3 7.2 copy-start.59
  592.3 150.1 %reduce-scatter.15.cloned.1.call-start = ((), (), s32[]{:S(2)}) async-start(), calls=%async_computation.17 | async-start | bytes 270336 | tf_op jit(solution)/shard_map/reduce_scatter | solution.py:310
  593.5 229.1 %reduce-scatter.19.cloned.1.call-start = ((), (), s32[]{:S(2)}) async-start(), calls=%async_computation.19 | async-start | bytes 540672 | tf_op jit(solution)/shard_map/reduce_scatter | solution.py:310
  594.7 309.3 %reduce-scatter.17.cloned.1.call-start = ((), (), s32[]{:S(2)}) async-start(), calls=%async_computation.18 | async-start | bytes 1622016 | tf_op jit(solution)/shard_map/reduce_scatter | solution.py:310
  598.0 387.7 %reduce-scatter.23.cloned.1.call-start = ((), (), s32[]{:S(2)}) async-start(), calls=%async_computation.21 | async-start | bytes 2162688 | tf_op jit(solution)/shard_map/reduce_scatter | solution.py:310
  600.2 467.0 %reduce-scatter.21.cloned.1.call-start = ((), (), s32[]{:S(2)}) async-start(), calls=%async_computation.20 | async-start | bytes 2162688 | tf_op jit(solution)/shard_map/reduce_scatter | solution.py:310
  603.7 627.5 %reduce-scatter.13.cloned.1.call-start = ((), (), s32[]{:S(2)}) async-start(), calls=%async_computation.16 | async-start | bytes 32440320 | tf_op jit(solution)/shard_map/reduce_scatter | solution.py:305
  691.0 541.1 %copy-start.81 = (f32[64]{0:T(128)S(1)}, f32[64]{0:T(128)}, u32[]{:S(2)}) copy-start(f32[64]{0:T(128)} %get-tuple-element.94) | copy-start | bytes 772
  691.0 541.1 %copy-start.83 = (f32[64]{0:T(128)S(1)}, f32[64]{0:T(128)}, u32[]{:S(2)}) copy-start(f32[64]{0:T(128)} %copy-done.82) | copy-start | bytes 772
  691.0 541.1 %copy-start.85 = (f32[64]{0:T(128)S(1)}, f32[64]{0:T(128)}, u32[]{:S(2)}) copy-start(f32[64]{0:T(128)} %copy-done.84) | copy-start | bytes 772
  691.0 541.1 %copy-start.88 = (s32[1,64]{1,0:T(1,128)S(1)}, s32[1,64]{1,0:T(1,128)}, u32[]{:S(2)}) copy-start(s32[1,64]{1,0:T(1,128)} %param.34) | copy-start | bytes 772
  691.0 660.8 %copy-start.45 = (f32[16,6]{0,1:T(8,128)S(1)}, f32[16,6]{0,1:T(8,128)}, u32[]{:S(2)}) copy-start(f32[16,6]{0,1:T(8,128)} %param.42) | copy-start | bytes 1156
  691.0 660.8 %copy-start.70 = (f32[16,6]{0,1:T(8,128)S(1)}, f32[16,6]{0,1:T(8,128)}, u32[]{:S(2)}) copy-start(f32[16,6]{0,1:T(8,128)} %param.56) | copy-start | bytes 1156
  691.0 660.8 %copy-start.71 = (f32[16,6]{0,1:T(8,128)S(1)}, f32[16,6]{0,1:T(8,128)}, u32[]{:S(2)}) copy-start(f32[16,6]{0,1:T(8,128)} %param.49) | copy-start | bytes 1156
  691.0 662.2 %copy-start.21 = (f32[64,512]{1,0:T(8,128)S(1)}, f32[64,512]{1,0:T(8,128)}, u32[]{:S(2)}) copy-start(f32[64,512]{1,0:T(8,128)} %param.41) | copy-start | bytes 393220
  691.0 662.2 %copy-start.33 = (f32[64,512]{1,0:T(8,128)S(1)}, f32[64,512]{1,0:T(8,128)}, u32[]{:S(2)}) copy-start(f32[64,512]{1,0:T(8,128)} %param.55) | copy-start | bytes 393220
  691.1 662.2 %copy-start.34 = (f32[64,512]{1,0:T(8,128)S(1)}, f32[64,512]{1,0:T(8,128)}, u32[]{:S(2)}) copy-start(f32[64,512]{1,0:T(8,128)} %param.48) | copy-start | bytes 393220
  691.1 663.8 %copy-start.22 = (f32[16,2048]{1,0:T(8,128)S(1)}, f32[16,2048]{1,0:T(8,128)}, u32[]{:S(2)}) copy-start(f32[16,2048]{1,0:T(8,128)} %param.40) | copy-start | bytes 393220
  691.1 663.8 %copy-start.35 = (f32[16,2048]{1,0:T(8,128)S(1)}, f32[16,2048]{1,0:T(8,128)}, u32[]{:S(2)}) copy-start(f32[16,2048]{1,0:T(8,128)} %param.54) | copy-start | bytes 393220
  691.1 663.7 %copy-start.36 = (f32[16,2048]{1,0:T(8,128)S(1)}, f32[16,2048]{1,0:T(8,128)}, u32[]{:S(2)}) copy-start(f32[16,2048]{1,0:T(8,128)} %param.47) | copy-start | bytes 393220
  691.1 665.4 %copy-start.41 = (f32[16,512]{1,0:T(8,128)S(1)}, f32[16,512]{1,0:T(8,128)}, u32[]{:S(2)}) copy-start(f32[16,512]{1,0:T(8,128)} %param.53) | copy-start | bytes 98308
  691.1 665.4 %copy-start.42 = (f32[16,512]{1,0:T(8,128)S(1)}, f32[16,512]{1,0:T(8,128)}, u32[]{:S(2)}) copy-start(f32[16,512]{1,0:T(8,128)} %param.46) | copy-start | bytes 98308
  691.2 666.7 %copy-start.23 = (f32[16,1536]{1,0:T(8,128)S(1)}, f32[16,1536]{1,0:T(8,128)}, u32[]{:S(2)}) copy-start(f32[16,1536]{1,0:T(8,128)} %param.38) | copy-start | bytes 294916
  691.2 666.7 %copy-start.37 = (f32[16,1536]{1,0:T(8,128)S(1)}, f32[16,1536]{1,0:T(8,128)}, u32[]{:S(2)}) copy-start(f32[16,1536]{1,0:T(8,128)} %param.52) | copy-start | bytes 294916
  691.2 666.7 %copy-start.38 = (f32[16,1536]{1,0:T(8,128)S(1)}, f32[16,1536]{1,0:T(8,128)}, u32[]{:S(2)}) copy-start(f32[16,1536]{1,0:T(8,128)} %param.45) | copy-start | bytes 294916
  691.2 667.4 %copy-start.46 = (f32[8,512]{1,0:T(8,128)S(1)}, f32[8,512]{1,0:T(8,128)}, u32[]{:S(2)}) copy-start(f32[8,512]{1,0:T(8,128)} %param.51) | copy-start | bytes 49156
  691.2 667.4 %copy-start.47 = (f32[8,512]{1,0:T(8,128)S(1)}, f32[8,512]{1,0:T(8,128)}, u32[]{:S(2)}) copy-start(f32[8,512]{1,0:T(8,128)} %param.44) | copy-start | bytes 49156
  691.2 581.1 %all-reduce.10.cloned.1.call-start = ((), (), s32[]{:S(2)}) async-start(), calls=%async_computation.23 | async-start | bytes 151552 | tf_op jit(solution)/shard_map/psum | solution.py:314
  904.0 419.1 %all-reduce.12.cloned.1.call-start = ((), (), s32[]{:S(2)}) async-start(), calls=%async_computation.24 | async-start | bytes 2228224 | tf_op jit(solution)/shard_map/psum | solution.py:314
  1272.3 85.5 %copy-start.31 = (bf16[16,1536]{1,0:T(8,128)(2,1)S(1)}, bf16[16,1536]{1,0:T(8,128)(2,1)}, u32[]{:S(2)}) copy-start(bf16[16,1536]{1,0:T(8,128)(2,1)} %get-tuple-element.54) | copy-start | bytes 147460
  1272.3 86.3 %copy-start.43 = (bf16[8,512]{1,0:T(8,128)(2,1)S(1)}, bf16[8,512]{1,0:T(8,128)(2,1)}, u32[]{:S(2)}) copy-start(bf16[8,512]{1,0:T(8,128)(2,1)} %get-tuple-element.53) | copy-start | bytes 24580
  1333.5 15.6 %all-to-all-start.1 = ((f32[32,1,1]{2,1,0:T(1,128)}), f32[32,1,1]{2,1,0:T(1,128)S(1)}, u32[]{:S(2)}, u32[]{:S(2)}) async-start(f32[32,1,1]{2,1,0:T(1,128)} %broadcast_in_dim.203), calls=%async_computation.8 | async-start | bytes 32768 | tf_op jit(solution)/shard_map/all_to_all | solution.py:46
  1351.9 7.4 copy-start.10
  (56 other events, 174.9 us)
Sparse Core Ops, SparseCore 0:
  10.3 152.7 all-gather.7
  165.3 107.4 all-gather.9
  275.7 42.5 all-gather.11
  320.9 43.0 all-gather.13
  366.7 42.9 all-gather.15
  412.0 139.6 reduce-scatter.10
  592.5 70.3 reduce-scatter.24
  666.3 76.0 reduce-scatter.14
  745.9 76.6 reduce-scatter.18
  826.5 77.4 reduce-scatter.16
  907.5 78.0 reduce-scatter.22
  989.1 78.0 reduce-scatter.20
  1071.2 159.9 reduce-scatter.12
  1234.4 37.9 all-reduce.9
  1274.8 48.2 all-reduce.11
where the time goes:
time: 1380 us; the launch traced here: 1370 us
  waiting for transfers between devices  773 us (56%)
  matrix products  201 us (15%)
  other arithmetic  186 us (13%)
  blocking collectives  125 us (9%)
  local copies, waits for them, and re-layouts  52.9 us (4%)
  between operations  24.8 us (2%)
    reduce_scatter x5, waiting for transfers between devices, per_device(): lax.psum_scatter(for_sending(terms[1:]), FSDP, scatter_dimension=0, tiled...  374 us
    reduce_scatter x1, waiting for transfers between devices, per_device(): lax.psum_scatter((g_lookup + head_grad).astype(jnp.bfloat16), FSDP, scatt...  164 us
    all_gather x1, waiting for transfers between devices, per_device(): teacher_rows = lax.all_gather(t_table, FSDP, axis=1, tiled=True)[0]  127 us
    all_gather x3, blocking collectives, per_device(): lax.all_gather(for_sending(lowered), FSDP, axis=0, tiled=True)  72.1 us
    dot_general x8, matrix products, project(): jnp.einsum('blk,kn->bln', left, right, preferred_element_type=jnp.float32)  69.3 us
    reduce_scatter x1, waiting for transfers between devices, side_by_side(): out = lax.psum_scatter(both, axis, scatter_dimension=dim, tiled=True)  50.1 us
    psum x2, waiting for transfers between devices, per_device(): lax.psum(for_sending((table_part,) + tuple(rest)), 'grp')  50 us
    psum x4, blocking collectives, over_axes(): return functools.reduce(lax.psum, axes, value)  35 us
  transfers between devices with their start and end apart: 16, of which 11 were waited for; matrix products, arithmetic and copies ran while one was open for 27% of the time, Pallas kernels for 0%

commit v1 on v0

--- a/solution.py
+++ b/solution.py
@@ -1,6 +1,5 @@
+import math
 from functools import partial
-import functools
-import math
 
 import jax
 import jax.numpy as jnp
@@ -9,9 +8,8 @@
 from jax.sharding import PartitionSpec as P
 
 HD = 64
-FSDP = ("fsdp_0", "fsdp_1", "fsdp_2")
-GRP_FSDP = ("grp", "fsdp_0", "fsdp_1", "fsdp_2")
-
+FSDP = ("y", "x", "c")
+GRP_FSDP = ("grp", "y", "x", "c")
 
 norm_eps = 1e-12
 clip_limit = 0.001
@@ -20,52 +18,31 @@
 average_decay = 0.9
 
 
-def for_sending(value):
-    return jax.tree.map(lambda a: a.astype(jnp.bfloat16) if a.dtype == jnp.float32 else a, value)
-
-
-def in_one_piece(arrays, axis, dim, along):
-    columns = [a.reshape(*a.shape[:along], -1) for a in arrays]
-    both = jnp.concatenate(columns, axis=along)
-    out, at, finished = (lax.all_gather(both, axis, axis=dim, tiled=True), 0, [])
-    for a, column in zip(arrays, columns):
-        piece = out[..., at : at + column.shape[along]]
-        finished.append(piece.reshape(*piece.shape[:along], *a.shape[along:]))
-        at += column.shape[along]
-    return tuple(finished)
-
-
-def in_order(blocks, dim):
-    blocks = jnp.moveaxis(blocks, 0, dim)
-    dims = blocks.shape
-    return blocks.reshape(*dims[:dim], dims[dim] * dims[dim + 1], *dims[dim + 2 :])
-
-
 def from_everyone(value, axis):
     copies = jnp.broadcast_to(value, (lax.axis_size(axis), *value.shape))
     return lax.all_to_all(copies, axis, split_axis=0, concat_axis=0, tiled=True)
 
 
-def gathered_copies(value, axis, dim):
-    return in_order(from_everyone(value, axis), dim)
-
-
-def side_by_side(arrays, axis, dim, along):
-    widths = [math.prod(a.shape[along:]) for a in arrays]
-    both = jnp.concatenate(
-        [a.reshape(*a.shape[:along], w) for a, w in zip(arrays, widths)], axis=along
-    )
-    out = lax.psum_scatter(both, axis, scatter_dimension=dim, tiled=True)
-    blocks = jnp.split(out, [sum(widths[:k]) for k in range(1, len(widths))], axis=along)
-    return tuple((b.reshape(*out.shape[:along], *a.shape[along:]) for a, b in zip(arrays, blocks)))
-
-
-def over_axes(value, axes):
-    return functools.reduce(lax.psum, axes, value)
-
-
-def of_everyone(value, axis):
-    return from_everyone(value, axis).sum(axis=0)
+def sum_of_groups(value):
+    groups = lax.axis_size("grp")
+    me = lax.axis_index("grp")
+    parts = [value]
+    for step in range(1, groups):
+        parts.append(lax.ppermute(value, "grp", [(g, (g + step) % groups) for g in range(groups)]))
+    return jnp.stack(parts)[(me - jnp.arange(groups)) % groups].sum(0)
+
+
+def sum_and_scatter(parts):
+    shape = parts.shape[1:]
+    parts = parts.reshape(4, 4, 2, *shape)
+    parts = jnp.moveaxis(parts, (2, 1), (0, 1)).reshape(2, 16, *shape)
+    for axis in ("c", "x", "y"):
+        parts = lax.all_to_all(parts, axis, split_axis=0, concat_axis=0, tiled=True)
+        parts = parts.astype(jnp.float32).sum(0)
+        if axis != "y":
+            parts = parts.astype(jnp.bfloat16)
+            parts = parts.reshape(4, -1, *shape) if axis == "c" else parts
+    return parts
 
 
 def layer_norm(value, gain, shift):
@@ -108,13 +85,10 @@
     return jnp.where(valid[:, None, None, :], scores, -1e30)
 
 
-def forward(ids, lengths, weights):
-    table, positions, w_qkv, w_out, w_up, w_down, norms = weights
+def forward(embedded, lengths, weights):
+    w_qkv, w_out, w_up, w_down, norms = weights
     norms = norms.astype(jnp.float32)
-    width = table.shape[1]
-    embedded = (
-        jnp.take(table, ids, axis=0).astype(jnp.float32) + positions.astype(jnp.float32)[None]
-    )
+    width = w_out.shape[1]
     first = layer_norm(embedded, norms[:, 0], norms[:, 1])
     first_low = first.astype(jnp.bfloat16)
     packed = project(first_low, w_qkv).astype(jnp.bfloat16)
@@ -149,7 +123,7 @@
 
 
 def backward(lengths, weights, saved, grad_final):
-    table, positions, w_qkv, w_out, w_up, w_down, norms = weights
+    w_qkv, w_out, w_up, w_down, norms = weights
     norms = norms.astype(jnp.float32)
     (
         embedded,
@@ -164,7 +138,7 @@
         active,
         summed,
     ) = saved
-    width = table.shape[1]
+    width = w_out.shape[1]
     grad_summed, gain_c, shift_c = norm_back(summed, norms[:, 4], norms[:, 5], grad_final)
     grad_ffn = grad_summed.astype(jnp.bfloat16)
     g_down = weight_grad(active, grad_ffn)
@@ -247,75 +221,146 @@
     masters = (s_table, s_pos, s_qkv, s_out, s_up, s_down, s_norms)
     momenta = (m_table, m_pos, m_qkv, m_out, m_up, m_down, m_norms)
     averages = (a_table, a_pos, a_qkv, a_out, a_up, a_down, a_norms)
-    lowered = tuple((weight.astype(jnp.bfloat16) for weight in masters))
-    student = jax.tree.map(
-        lambda part, own: part.astype(own.dtype),
-        lax.all_gather(for_sending(lowered), FSDP, axis=0, tiled=True),
-        lowered,
-    )
-    group_ids, group_lengths, group_picks, group_labels = in_one_piece(
-        (ids, lengths, picks, labels), "grp", 0, 1
-    )
-    teacher_rows = lax.all_gather(t_table, FSDP, axis=1, tiled=True)[0]
-    teacher = (teacher_rows, t_pos[0], t_qkv[0], t_out[0], t_up[0], t_down[0], t_norms[0])
-    teacher_final, _ = forward(group_ids, group_lengths, teacher)
-    taken = jnp.take_along_axis(teacher_final, group_picks[:, :, None], axis=1).astype(jnp.bfloat16)
-    teacher_logits = jnp.einsum(
-        "bpd,vd->bpv", taken, teacher_rows, preferred_element_type=jnp.float32
-    )
-    log_probs = jax.nn.log_softmax(teacher_logits, axis=-1)
-    group_counted = (group_picks < group_lengths[:, None]).astype(jnp.float32)
-    label_logp = jnp.take_along_axis(log_probs, group_labels[:, :, None], axis=2)[:, :, 0]
-    label_loss = -jnp.sum(group_counted * label_logp, -1) / jnp.maximum(
-        jnp.sum(group_counted, -1), 1.0
-    )
-    all_losses = gathered_copies(label_loss[None], "grp", 0)
-    blend = jax.nn.softmax(-all_losses, axis=0)
-    mine = lax.dynamic_index_in_dim(blend, lax.axis_index("grp"), 0, keepdims=False)
-    teacher_probs = jnp.exp(log_probs)
-    share = (mine[:, None, None] * teacher_probs).astype(jnp.bfloat16)
-    spread = (mine[:, None] * jnp.sum(teacher_probs * log_probs, -1)).astype(jnp.bfloat16)
-    target, entropy = tuple(
-        (part.astype(jnp.float32) for part in side_by_side((share, spread), "grp", 0, 2))
-    )
-    final, saved = forward(ids, lengths, student)
-    counted = (picks < lengths[:, None]).astype(jnp.float32)
-    rows_low = jnp.take_along_axis(final, picks[:, :, None], axis=1).astype(jnp.bfloat16)
-    logits = jnp.einsum("bpd,vd->bpv", rows_low, student[0], preferred_element_type=jnp.float32)
-    log_total = jax.scipy.special.logsumexp(logits, axis=-1)
-    per_row = entropy - jnp.sum(target * logits, -1) + log_total
-    loss_local = jnp.sum(counted * per_row)
+    f32, bf16 = jnp.float32, jnp.bfloat16
+    fsdp = lax.axis_size(FSDP)
+    width, t_width = s_table.shape[1], t_table.shape[2]
+    vocab_own = s_table.shape[0]
+    picked = picks.shape[1]
+    span = ids.shape[1]
+
+    facts = jnp.concatenate([ids, picks, labels, lengths[:, None]], axis=1)
+
+    def taken_apart(gathered):
+        i, p, l, n = jnp.split(gathered, [span, span + picked, span + 2 * picked], axis=1)
+        return i, p, l, n[:, 0]
+
+    group_ids, group_picks, _, group_lengths = taken_apart(
+        lax.all_gather(facts, "grp", axis=0, tiled=True)
+    )
+    teacher_rows = lax.all_gather(t_table[0], FSDP, axis=0, tiled=True)
+    plane_ids, plane_picks, plane_labels, plane_lengths = taken_apart(
+        lax.all_gather(facts, FSDP, axis=0, tiled=True)
+    )
+
+    lead = s_qkv.shape[0]
+    cols = [s_qkv, s_out, s_up, s_down.reshape(lead, -1), s_pos.reshape(lead, -1), s_norms]
+    widths = [c.shape[1] for c in cols]
+    packed_width = -(-sum(widths) // 128) * 128
+    starts = [sum(widths[:k]) for k in range(len(widths))]
+
+    def pack(parts):
+        pad = jnp.zeros((parts[0].shape[0], packed_width - sum(widths)), bf16)
+        return jnp.concatenate([part.astype(bf16) for part in parts] + [pad], axis=1)
+
+    own_packed, own_table, own_head, _ = lax.optimization_barrier(
+        (pack(cols), s_table.astype(bf16), t_table[0], teacher_rows)
+    )
+    packed = lax.all_gather(own_packed, FSDP, axis=0, tiled=True)
+    whole = [packed[:, at : at + w] for at, w in zip(starts, widths)]
+    w_qkv, w_out, w_up, w_down, positions, norms = whole
+    w_down = w_down.reshape(-1, width)
+    positions = positions.reshape(-1, width)
+    student = (w_qkv, w_out, w_up, w_down, norms)
+    table = lax.all_gather(own_table, FSDP, axis=0, tiled=True)
+    heads = lax.all_gather(own_head, "grp", axis=0, tiled=False)
+
+    teacher = (t_qkv[0], t_out[0], t_up[0], t_down[0], t_norms[0])
+    t_embedded = jnp.take(teacher_rows, group_ids, axis=0).astype(f32) + t_pos[0].astype(f32)[None]
+    teacher_final, _ = forward(t_embedded, group_lengths, teacher)
+    taken = jnp.take_along_axis(teacher_final, group_picks[:, :, None], axis=1).astype(bf16)
+    rows = lax.all_to_all(taken, "grp", split_axis=0, concat_axis=0, tiled=True)
+    rows = lax.all_gather(rows, FSDP, axis=0, tiled=False)
+
+    table, _ = lax.optimization_barrier((table, taken))
+    embedded = jnp.take(table, ids, axis=0).astype(f32) + positions.astype(f32)[None]
+    final, saved = forward(embedded, lengths, student)
+    own_rows = jnp.take_along_axis(final, picks[:, :, None], axis=1).astype(bf16)[0]
+    h = lax.all_gather(own_rows, FSDP, axis=0, tiled=True)
+    z = jnp.einsum("rd,vd->rv", h, own_table, preferred_element_type=f32)
+
+    logits = jnp.einsum("fkpd,kvd->kfpv", rows, heads, preferred_element_type=f32)
+    logits = logits.reshape(logits.shape[0], -1, vocab_own)
+    base = lax.axis_index(FSDP) * vocab_own
+    column = lax.broadcasted_iota(jnp.int32, (1, 1, vocab_own), 2) + base
+    at_label = column == plane_labels.reshape(1, -1, 1)
+    top = jnp.max(logits, -1)
+    spread = jnp.exp(logits - top[..., None])
+    stats = [
+        top,
+        jnp.sum(spread, -1),
+        jnp.sum(spread * logits, -1),
+        jnp.sum(jnp.where(at_label, logits, 0.0), -1),
+    ]
+    z_top = jnp.max(z, -1)
+    z_stats = [z_top, jnp.sum(jnp.exp(z - z_top[:, None]), -1)]
+    sent = jnp.concatenate(stats + [s[None] for s in z_stats], axis=0)
+    sent = jnp.moveaxis(sent.reshape(-1, fsdp, picked), 1, 0)
+    seen = lax.all_to_all(sent, FSDP, split_axis=0, concat_axis=0, tiled=True)
+    tops, sums, dots, hits = [seen[:, 4 * j : 4 * j + 4] for j in range(4)]
+
+    def log_sum(tops, sums):
+        best = jnp.max(tops, 0)
+        scale = jnp.exp(tops - best)
+        return best, scale, jnp.sum(sums * scale, 0)
+
+    best, scale, total = log_sum(tops, sums)
+    t_lse = best + jnp.log(total)
+    t_ent = jnp.sum(dots * scale, 0) / total - t_lse
+    label_logp = jnp.sum(hits, 0) - t_lse
+    s_best, _, s_total = log_sum(seen[:, 16], seen[:, 17])
+    s_lse = s_best + jnp.log(s_total)
+    counted = (picks < lengths[:, None]).astype(f32)[0]
     count_local = jnp.sum(counted)
-    grad_logits = (counted[:, :, None] * (jnp.exp(logits - log_total[:, :, None]) - target)).astype(
-        jnp.bfloat16
-    )
-    grad_rows = jnp.einsum(
-        "bpv,vd->bpd", grad_logits, student[0], preferred_element_type=jnp.float32
-    )
-    grad_final = jnp.zeros(final.shape, jnp.float32).at[0, picks[0]].add(grad_rows[0])
+    label_loss = -jnp.sum(counted[None] * label_logp, -1) / jnp.maximum(count_local, 1.0)
+    log_blend = jax.nn.log_softmax(-label_loss)
+    blend = jax.nn.softmax(-label_loss)
+    entropy = jnp.sum((blend[:, None] * t_ent).astype(bf16).astype(f32), 0)
+    shift = jnp.concatenate([log_blend[:, None] - t_lse, s_lse[None]], axis=0)
+    shift = jnp.moveaxis(from_everyone(shift, FSDP), 0, 1).reshape(5, -1)
+
+    plane_counted = (plane_picks < plane_lengths[:, None]).astype(f32).reshape(-1)
+    target = jnp.sum(jnp.exp(logits + shift[:4, :, None]).astype(bf16).astype(f32), 0)
+    loss_local = jnp.sum(counted * (entropy + s_lse)) - jnp.sum(
+        plane_counted * jnp.sum(target * z, -1)
+    )
+    grad_logits = (plane_counted[:, None] * (jnp.exp(z - shift[4][:, None]) - target)).astype(bf16)
+    grad_rows = jnp.einsum("rv,vd->rd", grad_logits, own_table, preferred_element_type=f32)
+    grad_rows = sum_and_scatter(grad_rows.astype(bf16).reshape(fsdp, picked, width))
+    head_grad = jnp.einsum("rv,rd->vd", grad_logits, h, preferred_element_type=f32)
+
+    loss_count = sum_of_groups(jnp.stack([loss_local, count_local]))
+    grad_final = jnp.zeros(final.shape, f32).at[0, picks[0]].add(grad_rows)
     terms = backward(lengths, student, saved, grad_final)
     grad_embedded = terms[0]
-    width = s_table.shape[1]
-    head_grad = jnp.einsum("bpv,bpd->vd", grad_logits, rows_low, preferred_element_type=jnp.float32)
-    g_lookup = (
-        jnp.zeros((student[0].shape[0], width), jnp.float32)
-        .at[ids.reshape(-1)]
-        .add(grad_embedded.reshape(-1, width))
-    )
-    table_part = lax.psum_scatter(
-        (g_lookup + head_grad).astype(jnp.bfloat16), FSDP, scatter_dimension=0, tiled=True
-    ).astype(jnp.float32)
-    rest = jax.tree.map(
-        lambda part: part.astype(jnp.float32),
-        lax.psum_scatter(for_sending(terms[1:]), FSDP, scatter_dimension=0, tiled=True),
-    )
-    shards = jax.tree.map(
-        lambda part: part.astype(jnp.float32),
-        lax.psum(for_sending((table_part,) + tuple(rest)), "grp"),
-    )
-    squares = sum((jnp.sum(piece * piece) for piece in shards))
-    loss_sum, count = (over_axes(loss_local, GRP_FSDP), over_axes(count_local, GRP_FSDP))
-    squares = of_everyone(squares, FSDP)
+    everyones = lax.all_gather(grad_embedded[0].astype(bf16), FSDP, axis=0, tiled=True)
+    own_id = lax.broadcasted_iota(jnp.int32, (vocab_own, 1), 0) + base
+    at_id = (own_id == plane_ids.reshape(1, -1)).astype(bf16)
+    g_lookup = jnp.dot(at_id, everyones, preferred_element_type=f32)
+    table_part = (head_grad + g_lookup).astype(bf16)
+    g_pos, g_qkv, g_out, g_up, g_down, g_norms = terms[1:]
+    whole_lead = g_qkv.shape[0]
+    parts = pack(
+        [g_qkv, g_out, g_up, g_down.reshape(whole_lead, -1), g_pos.reshape(whole_lead, -1), g_norms]
+    )
+    rest = sum_and_scatter(parts.reshape(fsdp, lead, packed_width)).astype(bf16)
+    table_sum, rest_sum = lax.psum((table_part, rest), "grp")
+    table_sum, rest_sum = table_sum.astype(f32), rest_sum.astype(f32)
+    squares = jnp.sum(table_sum * table_sum) + jnp.sum(rest_sum * rest_sum)
+    scalars = jnp.concatenate([squares[None], loss_count])
+    scalars = from_everyone(scalars, FSDP).sum(0)
+    squares, loss_sum, count = scalars[0], scalars[1], scalars[2]
+    r_qkv, r_out, r_up, r_down, r_pos, r_norms = [
+        rest_sum[:, at : at + w] for at, w in zip(starts, widths)
+    ]
+    shards = (
+        table_sum,
+        r_pos.reshape(s_pos.shape),
+        r_qkv,
+        r_out,
+        r_up,
+        r_down.reshape(s_down.shape),
+        r_norms,
+    )
     clip_norm = jnp.sqrt(squares) / count
     factor = jnp.minimum(1.0, clip_limit / clip_norm) / count
     new_weights, new_moments, new_averages = ([], [], [])
@@ -333,7 +378,7 @@
 
 def solution(mesh):
     finer = Mesh(
-        mesh.devices.reshape(mesh.shape["grp"], 4, 4, 2), ("grp", "fsdp_0", "fsdp_1", "fsdp_2")
+        mesh.devices.reshape(mesh.shape["grp"], 4, 4, 2), ("grp", "y", "x", "c")
     )
     return jax.shard_map(
         per_device,

time: 1380 us -> 915 us (0.66)
  waiting for transfers between devices: 773 us -> 339 us
  local copies, waits for them, and re-layouts: 52.9 us -> 125 us
  other arithmetic: 186 us -> 131 us
  matrix products: 201 us -> 165 us
  blocking collectives: 125 us -> 93 us
  starting transfers between devices: 9.5 us -> 28.6 us
    reduce_scatter x7 -> x0, waiting for transfers between devices: 588 us -> none  [the longest x5 374 us: per_device(): lax.psum_scatter(for_sending(terms[1:]), FSDP, scatter_dimension=0, tiled...]
    all_gather x5 -> x7, waiting for transfers between devices: 127 us -> 229 us  [the longest x1 138 us: per_device(): teacher_rows = lax.all_gather(t_table[0], FSDP, axis=0, tiled=True)]
    all_to_all x1 -> x5, blocking collectives: 8.22 us -> 55.4 us  [the longest x4 45.9 us: sum_and_scatter(): parts = lax.all_to_all(parts, axis, split_axis=0, concat_axis=0, tiled=True)]
    all_gather x4 -> x2, blocking collectives: 82.2 us -> 37.5 us  [the longest x1 29 us: per_device(): lax.all_gather(facts, FSDP, axis=0, tiled=True)]
    all_to_all x0 -> x3, waiting for transfers between devices: none -> 42.9 us  [the longest x2 36.4 us: sum_and_scatter(): parts = lax.all_to_all(parts, axis, split_axis=0, concat_axis=0, tiled=True)]
    convert_element_type x11 -> x13, other arithmetic: 58.7 us -> 21.9 us  [the longest x6 8.22 us: pack(): part.astype(bf16)]
    dot_general x4 -> x5, matrix products: 86.8 us -> 51.3 us  [the longest x1 22.8 us: per_device(): jnp.einsum('fkpd,kvd->kfpv', rows, heads, preferred_element_type=f32)]
    psum x4 -> x0, blocking collectives: 35 us -> none  [over_axes(): return functools.reduce(lax.psum, axes, value)]
  transfers between devices with their start and end apart: 16 -> 16, of which waited for: 11 -> 11; matrix products, arithmetic and copies ran while one was open for 27% -> 31% of each run, Pallas kernels for 0% -> 0%
where the time goes in v1:
time: 915 us; the launch traced here: 906 us
  waiting for transfers between devices  339 us (37%)
  matrix products  165 us (18%)
  other arithmetic  131 us (14%)
  local copies, waits for them, and re-layouts  125 us (14%)
  blocking collectives  93 us (10%)
  starting transfers between devices  28.6 us (3%)
  between operations  24.8 us (3%)
    all_gather x1, waiting for transfers between devices, per_device(): teacher_rows = lax.all_gather(t_table[0], FSDP, axis=0, tiled=True)  138 us
    dot_general x8, matrix products, project(): jnp.einsum('blk,kn->bln', left, right, preferred_element_type=jnp.float32)  67.5 us
    all_gather x1, waiting for transfers between devices, per_device(): rows = lax.all_gather(rows, FSDP, axis=0, tiled=False)  65.8 us
    psum x1, waiting for transfers between devices, per_device(): table_sum, rest_sum = lax.psum((table_part, rest), 'grp')  57.1 us
    all_to_all x4, blocking collectives, sum_and_scatter(): parts = lax.all_to_all(parts, axis, split_axis=0, concat_axis=0, tiled=True)  45.9 us
    all_to_all x2, waiting for transfers between devices, sum_and_scatter(): parts = lax.all_to_all(parts, axis, split_axis=0, concat_axis=0, tiled=True)  36.4 us
    all_gather x1, blocking collectives, per_device(): lax.all_gather(facts, FSDP, axis=0, tiled=True)  29 us
    unnamed x264, local copies, waits for them, and re-layouts  23.2 us
  transfers between devices with their start and end apart: 16, of which 11 were waited for; matrix products, arithmetic and copies ran while one was open for 31% of the time, Pallas kernels for 0%

profile of v1, /device:TPU:1, one launch (start us, length us, event | category | flops | bytes accessed | tf_op | source)
XLA Modules:
  0.0 905.8 jit_solution(12164956379023287293)
XLA Ops:
  20.4 2.6 convert_element_type.293
  25.4 137.7 %all-gather.20.cloned.1.call-done = bf16[1,30720,768]{2,1,0:T(8,128)(2,1)} async-done(((bf16[1,960,768]{2,1,0:T(8,128)(2,1)}), bf16[1,30720,768]{2,1,0:T(8,128)(2,1)}) %all-gather.20.cloned.1.call-update) | async-done | bytes 47185936 | tf_op jit(solution)/shard_map/all_gather | solution.py:240
  165.3 8.5 all-gather.5
  179.1 18.8 %gather_fusion = bf16[1024,768]{1,0:T(8,128)(2,1)} fusion(bf16[30720,768]{1,0:T(8,128)(2,1)} %bitcast.239, s32[1024]{0:T(1024)S(1)} %broadcast_clamp_fusion), kind=kCustom, calls=%fused_computation | custom fusion | bytes 3149824 | tf_op jit(solution)/shard_map/jit(_take)/gather | solution.py:268
  197.9 2.5 fusion.31
  202.5 4.6 convolution_convert_fusion
  208.8 2.6 copy.424
  214.7 10.7 %fusion.196 = (f32[4,12,256]{2,1,0:T(8,128)S(1)}, f32[4,12,256,256]{2,3,1,0:T(8,128)}) fusion(pred[4,256]{1,0:T(4,128)(4,1)S(1)} %copy-done.118, bf16[4,256,12,64]{1,3,2,0:T(8,128)(2,1)S(1)} %bitcast.242, bf16[4,256,12,64]{1,3,2,0:T(8,128)(2,1)} %bitcast.243), kind=kOutput, calls=%fused_computation.380 | convolution fusion | flops 415236352 | bytes 15778816 | tf_op jit(solution)/shard_map/sub | solution.py:99
  225.4 6.9 fusion.59
  232.3 2.3 fusion.197
  236.8 12.6 %fusion.33 = (u8[256,3072]{1,0:T(8,128)(4,1)S(1)}, u8[256,3072]{1,0:T(8,128)(4,1)S(1)}, f32[4,256,3072]{2,1,0:T(8,128)S(1)}) fusion(bf16[1,768,3072]{2,1,0:T(8,128)(2,1)} %param.61, f32[4,256,768]{2,1,0:T(8,128)} %copy-done.16, f32[768]{0:T(1024)S(1)} %copy-done.97, f32[768]{0:T(1024)S(1)} %copy-done.98, f32[4,256]{1,0:T(4,128)S(1)} %add_rsqrt_fusion.1, ...), kind=kOutput, calls=%fused_computation.73 | convolution fusion | flops 4875091968 | bytes 22034432 | tf_op jit(solution)/shard_map/blk,kn->bln/dot_general | solution.py:61
  249.5 35.6 %fusion.198 = (f32[4,256]{1,0:T(4,128)S(1)}, f32[4,256,768]{2,1,0:T(8,128)S(1)}) fusion(bf16[1,3072,768]{2,1,0:T(8,128)(2,1)} %param.62, f32[4,256,3072]{2,1,0:T(8,128)S(1)} %get-tuple-element.339, u8[256,3072]{1,0:T(8,128)(4,1)S(1)} %get-tuple-element.252, u8[256,3072]{1,0:T(8,128)(4,1)S(1)} %get-tuple-element.251, f32[768]{0:T(1024)S(1)} %copy-done.97, ...), kind=kOutput, calls=%fused_computation.382 | convolution fusion | flops 5056756736 | bytes 25184256 | tf_op jit(solution)/shard_map/blk,kn->bln/dot_general | solution.py:61
  286.4 2.4 gather_fusion.4
  289.0 9.5 %all_to_all.51 = bf16[4,64,768]{2,1,0:T(8,128)(2,1)} all-to-all(bf16[4,64,768]{2,1,0:T(8,128)(2,1)S(1)} %select_convert_fusion), channel_id=1, replica_groups=mesh['grp'=4,'y'=4,'x'=4,'c'=2] {'grp'}, dimensions={0} | all-to-all | bytes 786432 | tf_op jit(solution)/shard_map/all_to_all | solution.py:271
  298.6 29.0 %all-gather.4 = s32[32,1,385]{2,1,0:T(1,128)S(1)} all-gather(s32[1,1,385]{2,1,0:T(1,128)S(1)} %copy-done.63), channel_id=1, replica_groups=mesh['grp'=4,'y'=4,'x'=4,'c'=2] {'y','x','c'}, dimensions={0}, use_global_device_ids=true | all-gather | bytes 50820 | tf_op jit(solution)/shard_map/all_gather | solution.py:242
  331.8 3.3 slice.205
  335.0 4.5 reshape.1258
  341.4 3.1 gather_fusion.1
  345.0 2.3 fusion.36
  356.2 7.8 multiply_convert_fusion.2
  366.7 20.3 %all-gather.24.cloned.1.call-done = bf16[3840,768]{1,0:T(8,128)(2,1)} async-done(((bf16[960,768]{1,0:T(8,128)(2,1)}), bf16[3840,768]{1,0:T(8,128)(2,1)}) %all-gather.24.cloned.1.call-update) | async-done | bytes 5898256 | tf_op jit(solution)/shard_map/all_gather | solution.py:265
  387.0 65.8 %all-gather.22.cloned.1.call-done = bf16[128,64,768]{2,1,0:T(8,128)(2,1)} async-done(((bf16[4,64,768]{2,1,0:T(8,128)(2,1)}), bf16[128,64,768]{2,1,0:T(8,128)(2,1)}) %all-gather.22.cloned.1.call-update) | async-done | bytes 12582928 | tf_op jit(solution)/shard_map/all_gather | solution.py:272
  452.8 22.8 %fusion.199 = (f32[4,32,64]{2,1,0:T(8,128)S(1)}, f32[4,32,64,960]{3,2,1,0:T(8,128)}) fusion(bf16[4,960,768,1]{2,1,3,0:T(8,128)(2,1)} %bitcast.281, bf16[32,4,64,768]{3,2,1,0:T(8,128)(2,1)} %bitcast.280), kind=kOutput, calls=%fused_computation.383 | convolution fusion | flops 12087451648 | bytes 49971200 | tf_op jit(solution)/shard_map/fkpd,kvd->kfpv/dot_general | solution.py:281
  475.6 18.1 %multiply_reduce_fusion = (f32[4,32,64]{2,1,0:T(8,128)S(1)}, f32[4,32,64]{2,1,0:T(8,128)S(1)}, f32[4,32,64]{2,1,0:T(8,128)S(1)}) fusion(f32[4,32,64,960]{3,2,1,0:T(8,128)} %get-tuple-element.343, f32[4,32,64]{2,1,0:T(8,128)S(1)} %get-tuple-element.342, pred[32,64,960]{2,1,0:T(8,128)(4,1)S(1)} %broadcast_compare_fusion), kind=kLoop, calls=%fused_computation.11 | loop fusion | flops 47161344 | bytes 33554432 | tf_op jit(solution)/shard_map/reduce_sum | solution.py:291
  493.8 5.0 all-gather.18.cloned.1.call-done
  498.8 7.2 fusion.203
  506.0 4.3 exponential_reduce_fusion
  513.2 5.1 all-to-all-start.1
  519.6 6.4 all-to-all-done.1
  533.3 3.8 all-to-all-start.2
  538.0 6.6 all-to-all-done.2
  545.5 17.6 %convert_reduce_fusion = f32[32,64,960]{2,1,0:T(8,128)} fusion(f32[4,32,64,960]{3,2,1,0:T(8,128)} %get-tuple-element.343, f32[4,32,64]{2,1,0:T(8,128)S(1)} %copy.436), kind=kLoop, calls=%fused_computation.8 | loop fusion | flops 29491200 | bytes 39354368 | tf_op jit(solution)/shard_map/reduce_sum | solution.py:322
  563.1 9.0 copy.437
  572.3 6.7 multiply_convert_fusion
  579.0 2.5 convolution_convert_fusion.3
  581.7 6.3 all_to_all.52
  590.2 17.3 %all_to_all.53 = bf16[4,4,64,512]{3,2,1,0:T(8,128)(2,1)S(1)} all-to-all(bf16[4,4,64,512]{3,2,1,0:T(8,128)(2,1)S(1)} %bitcast.238), channel_id=1, replica_groups=mesh['grp'=4,'y'=4,'x'=4,'c'=2] {'x'}, dimensions={0} | all-to-all | bytes 2097152 | tf_op jit(solution)/shard_map/all_to_all | solution.py:40
  607.7 8.0 all_to_all.54
  620.3 3.6 add_convert_fusion
  624.0 3.5 fusion.104
  629.4 2.2 convolution_convert_fusion.7
  634.6 2.8 multiply_reduce_fusion.7
  641.5 3.4 convolution_convert_fusion.1
  644.9 3.2 convert_element_type.343
  652.2 3.4 convolution_convert_fusion.4
  655.7 2.2 convolution_convert_fusion.2
  657.9 11.6 %concatenate.52 = bf16[512,6528]{1,0:T(8,128)(2,1)} concatenate(bf16[512,1536]{1,0:T(8,128)(2,1)} %convolution_convert_fusion.4, bf16[512,512]{1,0:T(8,128)(2,1)S(1)} %copy.443, bf16[512,2048]{1,0:T(8,128)(2,1)} %convolution_convert_fusion.2, bf16[512,2048]{1,0:T(8,128)(2,1)S(1)} %convert_element_type.343, bf16[512,256]{1,0:T(8,128)(2,1)S(1)} %copy-done.25, ...), dimensions={1} | concatenate | bytes 13369344 | tf_op jit(solution)/shard_map/concatenate | solution.py:253
  669.5 3.5 copy.450
  673.0 14.3 %all_to_all.55 = bf16[2,16,16,6528]{3,2,1,0:T(8,128)(2,1)} all-to-all(bf16[2,16,16,6528]{3,2,1,0:T(8,128)(2,1)S(1)} %bitcast.231), channel_id=1, replica_groups=mesh['grp'=4,'y'=4,'x'=4,'c'=2] {'c'}, dimensions={0} | all-to-all | bytes 13369344 | tf_op jit(solution)/shard_map/all_to_all | solution.py:40
  687.3 6.9 reduce_sum.620
  694.1 3.8 all-to-all-start.7
  703.1 34.5 %all-to-all-done.7 = bf16[4,4,16,6528]{3,2,1,0:T(8,128)(2,1)S(1)} async-done(((bf16[4,4,16,6528]{3,2,1,0:T(8,128)(2,1)}), bf16[4,4,16,6528]{3,2,1,0:T(8,128)(2,1)S(1)}, u32[]{:S(2)}, u32[]{:S(2)}) %all-to-all-start.7) | async-done | bytes 3342368 | tf_op jit(solution)/shard_map/all_to_all | solution.py:40
  739.2 3.6 all-to-all-start.8
  747.2 5.6 fusion.204
  756.7 13.3 %add_convert_fusion.1 = bf16[960,512]{1,0:T(8,128)(2,1)} fusion(f32[960,512]{1,0:T(8,128)} %fusion.204, bf16[1,8192,512]{2,1,0:T(8,128)(2,1)} %all-gather.26.cloned.1.call-done, s32[8192]{0:T(1024)S(1)} %bitcast.274, s32[960]{0:T(1024)S(1)} %copy-done.65), kind=kOutput, calls=%fused_computation.112 | convolution fusion | flops 8061911040 | bytes 11374336 | tf_op jit(solution)/shard_map/dot_general | solution.py:338
  772.8 2.7 collective-permute-start.2
  780.1 57.1 %all-reduce.4.cloned.1.call-done = (bf16[960,512]{1,0:T(8,128)(2,1)}, bf16[16,6528]{0,1:T(8,128)(2,1)}) async-done(((bf16[960,512]{1,0:T(8,128)(2,1)}, bf16[16,6528]{0,1:T(8,128)(2,1)}), (bf16[960,512]{1,0:T(8,128)(2,1)}, bf16[16,6528]{0,1:T(8,128)(2,1)})) %all-reduce.4.cloned.1.call-update) | async-done | bytes 1191952 | tf_op jit(solution)/shard_map/psum | solution.py:346
  837.3 2.3 fusion.53
  839.6 2.9 multiply_reduce_fusion.2
  844.5 7.9 all-to-all-start.9
  864.4 3.2 multiply_add_fusion.5
  873.3 4.1 multiply_add_fusion.4
  877.5 2.3 copy.473
  888.4 6.5 multiply_add_fusion.3
  (461 shorter events, 130.5 us)
Async XLA Ops:
  7.2 195.3 %copy-start = (bf16[1,768,2304]{2,1,0:T(8,128)(2,1)S(1)}, bf16[1,768,2304]{2,1,0:T(8,128)(2,1)}, u32[]{:S(2)}) copy-start(bf16[1,768,2304]{2,1,0:T(8,128)(2,1)} %param.59) | copy-start | bytes 10616836
  7.2 155.9 %all-gather.20.cloned.1.call-start = ((), (), s32[]{:S(2)}) async-start(), calls=%async_computation.13 | async-start | bytes 48660480 | tf_op jit(solution)/shard_map/all_gather | solution.py:240
  7.9 321.7 %all-gather.16.cloned.1.call-start = ((), (), s32[]{:S(2)}) async-start(), calls=%async_computation.11 | async-start | bytes 6893568 | tf_op jit(solution)/shard_map/all_gather | solution.py:258
  163.1 178.3 %all-gather.14.cloned.1.call-start = ((), (), s32[]{:S(2)}) async-start(), calls=%async_computation.10 | async-start | bytes 32440320 | tf_op jit(solution)/shard_map/all_gather | solution.py:264
  163.8 223.2 %all-gather.24.cloned.1.call-start = ((), (), s32[]{:S(2)}) async-start(), calls=%async_computation.15 | async-start | bytes 7372800 | tf_op jit(solution)/shard_map/all_gather | solution.py:265
  165.3 8.6 copy-start.62
  236.8 216.0 %all-gather.22.cloned.1.call-start = ((), (), s32[]{:S(2)}) async-start(), calls=%async_computation.14 | async-start | bytes 12976128 | tf_op jit(solution)/shard_map/all_gather | solution.py:272
  236.8 12.7 %copy-start.17 = (f32[4,256,768]{2,1,0:T(8,128)S(1)}, f32[4,256,768]{2,1,0:T(8,128)}, u32[]{:S(2)}) copy-start(f32[4,256,768]{2,1,0:T(8,128)} %copy-done.16) | copy-start | bytes 9437188
  286.4 12.2 %copy-start.63 = (s32[1,1,385]{2,1,0:T(1,128)S(1)}, s32[1,1,385]{2,1,0:T(1,128)}, u32[]{:S(2)}) copy-start(s32[1,1,385]{2,1,0:T(1,128)} %copy-done.62) | copy-start | bytes 4624
  286.4 41.3 %copy-start.96 = (s32[1,256]{1,0:T(1,128)S(1)}, s32[1,256]{1,0:T(1,128)}, u32[]{:S(2)}) copy-start(s32[1,256]{1,0:T(1,128)} %param.32) | copy-start | bytes 3076
  286.4 41.4 %copy-start.106 = (s32[1,64]{1,0:T(1,128)S(1)}, s32[1,64]{1,0:T(1,128)}, u32[]{:S(2)}) copy-start(s32[1,64]{1,0:T(1,128)} %param.34) | copy-start | bytes 772
  298.5 200.3 %all-gather.18.cloned.1.call-start = ((), (), s32[]{:S(2)}) async-start(), calls=%async_computation.12 | async-start | bytes 2162688 | tf_op jit(solution)/shard_map/all_gather | solution.py:278
  327.6 209.7 %copy-start.44 = (s32[32,1,385]{2,0,1:T(8,128)}, s32[32,1,385]{2,0,1:T(8,128)S(1)}, u32[]{:S(2)}) copy-start(s32[32,1,385]{2,0,1:T(8,128)S(1)} %copy.502) | copy-start | bytes 147844
  327.7 26.6 %copy-start.105 = (pred[256]{0:T(512)(128)(4,1)}, pred[256]{0:T(512)(128)(4,1)S(1)}, u32[]{:S(2)}) copy-start(pred[256]{0:T(512)(128)(4,1)S(1)} %get-tuple-element.313) | copy-start | bytes 772
  341.3 13.0 %copy-start.89 = (f32[512]{0:T(512)}, f32[512]{0:T(512)S(1)}, u32[]{:S(2)}) copy-start(f32[512]{0:T(512)S(1)} %get-tuple-element.269) | copy-start | bytes 6148
  341.3 13.0 %copy-start.104 = (f32[512]{0:T(512)}, f32[512]{0:T(512)S(1)}, u32[]{:S(2)}) copy-start(f32[512]{0:T(512)S(1)} %get-tuple-element.268) | copy-start | bytes 6148
  341.3 22.7 %copy-start.60 = (f32[512]{0:T(512)}, f32[512]{0:T(512)S(1)}, u32[]{:S(2)}) copy-start(f32[512]{0:T(512)S(1)} %get-tuple-element.267) | copy-start | bytes 6148
  341.3 22.7 %copy-start.87 = (f32[512]{0:T(512)}, f32[512]{0:T(512)S(1)}, u32[]{:S(2)}) copy-start(f32[512]{0:T(512)S(1)} %get-tuple-element.266) | copy-start | bytes 6148
  344.4 9.9 %copy-start.26 = (bf16[256,512]{1,0:T(8,128)(2,1)}, bf16[256,512]{1,0:T(8,128)(2,1)S(1)}, u32[]{:S(2)}) copy-start(bf16[256,512]{1,0:T(8,128)(2,1)S(1)} %gather_fusion.1) | copy-start | bytes 786436
  344.7 9.7 %copy-start.75 = (f32[256]{0:T(256)}, f32[256]{0:T(256)S(1)}, u32[]{:S(2)}) copy-start(f32[256]{0:T(256)S(1)} %broadcast_multiply_fusion.11) | copy-start | bytes 3076
  344.9 9.4 %copy-start.92 = (f32[256]{0:T(256)}, f32[256]{0:T(256)S(1)}, u32[]{:S(2)}) copy-start(f32[256]{0:T(256)S(1)} %fusion.124) | copy-start | bytes 3076
  355.9 8.1 copy-start.10
  355.9 8.1 copy-start.73
  356.1 7.9 copy-start.79
  356.2 7.9 copy-start.82
  356.2 7.9 copy-start.19
  365.1 110.5 %copy-start.81 = (f32[256]{0:T(256)}, f32[256]{0:T(256)S(1)}, u32[]{:S(2)}) copy-start(f32[256]{0:T(256)S(1)} %multiply_reduce_fusion.9) | copy-start | bytes 3076
  365.1 110.5 %copy-start.72 = (f32[256]{0:T(256)}, f32[256]{0:T(256)S(1)}, u32[]{:S(2)}) copy-start(f32[256]{0:T(256)S(1)} %fusion.126) | copy-start | bytes 3076
  506.0 21.8 %copy-start.113 = (f32[64]{0:T(128)S(1)}, f32[64]{0:T(128)}, u32[]{:S(2)}) copy-start(f32[64]{0:T(128)} %fusion.131) | copy-start | bytes 772
  506.0 26.0 %copy-start.107 = (s32[1,64]{1,0:T(1,128)S(1)}, s32[1,64]{1,0:T(1,128)}, u32[]{:S(2)}) copy-start(s32[1,64]{1,0:T(1,128)} %param.34) | copy-start | bytes 772
  513.2 12.9 %all-to-all-start.1 = ((f32[32,1,1152]{2,1,0:T(1,128)}), f32[32,1,1152]{2,1,0:T(1,128)S(1)}, u32[]{:S(2)}, u32[]{:S(2)}) async-start(f32[32,1,1152]{2,1,0:T(1,128)} %reshape.1369), calls=%async_computation.1 | async-start | bytes 294912 | tf_op jit(solution)/shard_map/all_to_all | solution.py:298
  533.3 11.2 %all-to-all-start.2 = ((f32[32,1,320]{2,1,0:T(1,128)}), f32[32,1,320]{2,1,0:T(1,128)S(1)}, u32[]{:S(2)}, u32[]{:S(2)}) async-start(f32[32,1,320]{2,1,0:T(1,128)} %reshape.1371), calls=%async_computation.2 | async-start | bytes 98304 | tf_op jit(solution)/shard_map/all_to_all | solution.py:23
  537.2 219.5 %all-gather.26.cloned.1.call-start = ((), (), s32[]{:S(2)}) async-start(), calls=%async_computation.16 | async-start | bytes 8650752 | tf_op jit(solution)/shard_map/all_gather | solution.py:335
  607.7 12.6 %copy-start.20 = (bf16[2048,512]{1,0:T(8,128)(2,1)S(1)}, bf16[2048,512]{1,0:T(8,128)(2,1)}, u32[]{:S(2)}) copy-start(bf16[2048,512]{1,0:T(8,128)(2,1)} %reshape.1258) | copy-start | bytes 6291460
  694.1 43.5 %all-to-all-start.7 = ((bf16[4,4,16,6528]{3,2,1,0:T(8,128)(2,1)}), bf16[4,4,16,6528]{3,2,1,0:T(8,128)(2,1)S(1)}, u32[]{:S(2)}, u32[]{:S(2)}) async-start(bf16[4,4,16,6528]{3,2,1,0:T(8,128)(2,1)} %bitcast.78), calls=%async_computation.7 | async-start | bytes 6684672 | tf_op jit(solution)/shard_map/all_to_all | solution.py:40
  703.1 41.9 %copy-start.54 = (f32[16,512]{1,0:T(8,128)S(1)}, f32[16,512]{1,0:T(8,128)}, u32[]{:S(2)}) copy-start(f32[16,512]{1,0:T(8,128)} %param.39) | copy-start | bytes 98308
  703.1 42.7 %copy-start.36 = (f32[16,2048]{1,0:T(8,128)S(1)}, f32[16,2048]{1,0:T(8,128)}, u32[]{:S(2)}) copy-start(f32[16,2048]{1,0:T(8,128)} %param.40) | copy-start | bytes 393220
  739.2 7.9 copy-start.56
  739.2 7.9 copy-start.115
  739.2 15.5 %all-to-all-start.8 = ((bf16[4,16,6528]{2,1,0:T(8,128)(2,1)}), bf16[4,16,6528]{2,1,0:T(8,128)(2,1)S(1)}, u32[]{:S(2)}, u32[]{:S(2)}) async-start(bf16[4,16,6528]{2,1,0:T(8,128)(2,1)} %reduce_sum.621), calls=%async_computation.8 | async-start | bytes 1671168 | tf_op jit(solution)/shard_map/all_to_all | solution.py:40
  742.9 94.4 %all-reduce.4.cloned.1.call-start = ((), (), s32[]{:S(2)}) async-start(), calls=%async_computation.17 | async-start | bytes 5308416 | tf_op jit(solution)/shard_map/psum | solution.py:346
  747.2 9.5 %copy-start.65 = (s32[960]{0:T(1024)S(1)}, s32[960]{0:T(1024)}, u32[]{:S(2)}) copy-start(s32[960]{0:T(1024)} %copy-done.64) | copy-start | bytes 11524
  756.7 13.3 %copy-start.59 = (f32[16,512]{1,0:T(8,128)S(1)}, f32[16,512]{1,0:T(8,128)}, u32[]{:S(2)}) copy-start(f32[16,512]{1,0:T(8,128)} %param.46) | copy-start | bytes 98308
  756.7 13.4 %copy-start.55 = (f32[16,2048]{1,0:T(8,128)S(1)}, f32[16,2048]{1,0:T(8,128)}, u32[]{:S(2)}) copy-start(f32[16,2048]{1,0:T(8,128)} %param.47) | copy-start | bytes 393220
  756.7 13.5 %copy-start.71 = (pred[32,64]{1,0:T(8,128)(4,1)S(1)}, pred[32,64]{1,0:T(8,128)(4,1)}, u32[]{:S(2)}) copy-start(pred[32,64]{1,0:T(8,128)(4,1)} %get-tuple-element.306) | copy-start | bytes 6148
  770.0 82.4 %copy-start.43 = (f32[16,1536]{1,0:T(8,128)S(1)}, f32[16,1536]{1,0:T(8,128)}, u32[]{:S(2)}) copy-start(f32[16,1536]{1,0:T(8,128)} %broadcast_multiply_fusion.2) | copy-start | bytes 294916
  770.0 83.6 %copy-start.42 = (f32[16,1536]{1,0:T(8,128)S(1)}, f32[16,1536]{1,0:T(8,128)}, u32[]{:S(2)}) copy-start(f32[16,1536]{1,0:T(8,128)} %broadcast_multiply_fusion.3) | copy-start | bytes 294916
  770.0 86.4 %copy-start.38 = (f32[16,2048]{1,0:T(8,128)S(1)}, f32[16,2048]{1,0:T(8,128)}, u32[]{:S(2)}) copy-start(f32[16,2048]{1,0:T(8,128)} %broadcast_multiply_fusion) | copy-start | bytes 393220
  772.8 4.7 collective-permute-start.2
  775.4 3.9 collective-permute-start.1
  775.9 3.6 collective-permute-start
  844.5 16.2 %all-to-all-start.9 = ((f32[32,1,3]{2,1,0:T(1,128)}), f32[32,1,3]{2,1,0:T(1,128)S(1)}, u32[]{:S(2)}, u32[]{:S(2)}) async-start(f32[32,1,3]{2,1,0:T(1,128)} %broadcast_in_dim.220), calls=%async_computation.9 | async-start | bytes 32768 | tf_op jit(solution)/shard_map/all_to_all | solution.py:23
  860.7 12.6 %copy-start.5 = (f32[16,6528]{0,1:T(8,128)}, f32[16,6528]{0,1:T(8,128)S(1)}, u32[]{:S(2)}) copy-start(f32[16,6528]{0,1:T(8,128)S(1)} %convert_element_type.345) | copy-start | bytes 1253380
  877.4 8.3 copy-start.18
  877.4 9.2 %copy-start.31 = (f32[16,512]{0,1:T(8,128)S(1)}, f32[16,512]{0,1:T(8,128)}, u32[]{:S(2)}) copy-start(f32[16,512]{0,1:T(8,128)} %get-tuple-element.287) | copy-start | bytes 98308
  877.4 9.9 %copy-start.12 = (f32[16,2048]{0,1:T(8,128)S(1)}, f32[16,2048]{0,1:T(8,128)}, u32[]{:S(2)}) copy-start(f32[16,2048]{0,1:T(8,128)} %get-tuple-element.284) | copy-start | bytes 393220
  888.3 7.9 copy-start.58
  888.3 7.9 copy-start.68
  888.3 7.9 copy-start.69
  888.3 8.5 copy-start.37
  888.3 8.5 copy-start.39
  888.3 8.5 copy-start.52
  888.4 8.5 copy-start.53
  888.4 9.2 %copy-start.1 = (bf16[1,768,2304]{2,1,0:T(8,128)(2,1)S(1)}, bf16[1,768,2304]{2,1,0:T(8,128)(2,1)}, u32[]{:S(2)}) copy-start(bf16[1,768,2304]{2,1,0:T(8,128)(2,1)} %param.59) | copy-start | bytes 10616836
  (71 other events, 287.8 us)
Sparse Core Ops, SparseCore 0:
  10.3 152.7 all-gather.19
  165.4 48.8 all-gather.15
  216.6 107.1 all-gather.13
  325.4 61.5 all-gather.23
  389.1 63.6 all-gather.21
  455.5 43.2 all-gather.17
  638.6 52.4 all-gather.25
  770.1 67.1 all-reduce.3

commit v2 on v1

--- a/solution.py
+++ b/solution.py
@@ -4,12 +4,16 @@
 import jax
 import jax.numpy as jnp
 from jax import lax
+from jax.experimental import pallas as pl
+from jax.experimental.pallas import tpu as pltpu
 from jax.sharding import Mesh
 from jax.sharding import PartitionSpec as P
 
 HD = 64
 FSDP = ("y", "x", "c")
 GRP_FSDP = ("grp", "y", "x", "c")
+T_ROOM = 48
+S_ROOM = 24
 
 norm_eps = 1e-12
 clip_limit = 0.001
@@ -18,31 +22,437 @@
 average_decay = 0.9
 
 
-def from_everyone(value, axis):
-    copies = jnp.broadcast_to(value, (lax.axis_size(axis), *value.shape))
-    return lax.all_to_all(copies, axis, split_axis=0, concat_axis=0, tiled=True)
-
-
-def sum_of_groups(value):
-    groups = lax.axis_size("grp")
-    me = lax.axis_index("grp")
-    parts = [value]
-    for step in range(1, groups):
-        parts.append(lax.ppermute(value, "grp", [(g, (g + step) % groups) for g in range(groups)]))
-    return jnp.stack(parts)[(me - jnp.arange(groups)) % groups].sum(0)
-
-
-def sum_and_scatter(parts):
-    shape = parts.shape[1:]
-    parts = parts.reshape(4, 4, 2, *shape)
-    parts = jnp.moveaxis(parts, (2, 1), (0, 1)).reshape(2, 16, *shape)
-    for axis in ("c", "x", "y"):
-        parts = lax.all_to_all(parts, axis, split_axis=0, concat_axis=0, tiled=True)
-        parts = parts.astype(jnp.float32).sum(0)
-        if axis != "y":
-            parts = parts.astype(jnp.bfloat16)
-            parts = parts.reshape(4, -1, *shape) if axis == "c" else parts
-    return parts
+SIZES = {"y": 4, "x": 4, "c": 2}
+MESH = pl.DeviceIdType.MESH
+ANY = pl.BlockSpec(memory_space=pl.ANY)
+VMEM = pl.BlockSpec(memory_space=pltpu.VMEM)
+AROUND = [((11 * k) % 32 // 8, (11 * k) % 8 // 2, (11 * k) % 2) for k in range(1, 32)]
+
+
+def here():
+    return {axis: lax.axis_index(axis) for axis in SIZES}
+
+
+def moved(me, dy, dx, dc):
+    return {
+        "y": lax.rem(me["y"] + dy, 4),
+        "x": lax.rem(me["x"] + dx, 4),
+        "c": lax.rem(me["c"] + dc, 2),
+    }
+
+
+def number(place):
+    return (place["y"] * 4 + place["x"]) * 2 + place["c"]
+
+
+def greet(places):
+    barrier = pltpu.get_barrier_semaphore()
+    for place in places:
+        pl.semaphore_signal(barrier, inc=1, device_id=place, device_id_type=MESH)
+    pl.semaphore_wait(barrier, len(places))
+
+
+def remote(source, target, sends, arrivals, at, place):
+    copy = pltpu.make_async_remote_copy(
+        src_ref=source,
+        dst_ref=target,
+        send_sem=sends.at[at],
+        recv_sem=arrivals.at[at],
+        device_id=place,
+        device_id_type=MESH,
+    )
+    copy.start()
+    return copy
+
+
+def exchange_kernel(source, target, sends, arrivals, local):
+    me = here()
+    greet([moved(me, *step) for step in AROUND])
+    copies = []
+    for k, step in enumerate(AROUND):
+        place = moved(me, *step)
+        copies.append(
+            remote(source.at[number(place)], target.at[number(me)], sends, arrivals, k, place)
+        )
+    own = pltpu.make_async_copy(source.at[number(me)], target.at[number(me)], local)
+    own.start()
+    own.wait()
+    for copy in copies:
+        copy.wait()
+
+
+def exchange(value, collective):
+    return pl.pallas_call(
+        exchange_kernel,
+        out_shape=jax.ShapeDtypeStruct(value.shape, value.dtype),
+        in_specs=[ANY],
+        out_specs=ANY,
+        scratch_shapes=[
+            pltpu.SemaphoreType.DMA((len(AROUND),)),
+            pltpu.SemaphoreType.DMA((len(AROUND),)),
+            pltpu.SemaphoreType.DMA,
+        ],
+        compiler_params=pltpu.CompilerParams(collective_id=collective, has_side_effects=True),
+    )(value)
+
+
+def group_exchange_kernel(source, target, sends, arrivals, local):
+    group = lax.axis_index("grp")
+    groups = [lax.rem(group + d, 4) for d in (1, 2, 3)]
+    greet([{"grp": g} for g in groups])
+    copies = [
+        remote(source.at[g], target.at[group], sends, arrivals, d, {"grp": g})
+        for d, g in enumerate(groups)
+    ]
+    own = pltpu.make_async_copy(source.at[group], target.at[group], local)
+    own.start()
+    own.wait()
+    for copy in copies:
+        copy.wait()
+
+
+def exchange_groups(value, collective):
+    return pl.pallas_call(
+        group_exchange_kernel,
+        out_shape=jax.ShapeDtypeStruct(value.shape, value.dtype),
+        in_specs=[ANY],
+        out_specs=ANY,
+        scratch_shapes=[
+            pltpu.SemaphoreType.DMA((3,)),
+            pltpu.SemaphoreType.DMA((3,)),
+            pltpu.SemaphoreType.DMA,
+        ],
+        compiler_params=pltpu.CompilerParams(collective_id=collective, has_side_effects=True),
+    )(value)
+
+
+def gather_kernel(source, target, sends, arrivals, local):
+    me = here()
+    chip, core = me["y"] * 4 + me["x"], me["c"]
+    chips = [moved(me, (7 * k) % 16 // 4, (7 * k) % 4, 0) for k in range(1, 16)]
+    sibling = moved(me, 0, 0, 1)
+    greet(chips + [sibling])
+    copies = [
+        remote(source, target.at[chip, core], sends, arrivals, k, place)
+        for k, place in enumerate(chips)
+    ]
+    own = pltpu.make_async_copy(source, target.at[chip, core], local)
+    own.start()
+    own.wait()
+    for copy in copies:
+        copy.wait()
+    remote(target.at[:, core], target.at[:, core], sends, arrivals, 15, sibling).wait()
+
+
+def gather_plane(value, collective):
+    rows, width = value.shape
+    out = pl.pallas_call(
+        gather_kernel,
+        out_shape=jax.ShapeDtypeStruct((16, 2, rows, width), value.dtype),
+        in_specs=[ANY],
+        out_specs=ANY,
+        scratch_shapes=[
+            pltpu.SemaphoreType.DMA((16,)),
+            pltpu.SemaphoreType.DMA((16,)),
+            pltpu.SemaphoreType.DMA,
+        ],
+        compiler_params=pltpu.CompilerParams(collective_id=collective, has_side_effects=True),
+    )(value)
+    return out.reshape(32 * rows, width)
+
+
+def update_kernel(factor_ref, table_grad, rest_grad, norms_grad, *refs):
+    masters, momenta, averages = refs[:7], refs[7:14], refs[14:21]
+    outs = refs[21:]
+    factor = factor_ref[0, 0]
+
+    def step(k, grad):
+        clipped = grad * factor
+        moment = momentum_decay * momenta[k][...] + clipped
+        weight = masters[k][...] - learn_rate * (clipped + momentum_decay * moment)
+        outs[k][...] = weight
+        outs[7 + k][...] = moment
+        outs[14 + k][...] = average_decay * averages[k][...] + (1.0 - average_decay) * weight
+
+    step(0, table_grad[...].astype(jnp.float32))
+
+    @pl.when(pl.program_id(0) == 0)
+    def _():
+        width = rest_grad.shape[1]
+        at = 0
+        for k in (2, 3, 4, 5):
+            rows, columns = masters[k].shape
+            blocks = []
+            for _ in range(columns // width):
+                blocks.append(rest_grad[at : at + rows].astype(jnp.float32))
+                at += rows
+            step(k, blocks[0] if len(blocks) == 1 else jnp.concatenate(blocks, axis=1))
+        step(1, rest_grad[at : at + 16].astype(jnp.float32)[: masters[1].shape[0]])
+        step(6, norms_grad[...])
+
+
+def update(factor, table_grad, rest_grad, norms_grad, masters, momenta, averages):
+    steps = 5
+    rows, width = table_grad.shape
+
+    def whole(shape):
+        return pl.BlockSpec(shape, lambda i: (0, 0))
+
+    tall = pl.BlockSpec((rows // steps, width), lambda i: (i, 0))
+    states = [tall] + [whole(m.shape) for m in masters[1:]]
+    outs = pl.pallas_call(
+        update_kernel,
+        grid=(steps,),
+        out_shape=[jax.ShapeDtypeStruct(m.shape, m.dtype) for m in masters] * 3,
+        in_specs=[
+            pl.BlockSpec(memory_space=pltpu.SMEM),
+            tall,
+            whole(rest_grad.shape),
+            whole(norms_grad.shape),
+        ]
+        + states * 3,
+        out_specs=states * 3,
+        compiler_params=pltpu.CompilerParams(vmem_limit_bytes=40 * 2**20),
+    )(factor.reshape(1, 1), table_grad, rest_grad, norms_grad, *masters, *momenta, *averages)
+    return tuple(outs)
+
+
+def scatter_sum_kernel(plan, *refs):
+    f32, bf16 = jnp.float32, jnp.bfloat16
+    parts, refs = refs[: len(plan)], refs[len(plan) :]
+    out, own, other, both, in_a, in_b, mid_a, mid_b, end_a, end_b, sends, arrivals, local = refs
+    me = here()
+    steps_x = [moved(me, 0, d, 0) for d in (1, 2, 3)]
+    steps_y = [moved(me, d, 0, 0) for d in (1, 2, 3)]
+    sibling = moved(me, 0, 0, 1)
+    greet([sibling] + steps_x + steps_y)
+    copies, at, k = [], 0, 13
+    width = own.shape[-1]
+    for part, (rows, columns) in zip(parts, plan):
+        for column in range(0, columns, width):
+            span = (slice(None), pl.ds(at, rows))
+            cols = pl.ds(column, width)
+            copies.append(
+                remote(
+                    part.at[:, sibling["c"], :, cols],
+                    other.at[span],
+                    sends,
+                    arrivals,
+                    k,
+                    sibling,
+                )
+            )
+            mine = pltpu.make_async_copy(
+                part.at[:, me["c"], :, cols], own.at[span], local.at[k - 13]
+            )
+            mine.start()
+            copies.append(mine)
+            at += rows
+            k += 1
+    for copy in copies:
+        copy.wait()
+
+    @pl.loop(0, 16)
+    def _(k):
+        both[k // 4, lax.rem(k, 4)] = (own[k].astype(f32) + other[k].astype(f32)).astype(bf16)
+
+    cut = in_a.shape[-1]
+    left, right = pl.ds(0, cut), pl.ds(cut, width - cut)
+    copies = []
+    for d in range(3):
+        to_x, to_y = steps_x[d], steps_y[d]
+        copies.append(
+            remote(both.at[:, to_x["x"], :, left], in_a.at[d], sends, arrivals, 1 + d, to_x)
+        )
+        copies.append(
+            remote(both.at[to_y["y"], :, :, right], in_b.at[d], sends, arrivals, 4 + d, to_y)
+        )
+    for copy in copies:
+        copy.wait()
+
+    @pl.loop(0, 4)
+    def _(k):
+        total_a = both[k, me["x"], :, left].astype(f32)
+        total_b = both[me["y"], k, :, right].astype(f32)
+        for d in range(3):
+            total_a += in_a[d, k].astype(f32)
+            total_b += in_b[d, k].astype(f32)
+        mid_a[k] = total_a.astype(bf16)
+        mid_b[k] = total_b.astype(bf16)
+
+    copies = []
+    for d in range(3):
+        to_x, to_y = steps_x[d], steps_y[d]
+        copies.append(remote(mid_a.at[to_y["y"]], end_a.at[d], sends, arrivals, 7 + d, to_y))
+        copies.append(remote(mid_b.at[to_x["x"]], end_b.at[d], sends, arrivals, 10 + d, to_x))
+    for copy in copies:
+        copy.wait()
+    total_a = mid_a[me["y"]].astype(f32)
+    total_b = mid_b[me["x"]].astype(f32)
+    for d in range(3):
+        total_a += end_a[d].astype(f32)
+        total_b += end_b[d].astype(f32)
+    out[:, left] = total_a.astype(out.dtype)
+    out[:, right] = total_b.astype(out.dtype)
+
+
+def sum_and_scatter(parts, width, dtype, collective):
+    plan = [part.shape[1:] for part in parts]
+    rows = sum(r * (c // width) for r, c in plan)
+    pieces = sum(c // width for _, c in plan)
+    cut = width // 2
+    rest = width - cut
+    bf16 = jnp.bfloat16
+    return pl.pallas_call(
+        partial(scatter_sum_kernel, plan),
+        out_shape=jax.ShapeDtypeStruct((rows, width), dtype),
+        in_specs=[ANY] * len(parts),
+        out_specs=VMEM,
+        scratch_shapes=[
+            pltpu.VMEM((16, rows, width), bf16),
+            pltpu.VMEM((16, rows, width), bf16),
+            pltpu.VMEM((4, 4, rows, width), bf16),
+            pltpu.VMEM((3, 4, rows, cut), bf16),
+            pltpu.VMEM((3, 4, rows, rest), bf16),
+            pltpu.VMEM((4, rows, cut), bf16),
+            pltpu.VMEM((4, rows, rest), bf16),
+            pltpu.VMEM((3, rows, cut), bf16),
+            pltpu.VMEM((3, rows, rest), bf16),
+            pltpu.SemaphoreType.DMA((13 + pieces,)),
+            pltpu.SemaphoreType.DMA((13 + pieces,)),
+            pltpu.SemaphoreType.DMA((pieces,)),
+        ],
+        compiler_params=pltpu.CompilerParams(
+            collective_id=collective, has_side_effects=True, vmem_limit_bytes=40 * 2**20
+        ),
+    )(*[part.reshape(16, 2, *part.shape[1:]) for part in parts])
+
+
+def group_sum_kernel(
+    table, rest, facts, table_out, rest_out, seen, table_in, rest_in, told, sends, arrivals, local
+):
+    f32, bf16 = jnp.float32, jnp.bfloat16
+    me = here()
+    group = lax.axis_index("grp")
+    groups = [{"grp": lax.rem(group + d, 4)} for d in (1, 2, 3)]
+    plane = [moved(me, *step) for step in AROUND]
+    greet(groups + plane)
+
+    def quarter(g):
+        return pl.ds(pl.multiple_of(g * 128, 128), 128)
+
+    mine = quarter(group)
+    copies = []
+    for d in range(3):
+        theirs = quarter(groups[d]["grp"])
+        copies.append(remote(table.at[:, theirs], table_in.at[d], sends, arrivals, d, groups[d]))
+        copies.append(remote(rest.at[:, theirs], rest_in.at[d], sends, arrivals, 3 + d, groups[d]))
+    for copy in copies:
+        copy.wait()
+
+    def summed(source, arrived, target):
+        rows = 16
+
+        def body(k, squares):
+            at = pl.ds(pl.multiple_of(k * rows, rows), rows)
+            total = source[at, mine].astype(f32)
+            for d in range(3):
+                total += arrived[d, at].astype(f32)
+            total = total.astype(bf16)
+            target[at, mine] = total
+            total = total.astype(f32)
+            total = total * total
+            return squares + total[:8] + total[8:]
+
+        return lax.fori_loop(0, source.shape[0] // rows, body, jnp.zeros((8, 128), f32))
+
+    squares = summed(table, table_in, table_out) + summed(rest, rest_in, rest_out)
+    told[group, 0:8] = squares
+    told[group, 8:16] = facts[...]
+    copies = []
+    for d in range(3):
+        copies.append(
+            remote(told.at[group], told.at[group], sends, arrivals, 6 + d, groups[d])
+        )
+    wide = []
+    for d in range(3):
+        wide.append(
+            remote(table_out.at[:, mine], table_out.at[:, mine], sends, arrivals, 9 + d, groups[d])
+        )
+        wide.append(
+            remote(rest_out.at[:, mine], rest_out.at[:, mine], sends, arrivals, 12 + d, groups[d])
+        )
+    for copy in copies:
+        copy.wait()
+    seen[number(me)] = told[0] + told[1] + told[2] + told[3]
+    copies = []
+    for k, place in enumerate(plane):
+        copies.append(
+            remote(seen.at[number(me)], seen.at[number(me)], sends, arrivals, 15 + k, place)
+        )
+    for copy in copies + wide:
+        copy.wait()
+
+
+def sum_of_groups(table, rest, facts, collective):
+    count = 15 + len(AROUND)
+    return pl.pallas_call(
+        group_sum_kernel,
+        out_shape=[
+            jax.ShapeDtypeStruct(table.shape, table.dtype),
+            jax.ShapeDtypeStruct(rest.shape, rest.dtype),
+            jax.ShapeDtypeStruct((32, 16, 128), jnp.float32),
+        ],
+        in_specs=[VMEM, VMEM, VMEM],
+        out_specs=[VMEM, VMEM, VMEM],
+        scratch_shapes=[
+            pltpu.VMEM((3, table.shape[0], 128), table.dtype),
+            pltpu.VMEM((3, rest.shape[0], 128), rest.dtype),
+            pltpu.VMEM((4, 16, 128), jnp.float32),
+            pltpu.SemaphoreType.DMA((count,)),
+            pltpu.SemaphoreType.DMA((count,)),
+            pltpu.SemaphoreType.DMA,
+        ],
+        compiler_params=pltpu.CompilerParams(
+            collective_id=collective, has_side_effects=True, vmem_limit_bytes=40 * 2**20
+        ),
+    )(table, rest, facts)
+
+
+def slots(tokens, own_rows):
+    count = tokens.shape[0]
+    row, column = tokens[:, None], tokens[None, :]
+    place = jnp.arange(count)
+    repeated = jnp.any((row == column) & (place[:, None] < place[None, :]), axis=0)
+    owner = tokens // own_rows
+    counts = ~repeated[:, None] & (row >= (owner * own_rows)[None, :]) & (row < column)
+    return owner, ~repeated, jnp.sum(counts.astype(jnp.int32), axis=0)
+
+
+def slot_in_round(owner, rank, room, turn):
+    at = rank - turn * room
+    return jnp.where((at >= 0) & (at < room), owner * room + at, -1)
+
+
+def wanted_rows(slot, first, local, places):
+    hit = (jnp.where(first, slot, -1)[:, None] == jnp.arange(places)[None, :])
+    return jnp.sum(jnp.where(hit, local[:, None] + 1, 0), axis=0) - 1
+
+
+def one_hot(index, count):
+    return (index[:, None] == jnp.arange(count)[None, :]).astype(jnp.bfloat16)
+
+
+def product(left, right):
+    return jnp.dot(left, right, preferred_element_type=jnp.float32)
+
+
+def folded(rows):
+    return jnp.concatenate(jnp.split(rows, 2, axis=2), axis=1)
+
+
+def unfolded(rows):
+    return jnp.concatenate(jnp.split(rows, 2, axis=1), axis=2)
 
 
 def layer_norm(value, gain, shift):
@@ -228,54 +638,139 @@
     picked = picks.shape[1]
     span = ids.shape[1]
 
-    facts = jnp.concatenate([ids, picks, labels, lengths[:, None]], axis=1)
-
-    def taken_apart(gathered):
-        i, p, l, n = jnp.split(gathered, [span, span + picked, span + 2 * picked], axis=1)
-        return i, p, l, n[:, 0]
-
-    group_ids, group_picks, _, group_lengths = taken_apart(
-        lax.all_gather(facts, "grp", axis=0, tiled=True)
-    )
-    teacher_rows = lax.all_gather(t_table[0], FSDP, axis=0, tiled=True)
-    plane_ids, plane_picks, plane_labels, plane_lengths = taken_apart(
-        lax.all_gather(facts, FSDP, axis=0, tiled=True)
-    )
-
-    lead = s_qkv.shape[0]
-    cols = [s_qkv, s_out, s_up, s_down.reshape(lead, -1), s_pos.reshape(lead, -1), s_norms]
-    widths = [c.shape[1] for c in cols]
-    packed_width = -(-sum(widths) // 128) * 128
-    starts = [sum(widths[:k]) for k in range(len(widths))]
+    facts = jnp.concatenate([ids, picks, jnp.broadcast_to(lengths[:, None], (1, 64))], axis=1)
+    facts = jnp.pad(facts.reshape(3, 128), ((0, 5), (0, 0)))
+    facts = exchange_groups(jnp.broadcast_to(facts, (4, 8, 128)), 9)[:, :3].reshape(4, -1)
+    group_ids, group_picks = facts[:, :span], facts[:, span : span + picked]
+    group_lengths = facts[:, span + picked]
+    own_table = s_table.astype(bf16)
+    t_owner, t_first, t_rank = slots(group_ids.reshape(-1), vocab_own)
+    s_owners, s_firsts, s_ranks = jax.vmap(lambda one: slots(one, vocab_own))(group_ids)
+    my_group = lax.axis_index("grp")
+    s_owner, s_first, s_rank = (
+        lax.dynamic_index_in_dim(v, my_group, 0, keepdims=False)
+        for v in (s_owners, s_firsts, s_ranks)
+    )
+    most = jnp.maximum(jnp.max(t_rank) // T_ROOM, jnp.max(s_ranks) // S_ROOM) + 1
+    t_local = group_ids.reshape(-1) - t_owner * vocab_own
+    s_local = ids[0] - s_owner * vocab_own
+
+    def asked(turn):
+        t_slot = slot_in_round(t_owner, t_rank, T_ROOM, turn)
+        s_slot = slot_in_round(s_owner, s_rank, S_ROOM, turn)
+        t_ask = wanted_rows(t_slot, t_first, t_local, fsdp * T_ROOM).reshape(fsdp, T_ROOM)
+        s_ask = wanted_rows(s_slot, s_first, s_local, fsdp * S_ROOM).reshape(fsdp, S_ROOM)
+        return t_slot, s_slot, t_ask, s_ask
+
+    def answer(t_want, s_want):
+        t_sent = product(one_hot(t_want.reshape(-1), vocab_own), t_table[0]).astype(bf16)
+        s_sent = product(one_hot(s_want.reshape(-1), vocab_own), own_table).astype(bf16)
+        return jnp.concatenate(
+            [t_sent.reshape(fsdp, T_ROOM, t_width), folded(s_sent.reshape(fsdp, S_ROOM, width))],
+            axis=2,
+        )
+
+    def placed(got, t_slot, s_slot):
+        t_got = got[:, :, :t_width].reshape(-1, t_width)
+        s_got = unfolded(got[:, :, t_width:]).reshape(-1, width)
+        return (
+            product(one_hot(t_slot, fsdp * T_ROOM), t_got),
+            product(one_hot(s_slot, fsdp * S_ROOM), s_got),
+        )
+
+    def swap(value):
+        return lax.all_to_all(value, FSDP, split_axis=0, concat_axis=0, tiled=True)
+
+    def ask_again(turn):
+        t_slot, s_slot, t_ask, s_ask = asked(turn)
+        wants = swap(jnp.concatenate([t_ask, s_ask], axis=1))
+        return t_slot, s_slot, wants[:, :T_ROOM], wants[:, T_ROOM:]
+
+    def more_rows(state):
+        turn, t_emb, s_emb = state
+        t_slot, s_slot, t_want, s_want = ask_again(turn)
+        t_more, s_more = placed(swap(answer(t_want, s_want)), t_slot, s_slot)
+        return turn + 1, t_emb + t_more, s_emb + s_more
+
+    t_slot, s_slot, t_ask, s_ask = asked(0)
+    line = jnp.concatenate(
+        [t_ask, s_ask, jnp.broadcast_to(most, (fsdp, 128 - T_ROOM - S_ROOM))], axis=1
+    )
+    lines = [
+        line,
+        jnp.broadcast_to(jnp.concatenate([picks, labels], axis=1), (fsdp, 2 * picked)),
+        jnp.broadcast_to(lengths[:, None], (fsdp, 128)),
+    ]
+    notes = jnp.stack(lines + [jnp.zeros((fsdp, 128), jnp.int32)] * 5, axis=1)
+    notes = exchange(notes, 1)
+    t_want, s_want = notes[:, 0, :T_ROOM], notes[:, 0, T_ROOM : T_ROOM + S_ROOM]
+    rounds = jnp.max(notes[:, 0, T_ROOM + S_ROOM])
+    plane_picks, plane_labels = notes[:, 1, :picked], notes[:, 1, picked : 2 * picked]
+    plane_lengths = notes[:, 2, 0]
+    t_emb, s_emb = placed(exchange(answer(t_want, s_want), 2), t_slot, s_slot)
+    _, t_emb, s_emb = lax.while_loop(
+        lambda state: state[0] < rounds, more_rows, (jnp.int32(1), t_emb, s_emb)
+    )
+
+    def pieces(blocks, qkv, out, up, down, pos, norms):
+        tail = norms.astype(f32).reshape(blocks, 1, -1)
+        tail = jnp.pad(tail, ((0, 0), (0, 7), (0, width - tail.shape[2])))
+        small = jnp.concatenate([pos.reshape(blocks, -1, width).astype(f32), tail], axis=1)
+        big = [part.astype(bf16).reshape(blocks, -1, part.shape[1]) for part in (qkv, out, up, down)]
+        return big + [lax.optimization_barrier(small.astype(bf16))]
 
     def pack(parts):
-        pad = jnp.zeros((parts[0].shape[0], packed_width - sum(widths)), bf16)
-        return jnp.concatenate([part.astype(bf16) for part in parts] + [pad], axis=1)
-
-    own_packed, own_table, own_head, _ = lax.optimization_barrier(
-        (pack(cols), s_table.astype(bf16), t_table[0], teacher_rows)
-    )
-    packed = lax.all_gather(own_packed, FSDP, axis=0, tiled=True)
-    whole = [packed[:, at : at + w] for at, w in zip(starts, widths)]
-    w_qkv, w_out, w_up, w_down, positions, norms = whole
-    w_down = w_down.reshape(-1, width)
-    positions = positions.reshape(-1, width)
+        columns = [
+            part[:, :, at : at + width] for part in parts for at in range(0, part.shape[2], width)
+        ]
+        return jnp.concatenate(columns, axis=1)
+
+    def unpack(packed):
+        blocks, lead = packed.shape[0], s_qkv.shape[0]
+
+        def across(at, count):
+            return jnp.concatenate(
+                [
+                    packed[:, at + k * lead : at + (k + 1) * lead].reshape(-1, width)
+                    for k in range(count)
+                ],
+                axis=1,
+            )
+
+        at_out = s_qkv.shape[1] // width * lead
+        at_up = at_out + lead
+        at_down = at_up + s_up.shape[1] // width * lead
+        at_pos = at_down + s_down.shape[0]
+        at_norms = at_pos + s_pos.shape[0]
+        return (
+            across(0, s_qkv.shape[1] // width),
+            across(at_out, 1),
+            across(at_up, s_up.shape[1] // width),
+            packed[:, at_down:at_pos].reshape(-1, width),
+            packed[:, at_pos:at_norms].reshape(-1, width),
+            packed[:, at_norms, : s_norms.size].reshape(-1, s_norms.shape[1]),
+        )
+
+    own_packed = pack(pieces(1, s_qkv, s_out, s_up, s_down, s_pos, s_norms))
+    w_qkv, w_out, w_up, w_down, positions, norms = unpack(
+        lax.all_gather(own_packed, FSDP, axis=0, tiled=True)
+    )
     student = (w_qkv, w_out, w_up, w_down, norms)
-    table = lax.all_gather(own_table, FSDP, axis=0, tiled=True)
-    heads = lax.all_gather(own_head, "grp", axis=0, tiled=False)
+    heads = lax.all_gather(t_table[0], "grp", axis=0, tiled=False)
 
     teacher = (t_qkv[0], t_out[0], t_up[0], t_down[0], t_norms[0])
-    t_embedded = jnp.take(teacher_rows, group_ids, axis=0).astype(f32) + t_pos[0].astype(f32)[None]
+    t_embedded = t_emb.reshape(-1, span, t_width) + t_pos[0].astype(f32)[None]
     teacher_final, _ = forward(t_embedded, group_lengths, teacher)
     taken = jnp.take_along_axis(teacher_final, group_picks[:, :, None], axis=1).astype(bf16)
-    rows = lax.all_to_all(taken, "grp", split_axis=0, concat_axis=0, tiled=True)
+    taken, heads = lax.optimization_barrier((taken, heads))
+    rows = exchange_groups(taken, 10)
+    s_emb, rows = lax.optimization_barrier((s_emb, rows))
     rows = lax.all_gather(rows, FSDP, axis=0, tiled=False)
 
-    table, _ = lax.optimization_barrier((table, taken))
-    embedded = jnp.take(table, ids, axis=0).astype(f32) + positions.astype(f32)[None]
+    embedded = s_emb[None] + positions.astype(f32)[None]
     final, saved = forward(embedded, lengths, student)
     own_rows = jnp.take_along_axis(final, picks[:, :, None], axis=1).astype(bf16)[0]
-    h = lax.all_gather(own_rows, FSDP, axis=0, tiled=True)
+    h = gather_plane(own_rows, 11)
     z = jnp.einsum("rd,vd->rv", h, own_table, preferred_element_type=f32)
 
     logits = jnp.einsum("fkpd,kvd->kfpv", rows, heads, preferred_element_type=f32)
@@ -295,7 +790,8 @@
     z_stats = [z_top, jnp.sum(jnp.exp(z - z_top[:, None]), -1)]
     sent = jnp.concatenate(stats + [s[None] for s in z_stats], axis=0)
     sent = jnp.moveaxis(sent.reshape(-1, fsdp, picked), 1, 0)
-    seen = lax.all_to_all(sent, FSDP, split_axis=0, concat_axis=0, tiled=True)
+    sent = jnp.pad(sent, ((0, 0), (0, 24 - sent.shape[1]), (0, 128 - picked)))
+    seen = exchange(sent, 3)[:, :, :picked]
     tops, sums, dots, hits = [seen[:, 4 * j : 4 * j + 4] for j in range(4)]
 
     def log_sum(tops, sums):
@@ -316,7 +812,9 @@
     blend = jax.nn.softmax(-label_loss)
     entropy = jnp.sum((blend[:, None] * t_ent).astype(bf16).astype(f32), 0)
     shift = jnp.concatenate([log_blend[:, None] - t_lse, s_lse[None]], axis=0)
-    shift = jnp.moveaxis(from_everyone(shift, FSDP), 0, 1).reshape(5, -1)
+    shift = jnp.pad(shift, ((0, 3), (0, 128 - picked)))
+    shift = exchange(jnp.broadcast_to(shift, (fsdp, 8, 128)), 4)[:, :5, :picked]
+    shift = jnp.moveaxis(shift, 0, 1).reshape(5, -1)
 
     plane_counted = (plane_picks < plane_lengths[:, None]).astype(f32).reshape(-1)
     target = jnp.sum(jnp.exp(logits + shift[:4, :, None]).astype(bf16).astype(f32), 0)
@@ -325,54 +823,47 @@
     )
     grad_logits = (plane_counted[:, None] * (jnp.exp(z - shift[4][:, None]) - target)).astype(bf16)
     grad_rows = jnp.einsum("rv,vd->rd", grad_logits, own_table, preferred_element_type=f32)
-    grad_rows = sum_and_scatter(grad_rows.astype(bf16).reshape(fsdp, picked, width))
+    grad_rows = sum_and_scatter([grad_rows.astype(bf16).reshape(fsdp, picked, width)], width, f32, 5)
     head_grad = jnp.einsum("rv,rd->vd", grad_logits, h, preferred_element_type=f32)
 
-    loss_count = sum_of_groups(jnp.stack([loss_local, count_local]))
     grad_final = jnp.zeros(final.shape, f32).at[0, picks[0]].add(grad_rows)
     terms = backward(lengths, student, saved, grad_final)
     grad_embedded = terms[0]
-    everyones = lax.all_gather(grad_embedded[0].astype(bf16), FSDP, axis=0, tiled=True)
-    own_id = lax.broadcasted_iota(jnp.int32, (vocab_own, 1), 0) + base
-    at_id = (own_id == plane_ids.reshape(1, -1)).astype(bf16)
-    g_lookup = jnp.dot(at_id, everyones, preferred_element_type=f32)
-    table_part = (head_grad + g_lookup).astype(bf16)
+    low_embedded = grad_embedded[0].astype(bf16)
+
+    def given(s_slot):
+        rows = product(one_hot(s_slot, fsdp * S_ROOM).T, low_embedded).astype(bf16)
+        return folded(rows.reshape(fsdp, S_ROOM, width))
+
+    def taken_in(got, s_want):
+        rows = unfolded(got).reshape(-1, width)
+        return product(one_hot(s_want.reshape(-1), vocab_own).T, rows)
+
+    def more_grads(state):
+        turn, total = state
+        _, s_slot, _, s_want = ask_again(turn)
+        return turn + 1, total + taken_in(swap(given(s_slot)), s_want)
+
+    g_lookup = taken_in(exchange(given(s_slot), 6), s_want)
+    _, g_table = lax.while_loop(
+        lambda state: state[0] < rounds, more_grads, (jnp.int32(1), head_grad + g_lookup)
+    )
     g_pos, g_qkv, g_out, g_up, g_down, g_norms = terms[1:]
-    whole_lead = g_qkv.shape[0]
-    parts = pack(
-        [g_qkv, g_out, g_up, g_down.reshape(whole_lead, -1), g_pos.reshape(whole_lead, -1), g_norms]
-    )
-    rest = sum_and_scatter(parts.reshape(fsdp, lead, packed_width)).astype(bf16)
-    table_sum, rest_sum = lax.psum((table_part, rest), "grp")
-    table_sum, rest_sum = table_sum.astype(f32), rest_sum.astype(f32)
-    squares = jnp.sum(table_sum * table_sum) + jnp.sum(rest_sum * rest_sum)
-    scalars = jnp.concatenate([squares[None], loss_count])
-    scalars = from_everyone(scalars, FSDP).sum(0)
-    squares, loss_sum, count = scalars[0], scalars[1], scalars[2]
-    r_qkv, r_out, r_up, r_down, r_pos, r_norms = [
-        rest_sum[:, at : at + w] for at, w in zip(starts, widths)
-    ]
-    shards = (
-        table_sum,
-        r_pos.reshape(s_pos.shape),
-        r_qkv,
-        r_out,
-        r_up,
-        r_down.reshape(s_down.shape),
-        r_norms,
-    )
+    parts = pieces(fsdp, g_qkv, g_out, g_up, g_down, g_pos, g_norms)
+    rest = sum_and_scatter(parts, width, bf16, 7)
+    row = jnp.arange(8)[:, None]
+    column_of = jnp.arange(128)[None, :]
+    told = jnp.where((row == 0) & (column_of == 0), loss_local, 0.0)
+    told += jnp.where((row == 1) & (column_of == 0), count_local, 0.0)
+    table_sum, rest_sum, seen = sum_of_groups(g_table.astype(bf16), rest, told, 8)
+    seen = seen.sum(0)
+    squares, loss_sum, count = jnp.sum(seen[:8]), seen[8, 0], seen[9, 0]
+    at_norms = rest_sum.shape[0] - 8
+    norms_sum = rest_sum[at_norms, : s_norms.size].astype(f32).reshape(s_norms.shape)
     clip_norm = jnp.sqrt(squares) / count
     factor = jnp.minimum(1.0, clip_limit / clip_norm) / count
-    new_weights, new_moments, new_averages = ([], [], [])
-    for weight, moment, average, grad in zip(masters, momenta, averages, shards):
-        clipped = grad * factor
-        moment_new = momentum_decay * moment + clipped
-        weight_new = weight - learn_rate * (clipped + momentum_decay * moment_new)
-        new_weights.append(weight_new)
-        new_moments.append(moment_new)
-        new_averages.append(average_decay * average + (1.0 - average_decay) * weight_new)
-    return (
-        (loss_sum, count, clip_norm) + tuple(new_weights) + tuple(new_moments) + tuple(new_averages)
+    return (loss_sum, count, clip_norm) + update(
+        factor, table_sum, rest_sum, norms_sum, masters, momenta, averages
     )
 
 

time: 915 us -> 661 us (0.72)
  waiting for transfers between devices: 339 us -> 0.75 us
  Pallas kernels: 0 us -> 241 us
  blocking collectives: 93 us -> 0 us
  starting transfers between devices: 28.6 us -> 0.12 us
  other arithmetic: 131 us -> 115 us
  local copies, waits for them, and re-layouts: 125 us -> 109 us
  matrix products: 165 us -> 154 us
    pallas_call x0 -> x12, Pallas kernels: none -> 241 us  [the longest x5 98.8 us: exchange(): pl.pallas_call(exchange_kernel, out_shape=jax.ShapeDtypeStruct(value.shap...]
    all_gather x6 -> x2, waiting for transfers between devices: 163 us -> 0.02 us  [the longest x1 0.02 us: per_device(): lax.all_gather(own_packed, FSDP, axis=0, tiled=True)]
    all_gather x1, waiting for transfers between devices: 65.8 us -> 0.01 us  [per_device(): rows = lax.all_gather(rows, FSDP, axis=0, tiled=False)]
    psum x1 -> x0, waiting for transfers between devices: 57.1 us -> none  [per_device(): table_sum, rest_sum = lax.psum((table_part, rest), 'grp')]
    all_to_all x5 -> x0, blocking collectives: 55.4 us -> none  [the longest x4 45.9 us: sum_and_scatter(): parts = lax.all_to_all(parts, axis, split_axis=0, concat_axis=0, tiled=True)]
    all_to_all x5 -> x0, waiting for transfers between devices: 49.5 us -> none  [the longest x2 36.4 us: sum_and_scatter(): parts = lax.all_to_all(parts, axis, split_axis=0, concat_axis=0, tiled=True)]
    all_gather x2 -> x0, blocking collectives: 37.5 us -> none  [the longest x1 29 us: per_device(): lax.all_gather(facts, FSDP, axis=0, tiled=True)]
    all_to_all x5 -> x0, starting transfers between devices: 24.3 us -> none  [the longest x2 11.7 us: from_everyone(): return lax.all_to_all(copies, axis, split_axis=0, concat_axis=0, tiled=True)]
  transfers between devices with their start and end apart: 16 -> 3, of which waited for: 11 -> 0; matrix products, arithmetic and copies ran while one was open for 31% -> 32% of each run, Pallas kernels for 0% -> 16%
where the time goes in v2:
time: 661 us; the launch traced here: 649 us
  Pallas kernels  241 us (36%)
  matrix products  154 us (23%)
  other arithmetic  115 us (17%)
  local copies, waits for them, and re-layouts  109 us (16%)
  between operations  27.2 us (4%)
    pallas_call x5, Pallas kernels, exchange(): pl.pallas_call(exchange_kernel, out_shape=jax.ShapeDtypeStruct(value.shap...  98.8 us
    dot_general x8, matrix products, project(): jnp.einsum('blk,kn->bln', left, right, preferred_element_type=jnp.float32)  63.6 us
    pallas_call x2, Pallas kernels, sum_and_scatter(): pl.pallas_call(partial(scatter_sum_kernel, plan), out_shape=jax.ShapeDtyp...  53 us
    unnamed x330, local copies, waits for them, and re-layouts  46 us
    pallas_call x1, Pallas kernels, sum_of_groups(): pl.pallas_call(group_sum_kernel, out_shape=[jax.ShapeDtypeStruct(table.sh...  36.1 us
    pallas_call x1, Pallas kernels, gather_plane(): pl.pallas_call(gather_kernel, out_shape=jax.ShapeDtypeStruct((16, 2, rows...  33.8 us
    dot_general x1, matrix products, per_device(): jnp.einsum('fkpd,kvd->kfpv', rows, heads, preferred_element_type=f32)  22.6 us
    reduce_sum x1, other arithmetic, per_device(): jnp.sum(spread * logits, -1)  18 us
  transfers between devices with their start and end apart: 3, of which 0 were waited for; matrix products, arithmetic and copies ran while one was open for 32% of the time, Pallas kernels for 16%

profile of v2, /device:TPU:1, one launch (start us, length us, event | category | flops | bytes accessed | tf_op | source)
XLA Modules:
  0.0 648.9 jit_solution(4050230760201869042)
XLA Ops:
  17.3 1.5 bitcast_dynamic-update-slice_fusion
  22.2 7.3 %shard_map.487 = s32[4,8,128]{2,1,0:T(8,128)} custom-call(s32[4,8,128]{2,1,0:T(8,128)} %broadcast_in_dim.351.source), custom_call_target="tpu_custom_call" | custom-call | tf_op jit(solution)/shard_map/pallas_call | solution.py:115
  46.9 1.5 select_reduce_fusion.5
  55.1 1.7 stack.39.source
  56.8 12.3 %shard_map.488 = s32[32,8,128]{2,1,0:T(8,128)} custom-call(s32[32,8,128]{2,1,0:T(8,128)} %stack.39.source), custom_call_target="tpu_custom_call" | custom-call | tf_op jit(solution)/shard_map/pallas_call | solution.py:85
  69.1 1.6 slice_reduce_fusion.10
  70.7 1.5 slice_reduce_fusion.11
  72.3 2.6 convert_element_type.265
  76.3 2.2 fusion.80
  80.8 4.6 fusion.45
  85.5 1.9 maximum_maximum_fusion.1.source
  87.4 45.4 %shard_map.489 = bf16[32,48,1024]{2,1,0:T(8,128)(2,1)} custom-call(bf16[32,48,1024]{2,1,0:T(8,128)(2,1)} %maximum_maximum_fusion.1.source), custom_call_target="tpu_custom_call" | custom-call | tf_op jit(solution)/shard_map/pallas_call | solution.py:85
  132.9 1.8 copy-done.43
  134.8 2.3 slice_reduce_fusion.12
  139.5 4.5 fusion.33
  146.5 2.7 fusion.53
  156.6 2.8 add_convert_fusion
  159.5 4.2 convolution_convert_fusion.1
  163.7 1.6 fusion.191
  165.3 2.6 copy.206
  168.0 1.6 copy.207
  169.5 1.6 copy.208
  171.1 10.6 %fusion.199 = (f32[4,12,256]{2,1,0:T(8,128)S(1)}, f32[4,12,256,256]{2,3,1,0:T(8,128)}) fusion(pred[4,256]{1,0:T(4,128)(4,1)S(1)} %iota_compare_fusion.48, bf16[4,256,12,64]{1,3,2,0:T(8,128)(2,1)S(1)} %bitcast.358, bf16[4,256,12,64]{1,3,2,0:T(8,128)(2,1)} %bitcast.359), kind=kOutput, calls=%fused_computation.450 | convolution fusion | flops 415236352 | bytes 15778816 | tf_op jit(solution)/shard_map/sub | solution.py:509
  181.7 6.4 fusion.68
  188.2 2.1 fusion.200
  192.1 12.5 %fusion.51 = (u8[256,3072]{1,0:T(8,128)(4,1)S(1)}, u8[256,3072]{1,0:T(8,128)(4,1)S(1)}, f32[4,256,3072]{2,1,0:T(8,128)S(1)}) fusion(bf16[1,768,3072]{2,1,0:T(8,128)(2,1)} %param.65, f32[4,256,768]{2,1,0:T(8,128)} %copy-done.56, f32[768]{0:T(1024)S(1)} %copy-done.161, f32[768]{0:T(1024)S(1)} %copy-done.162, f32[4,256]{1,0:T(4,128)S(1)} %add_rsqrt_fusion.1, ...), kind=kOutput, calls=%fused_computation.133 | convolution fusion | flops 4875091968 | bytes 22034432 | tf_op jit(solution)/shard_map/blk,kn->bln/dot_general | solution.py:471
  204.5 35.6 %fusion.201 = (f32[4,256]{1,0:T(4,128)S(1)}, f32[4,256,768]{2,1,0:T(8,128)S(1)}) fusion(bf16[1,3072,768]{2,1,0:T(8,128)(2,1)} %param.66, f32[4,256,3072]{2,1,0:T(8,128)S(1)} %get-tuple-element.794, u8[256,3072]{1,0:T(8,128)(4,1)S(1)} %get-tuple-element.626, u8[256,3072]{1,0:T(8,128)(4,1)S(1)} %get-tuple-element.625, f32[768]{0:T(1024)S(1)} %copy-done.161, ...), kind=kOutput, calls=%fused_computation.452 | convolution fusion | flops 5056756736 | bytes 25184256 | tf_op jit(solution)/shard_map/blk,kn->bln/dot_general | solution.py:471
  241.4 2.4 gather_fusion.1
  245.4 8.0 %shard_map.490 = bf16[4,64,768]{2,1,0:T(8,128)(2,1)} custom-call(bf16[4,64,768]{2,1,0:T(8,128)(2,1)} %select_convert_fusion.source), custom_call_target="tpu_custom_call" | custom-call | tf_op jit(solution)/shard_map/pallas_call | solution.py:115
  264.6 4.1 fusion.190
  272.2 1.9 copy.214
  274.1 3.2 slice.335
  277.3 3.1 fusion.203
  280.5 2.1 convolution_convert_fusion.11
  283.4 7.3 %multiply_convert_fusion.2 = (bf16[256,2048]{1,0:T(8,128)(2,1)S(1)}, f32[256,2048]{1,0:T(8,128)}, f32[256,2048]{1,0:T(8,128)}) fusion(bf16[512,512]{1,0:T(8,128)(2,1)S(1)} %bitcast.377, bf16[512,512]{1,0:T(8,128)(2,1)S(1)} %bitcast.379, bf16[512,512]{1,0:T(8,128)(2,1)S(1)} %bitcast.381, bf16[512,512]{1,0:T(8,128)(2,1)S(1)} %bitcast.383, ...), kind=kOutput, calls=%fused_computation.149 | convolution fusion | flops 579993600 | bytes 7870464 | tf_op jit(solution)/shard_map/blk,kn->bln/dot_general | solution.py:471
  294.0 33.8 %shard_map.491 = bf16[16,2,64,512]{3,2,1,0:T(8,128)(2,1)} custom-call(bf16[64,512]{1,0:T(8,128)(2,1)} %select_convert_fusion.1.source), custom_call_target="tpu_custom_call" | custom-call | tf_op jit(solution)/shard_map/pallas_call | solution.py:149
  327.8 7.3 %fusion.206 = (f32[2048]{0:T(1024)S(1)}, f32[2048,960]{0,1:T(8,128)}) fusion(bf16[2048,512]{1,0:T(8,128)(2,1)} %bitcast.353, bf16[960,512]{1,0:T(8,128)(2,1)} %get-tuple-element.1122), kind=kOutput, calls=%fused_computation.457 | convolution fusion | flops 2015229952 | bytes 10952704 | tf_op jit(solution)/shard_map/rd,vd->rv/dot_general | solution.py:774
  335.2 4.3 exponential_reduce_fusion
  339.6 22.6 %fusion.202 = (f32[4,32,64]{2,1,0:T(8,128)S(1)}, f32[4,32,64,960]{3,2,1,0:T(8,128)}) fusion(bf16[4,960,768]{2,1,0:T(8,128)(2,1)} %all-gather.5.cloned.1.call-done, bf16[32,4,64,768]{3,2,1,0:T(8,128)(2,1)} %bitcast.412), kind=kOutput, calls=%fused_computation.453 | convolution fusion | flops 12087451648 | bytes 49971200 | tf_op jit(solution)/shard_map/fkpd,kvd->kfpv/dot_general | solution.py:776
  362.3 18.0 %multiply_reduce_fusion = (f32[4,32,64]{2,1,0:T(8,128)S(1)}, f32[4,32,64]{2,1,0:T(8,128)S(1)}, f32[4,32,64]{2,1,0:T(8,128)S(1)}) fusion(f32[4,32,64,960]{3,2,1,0:T(8,128)} %get-tuple-element.798, f32[4,32,64]{2,1,0:T(8,128)S(1)} %get-tuple-element.797, pred[32,64,960]{2,1,0:T(8,128)(4,1)S(1)} %broadcast_compare_fusion), kind=kLoop, calls=%fused_computation.60 | loop fusion | flops 47161344 | bytes 33554432 | tf_op jit(solution)/shard_map/reduce_sum | solution.py:786
  381.4 14.1 %shard_map.492 = f32[32,24,128]{2,1,0:T(8,128)} custom-call(f32[32,24,128]{2,1,0:T(8,128)} %pad.25.source), custom_call_target="tpu_custom_call" | custom-call | tf_op jit(solution)/shard_map/pallas_call | solution.py:85
  404.1 9.8 %shard_map.493 = f32[32,8,128]{2,1,0:T(8,128)} custom-call(f32[32,8,128]{2,1,0:T(8,128)} %broadcast_in_dim.371.source), custom_call_target="tpu_custom_call" | custom-call | tf_op jit(solution)/shard_map/pallas_call | solution.py:85
  414.9 17.6 %convert_reduce_fusion = f32[32,64,960]{2,1,0:T(8,128)} fusion(f32[4,32,64,960]{3,2,1,0:T(8,128)} %get-tuple-element.798, f32[4,32,64]{2,1,0:T(8,128)S(1)} %copy.222), kind=kLoop, calls=%fused_computation.57 | loop fusion | flops 29491200 | bytes 39354368 | tf_op jit(solution)/shard_map/reduce_sum | solution.py:820
  432.5 9.0 %copy.223 = f32[2048,960]{0,1:T(8,128)} copy(f32[2048,960]{1,0:T(8,128)} %bitcast.339) | data formatting | bytes 15728640 | tf_op jit(solution)/shard_map/reduce_sum | solution.py:820
  441.6 6.8 %multiply_reduce_fusion.1 = (f32[2048]{0:T(1024)S(1)}, bf16[2048,960]{0,1:T(8,128)(2,1)S(1)}) fusion(f32[2048,960]{0,1:T(8,128)} %copy.223, f32[2048,960]{0,1:T(8,128)} %get-tuple-element.807, f32[2048]{0:T(1024)S(1)} %sub.396, f32[2048]{0:T(1024)S(1)} %compare_convert_fusion), kind=kLoop, calls=%fused_computation.91 | loop fusion | flops 11794432 | bytes 19685376 | tf_op jit(solution)/shard_map/reduce_sum | solution.py:822
  448.4 3.5 fusion.207
  451.9 2.5 convolution_convert_fusion.4
  454.4 16.0 %shard_map.494 = f32[64,512]{1,0:T(8,128)S(1)} custom-call(bf16[16,2,64,512]{3,2,1,0:T(8,128)(2,1)S(1)} %bitcast.331), custom_call_target="tpu_custom_call" | custom-call | tf_op jit(solution)/shard_map/pallas_call | solution.py:306
  472.9 4.2 add_convert_fusion.1
  479.2 2.2 convolution_convert_fusion.9
  486.5 1.4 convolution_convert_fusion.7
  488.7 1.9 convolution_convert_fusion.5
  492.0 2.1 convolution_convert_fusion.2
  498.2 17.2 %shard_map.495 = bf16[32,48,256]{2,1,0:T(8,128)(2,1)} custom-call(bf16[32,48,256]{2,1,0:T(8,128)(2,1)} %pad_maximum_fusion.7.source), custom_call_target="tpu_custom_call" | custom-call | tf_op jit(solution)/shard_map/pallas_call | solution.py:85
  517.1 2.5 fusion.69
  520.6 2.7 convert_element_type.311.table
  524.3 1.6 fusion.116
  527.9 1.6 copy-done.2
  530.9 37.0 %shard_map.496.rest = bf16[208,512]{1,0:T(8,128)(2,1)S(1)} custom-call(bf16[16,2,16,1536]{3,2,1,0:T(8,128)(2,1)S(1)} %bitcast.334, bf16[16,2,16,512]{3,2,1,0:T(8,128)(2,1)S(1)} %bitcast.332, bf16[16,2,16,2048]{3,2,1,0:T(8,128)(2,1)S(1)} %bitcast.329, bf16[16,2,64,512]{3,2,1,0:T(8,128)(2,1)S(1)} %bitcast.330, bf16[16,2,16,512]{3,2,1,0:T(8,128)(2,1)S(1)} %bitcast.333), custom_call_target="tpu_custom_call" | custom-call | tf_op jit(solution)/shard_map/pallas_call | solution.py:306
  567.9 36.1 %shard_map.497 = (bf16[960,512]{1,0:T(8,128)(2,1)S(1)}, bf16[208,512]{1,0:T(8,128)(2,1)S(1)}, f32[32,16,128]{2,1,0:T(8,128)S(1)}) custom-call(bf16[960,512]{1,0:T(8,128)(2,1)S(1)} %copy-done.4, bf16[208,512]{1,0:T(8,128)(2,1)S(1)} %shard_map.496.rest, f32[8,128]{1,0:T(8,128)S(1)} %select_add_fusion.facts), custom_call_target="tpu_custom_call" | custom-call | tf_op jit(solution)/shard_map/pallas_call | solution.py:399
  609.6 1.7 copy-done.3
  611.3 1.5 copy-done.5
  612.8 1.5 copy-done.6
  631.1 4.0 shard_map.498
  (515 shorter events, 127.5 us)
Async XLA Ops:
  7.2 152.3 %copy-start = (bf16[1,768,2304]{2,1,0:T(8,128)(2,1)S(1)}, bf16[1,768,2304]{2,1,0:T(8,128)(2,1)}, u32[]{:S(2)}) copy-start(bf16[1,768,2304]{2,1,0:T(8,128)(2,1)} %param.63) | copy-start | bytes 10616836
  7.2 238.2 %all-gather.5.cloned.1.call-start = ((), (), s32[]{:S(2)}) async-start(), calls=%async_computation.4 | async-start | bytes 7372800 | tf_op jit(solution)/shard_map/all_gather | solution.py:759
  7.9 253.3 %all-gather.7.cloned.1.call-start = ((), (), s32[]{:S(2)}) async-start(), calls=%async_computation.5 | async-start | bytes 7028736 | tf_op jit(solution)/shard_map/all_gather | solution.py:756
  19.4 320.2 %all-gather.9.cloned.1.call-start = ((), (), s32[]{:S(2)}) async-start(), calls=%async_computation.6 | async-start | bytes 12976128 | tf_op jit(solution)/shard_map/all_gather | solution.py:768
  80.8 4.6 copy-start.66
  80.8 4.6 copy-start.67
  132.8 5.7 copy-start.97
  132.8 6.7 %slice-start = ((bf16[32,48,1024]{2,1,0:T(8,128)(2,1)}), bf16[32,48,768]{2,1,0:T(8,128)(2,1)S(1)}, s32[]{:S(2)}) async-start(bf16[32,48,1024]{2,1,0:T(8,128)(2,1)} %shard_map.489), calls=%async_computation.7 | async-start | bytes 4718592 | tf_op jit(solution)/shard_map/slice | solution.py:674
  132.8 6.7 %copy-start.160 = (s32[1024]{0:T(1024)S(1)}, s32[1024]{0:T(1024)}, u32[]{:S(2)}) copy-start(s32[1024]{0:T(1024)} %get-tuple-element.723) | copy-start | bytes 12292
  139.5 4.6 copy-start.142
  146.4 4.9 copy-start.101
  146.4 4.9 copy-start.105
  146.4 4.9 copy-start.111
  146.5 4.9 copy-start.117
  181.7 6.5 copy-start.39
  181.7 6.5 copy-start.45
  181.7 6.5 copy-start.130
  181.7 6.5 %copy-start.158 = (f32[4,256]{1,0:T(4,128)S(1)}, f32[4,256]{1,0:T(4,128)}, u32[]{:S(2)}) copy-start(f32[4,256]{1,0:T(4,128)} %div.179) | copy-start | bytes 12292
  181.7 6.5 %copy-start.159 = (f32[4,256]{1,0:T(4,128)S(1)}, f32[4,256]{1,0:T(4,128)}, u32[]{:S(2)}) copy-start(f32[4,256]{1,0:T(4,128)} %rsqrt.65) | copy-start | bytes 12292
  181.7 6.5 %copy-start.173 = (bf16[1,768,768]{2,1,0:T(8,128)(2,1)S(1)}, bf16[1,768,768]{2,1,0:T(8,128)(2,1)}, u32[]{:S(2)}) copy-start(bf16[1,768,768]{2,1,0:T(8,128)(2,1)} %param.64) | copy-start | bytes 3538948
  192.1 12.5 %copy-start.57 = (f32[4,256,768]{2,1,0:T(8,128)S(1)}, f32[4,256,768]{2,1,0:T(8,128)}, u32[]{:S(2)}) copy-start(f32[4,256,768]{2,1,0:T(8,128)} %copy-done.56) | copy-start | bytes 9437188
  241.3 12.2 %copy-start.127 = (f32[16,6]{0,1:T(8,128)S(1)}, f32[16,6]{0,1:T(8,128)}, u32[]{:S(2)}) copy-start(f32[16,6]{0,1:T(8,128)} %param.46) | copy-start | bytes 1156
  241.3 14.0 %copy-start.153 = (s32[32]{0:T(128)S(1)}, s32[32]{0:T(128)}, u32[]{:S(2)}) copy-start(s32[32]{0:T(128)} %get-tuple-element.644) | copy-start | bytes 388
  241.3 14.2 %copy-start.155 = (f32[16,6]{0,1:T(8,128)S(1)}, f32[16,6]{0,1:T(8,128)}, u32[]{:S(2)}) copy-start(f32[16,6]{0,1:T(8,128)} %param.53) | copy-start | bytes 1156
  241.3 14.8 %copy-start.156 = (f32[16,6]{0,1:T(8,128)S(1)}, f32[16,6]{0,1:T(8,128)}, u32[]{:S(2)}) copy-start(f32[16,6]{0,1:T(8,128)} %param.60) | copy-start | bytes 1156
  241.3 15.5 %copy-start.164 = (s32[1,64]{1,0:T(1,128)S(1)}, s32[1,64]{1,0:T(1,128)}, u32[]{:S(2)}) copy-start(s32[1,64]{1,0:T(1,128)} %param.38) | copy-start | bytes 772
  243.8 18.6 %copy-start.42 = (f32[256,512]{1,0:T(8,128)S(1)}, f32[256,512]{1,0:T(8,128)}, u32[]{:S(2)}) copy-start(f32[256,512]{1,0:T(8,128)} %get-tuple-element.450) | copy-start | bytes 1572868
  263.4 220.2 %copy-start.46 = (f32[256,512]{1,0:T(8,128)}, f32[256,512]{1,0:T(8,128)S(1)}, u32[]{:S(2)}) copy-start(f32[256,512]{1,0:T(8,128)S(1)} %get-tuple-element.721) | copy-start | bytes 1572868
  263.5 19.1 %copy-start.125 = (f32[256]{0:T(256)}, f32[256]{0:T(256)S(1)}, u32[]{:S(2)}) copy-start(f32[256]{0:T(256)S(1)} %broadcast_multiply_fusion.7) | copy-start | bytes 3076
  263.7 5.1 copy-start.135
  264.5 18.1 %copy-start.123 = (f32[512]{0:T(512)}, f32[512]{0:T(512)S(1)}, u32[]{:S(2)}) copy-start(f32[512]{0:T(512)S(1)} %get-tuple-element.643) | copy-start | bytes 6148
  264.5 18.1 %copy-start.151 = (f32[512]{0:T(512)}, f32[512]{0:T(512)S(1)}, u32[]{:S(2)}) copy-start(f32[512]{0:T(512)S(1)} %get-tuple-element.642) | copy-start | bytes 6148
  264.6 26.2 %copy-start.121 = (f32[512]{0:T(512)}, f32[512]{0:T(512)S(1)}, u32[]{:S(2)}) copy-start(f32[512]{0:T(512)S(1)} %get-tuple-element.641) | copy-start | bytes 6148
  264.6 26.2 %copy-start.148 = (f32[512]{0:T(512)}, f32[512]{0:T(512)S(1)}, u32[]{:S(2)}) copy-start(f32[512]{0:T(512)S(1)} %get-tuple-element.640) | copy-start | bytes 6148
  264.6 18.0 %copy-start.133 = (f32[256]{0:T(256)}, f32[256]{0:T(256)S(1)}, u32[]{:S(2)}) copy-start(f32[256]{0:T(256)S(1)} %fusion.119) | copy-start | bytes 3076
  268.7 13.9 %copy-start.54 = (bf16[32,16,512]{2,1,0:T(8,128)(2,1)}, bf16[32,16,512]{2,1,0:T(8,128)(2,1)S(1)}, u32[]{:S(2)}) copy-start(bf16[32,16,512]{2,1,0:T(8,128)(2,1)S(1)} %get-tuple-element.747) | copy-start | bytes 1572868
  272.2 8.2 %copy-start.69 = (bf16[1,256,512]{1,2,0:T(8,128)(2,1)}, bf16[1,256,512]{1,2,0:T(8,128)(2,1)S(1)}, u32[]{:S(2)}) copy-start(bf16[1,256,512]{1,2,0:T(8,128)(2,1)S(1)} %copy.213) | copy-start | bytes 786436
  282.6 8.1 %copy-start.76 = (bf16[8,64,256]{2,1,0:T(8,128)(2,1)}, bf16[8,64,256]{2,1,0:T(8,128)(2,1)S(1)}, u32[]{:S(2)}) copy-start(bf16[8,64,256]{2,1,0:T(8,128)(2,1)S(1)} %convolution_convert_fusion.11) | copy-start | bytes 786436
  283.1 7.7 %copy-start.51 = (f32[256,512]{1,0:T(8,128)}, f32[256,512]{1,0:T(8,128)S(1)}, u32[]{:S(2)}) copy-start(f32[256,512]{1,0:T(8,128)S(1)} %get-tuple-element.802) | copy-start | bytes 1572868
  283.1 7.7 %copy-start.131 = (f32[256]{0:T(256)}, f32[256]{0:T(256)S(1)}, u32[]{:S(2)}) copy-start(f32[256]{0:T(256)S(1)} %broadcast_multiply_fusion.6) | copy-start | bytes 3076
  283.3 7.5 %copy-start.137 = (f32[256]{0:T(256)}, f32[256]{0:T(256)S(1)}, u32[]{:S(2)}) copy-start(f32[256]{0:T(256)S(1)} %multiply_reduce_fusion.7) | copy-start | bytes 3076
  283.3 7.5 %copy-start.144 = (f32[256]{0:T(256)}, f32[256]{0:T(256)S(1)}, u32[]{:S(2)}) copy-start(f32[256]{0:T(256)S(1)} %fusion.120) | copy-start | bytes 3076
  283.4 7.4 %copy-start.59 = (bf16[32,64,512]{2,1,0:T(8,128)(2,1)S(1)}, bf16[32,64,512]{2,1,0:T(8,128)(2,1)}, u32[]{:S(2)}) copy-start(bf16[32,64,512]{2,1,0:T(8,128)(2,1)} %slice.335) | copy-start | bytes 6291460
  291.6 43.5 %copy-start.48 = (f32[256,512]{1,0:T(8,128)}, f32[256,512]{1,0:T(8,128)S(1)}, u32[]{:S(2)}) copy-start(f32[256,512]{1,0:T(8,128)S(1)} %get-tuple-element.805) | copy-start | bytes 1572868
  362.3 36.4 %copy-start.167 = (f32[64]{0:T(128)S(1)}, f32[64]{0:T(128)}, u32[]{:S(2)}) copy-start(f32[64]{0:T(128)} %fusion.124) | copy-start | bytes 772
  380.3 22.5 %copy-start.165 = (s32[1,64]{1,0:T(1,128)S(1)}, s32[1,64]{1,0:T(1,128)}, u32[]{:S(2)}) copy-start(s32[1,64]{1,0:T(1,128)} %param.38) | copy-start | bytes 772
  441.6 6.8 %copy-start.60 = (bf16[16,2,64,512]{3,2,1,0:T(8,128)(2,1)S(1)}, bf16[16,2,64,512]{3,2,1,0:T(8,128)(2,1)}, u32[]{:S(2)}) copy-start(bf16[16,2,64,512]{3,2,1,0:T(8,128)(2,1)} %shard_map.491) | copy-start | bytes 6291460
  451.9 19.8 %copy-start.49 = (f32[256,512]{1,0:T(8,128)S(1)}, f32[256,512]{1,0:T(8,128)}, u32[]{:S(2)}) copy-start(f32[256,512]{1,0:T(8,128)} %copy-done.48) | copy-start | bytes 1572868
  451.9 19.9 %copy-start.129 = (f32[256]{0:T(256)S(1)}, f32[256]{0:T(256)}, u32[]{:S(2)}) copy-start(f32[256]{0:T(256)} %copy-done.128) | copy-start | bytes 3076
  454.4 18.2 %copy-start.140 = (f32[256]{0:T(256)S(1)}, f32[256]{0:T(256)}, u32[]{:S(2)}) copy-start(f32[256]{0:T(256)} %copy-done.139) | copy-start | bytes 3076
  471.8 5.4 copy-start.50
  472.8 4.4 copy-start.61
  472.8 4.3 copy-start.52
  472.8 4.3 copy-start.86
  472.9 4.3 copy-start.88
  472.9 4.3 copy-start.90
  472.9 4.3 copy-start.92
  497.2 19.6 %copy-start.157 = (s32[768]{0:T(1024)S(1)}, s32[768]{0:T(1024)}, u32[]{:S(2)}) copy-start(s32[768]{0:T(1024)} %eq.426) | copy-start | bytes 9220
  520.6 6.5 %copy-start.170 = (pred[128]{0:T(512)(128)(4,1)S(1)}, pred[128]{0:T(512)(128)(4,1)}, u32[]{:S(2)}) copy-start(pred[128]{0:T(512)(128)(4,1)} %iota_compare_fusion.51) | copy-start | bytes 388
  520.6 6.5 %copy-start.171 = (pred[8]{0:T(512)(128)(4,1)S(1)}, pred[8]{0:T(512)(128)(4,1)}, u32[]{:S(2)}) copy-start(pred[8]{0:T(512)(128)(4,1)} %get-tuple-element.814) | copy-start | bytes 28
  520.6 6.5 %copy-start.172 = (pred[8]{0:T(512)(128)(4,1)S(1)}, pred[8]{0:T(512)(128)(4,1)}, u32[]{:S(2)}) copy-start(pred[8]{0:T(512)(128)(4,1)} %get-tuple-element.815) | copy-start | bytes 28
  530.9 37.0 %copy-start.4 = (bf16[960,512]{1,0:T(8,128)(2,1)S(1)}, bf16[960,512]{1,0:T(8,128)(2,1)}, u32[]{:S(2)}) copy-start(bf16[960,512]{1,0:T(8,128)(2,1)} %convert_element_type.311.table) | copy-start | bytes 2949124
  530.9 78.7 %copy-start.22 = (f32[8,512]{1,0:T(8,128)S(1)}, f32[8,512]{1,0:T(8,128)}, u32[]{:S(2)}) copy-start(f32[8,512]{1,0:T(8,128)} %refs_1_.1) | copy-start | bytes 49156
  609.6 31.4 %copy-start.1 = (bf16[1,768,2304]{2,1,0:T(8,128)(2,1)S(1)}, bf16[1,768,2304]{2,1,0:T(8,128)(2,1)}, u32[]{:S(2)}) copy-start(bf16[1,768,2304]{2,1,0:T(8,128)(2,1)} %param.63) | copy-start | bytes 10616836
  (97 other events, 183.1 us)
Sparse Core Ops, SparseCore 0:
  9.7 65.9 all-gather.4
  78.0 82.2 all-gather.6
  253.6 76.3 all-gather.8

commit v3 on v2

--- a/solution.py
+++ b/solution.py
@@ -1,4 +1,4 @@
-import math
+import functools
 from functools import partial
 
 import jax
@@ -14,6 +14,7 @@
 GRP_FSDP = ("grp", "y", "x", "c")
 T_ROOM = 48
 S_ROOM = 24
+WIDE = 56 * 2**20
 
 norm_eps = 1e-12
 clip_limit = 0.001
@@ -94,6 +95,76 @@
         ],
         compiler_params=pltpu.CompilerParams(collective_id=collective, has_side_effects=True),
     )(value)
+
+
+def route_kernel(notes, t_table, s_table, heard, got, sent, sends, arrivals, local):
+    f32, bf16 = jnp.float32, jnp.bfloat16
+    me = here()
+    greet([moved(me, *step) for step in AROUND])
+    copies = []
+    for k, step in enumerate(AROUND):
+        place = moved(me, *step)
+        copies.append(
+            remote(notes.at[number(place)], heard.at[number(me)], sends, arrivals, k, place)
+        )
+    heard[number(me)] = notes[number(me)]
+    for copy in copies:
+        copy.wait()
+    wants = heard[:, 0, :].astype(f32).T
+    vocab, t_width = t_table.shape
+    half = s_table.shape[1] // 2
+    batch = 8
+
+    def rows_of(at, room, peers, table):
+        index = jnp.concatenate([wants[at : at + room, p : p + 1] for p in peers], axis=0)
+        entry = lax.broadcasted_iota(jnp.int32, (index.shape[0], vocab), 1).astype(f32)
+        hot = jnp.where(entry == index, 1.0, 0.0).astype(bf16)
+        return product(hot, table[...])
+
+    for first in range(0, 32, batch):
+        peers = range(first, first + batch)
+        t_rows = rows_of(0, T_ROOM, peers, t_table)
+        s_rows = rows_of(T_ROOM, S_ROOM, peers, s_table)
+        for j, p in enumerate(peers):
+            sent[p, :, :t_width] = t_rows[j * T_ROOM : (j + 1) * T_ROOM].astype(bf16)
+            own = s_rows[j * S_ROOM : (j + 1) * S_ROOM]
+            own = jnp.concatenate([own[:, :half], own[:, half:]], axis=0)
+            sent[p, :, t_width:] = own.astype(bf16)
+    copies = []
+    for k, step in enumerate(AROUND):
+        place = moved(me, *step)
+        copies.append(
+            remote(
+                sent.at[number(place)], got.at[number(me)], sends, arrivals, len(AROUND) + k, place
+            )
+        )
+    mine = pltpu.make_async_copy(sent.at[number(me)], got.at[number(me)], local)
+    mine.start()
+    mine.wait()
+    for copy in copies:
+        copy.wait()
+
+
+def route(notes, t_table, s_table, collective):
+    width = t_table.shape[1] + s_table.shape[1] // 2
+    return pl.pallas_call(
+        route_kernel,
+        out_shape=[
+            jax.ShapeDtypeStruct(notes.shape, notes.dtype),
+            jax.ShapeDtypeStruct((32, T_ROOM, width), jnp.bfloat16),
+        ],
+        in_specs=[VMEM, VMEM, VMEM],
+        out_specs=[VMEM, ANY],
+        scratch_shapes=[
+            pltpu.VMEM((32, T_ROOM, width), jnp.bfloat16),
+            pltpu.SemaphoreType.DMA((2 * len(AROUND),)),
+            pltpu.SemaphoreType.DMA((2 * len(AROUND),)),
+            pltpu.SemaphoreType.DMA,
+        ],
+        compiler_params=pltpu.CompilerParams(
+            collective_id=collective, has_side_effects=True, vmem_limit_bytes=40 * 2**20
+        ),
+    )(notes, t_table, s_table)
 
 
 def group_exchange_kernel(source, target, sends, arrivals, local):
@@ -212,9 +283,321 @@
         ]
         + states * 3,
         out_specs=states * 3,
-        compiler_params=pltpu.CompilerParams(vmem_limit_bytes=40 * 2**20),
+        compiler_params=pltpu.CompilerParams(vmem_limit_bytes=WIDE),
     )(factor.reshape(1, 1), table_grad, rest_grad, norms_grad, *masters, *momenta, *averages)
     return tuple(outs)
+
+
+def normed(value, gain, shift):
+    mean = jnp.mean(value, -1, keepdims=True)
+    centred = value - mean
+    var = jnp.mean(centred * centred, -1, keepdims=True)
+    return centred * lax.rsqrt(var + norm_eps) * gain + shift
+
+
+def teacher_kernel(
+    lengths, slot, picks, got, extra, pos, norms, w_qkv, w_out, w_up, w_down, out, qkv, ctx
+):
+    f32, bf16 = jnp.float32, jnp.bfloat16
+    span, width = pos.shape
+    length = lengths[0, pl.program_id(0)]
+
+    def pick(index, count):
+        wide = lax.broadcasted_iota(jnp.int32, (index.shape[0], count), 1)
+        return jnp.where(wide == index, 1.0, 0.0).astype(bf16)
+
+    def scale(k):
+        return norms[2 * k : 2 * k + 1], norms[2 * k + 1 : 2 * k + 2]
+
+    emb = product(pick(slot[0], got.shape[0]), got[...])
+    emb = emb + extra[0].astype(f32) + pos[...].astype(f32)
+    first = normed(emb, *scale(0))
+    qkv[...] = product(first.astype(bf16), w_qkv[...]).astype(bf16)
+    lane = lax.broadcasted_iota(jnp.int32, (span, 2 * HD), 1)
+    halves = [jnp.where(lane < HD, 1.0, 0.0), jnp.where(lane < HD, 0.0, 1.0)]
+    valid = lax.broadcasted_iota(jnp.int32, (span, span), 1) < length
+    for pair in range(width // (2 * HD)):
+        at = 2 * HD * pair
+        query = qkv[:, at : at + 2 * HD]
+        keyed = qkv[:, width + at : width + at + 2 * HD]
+        valued = qkv[:, 2 * width + at : 2 * width + at + 2 * HD]
+        total = jnp.zeros((span, 2 * HD), f32)
+        for half in halves:
+            scores = lax.dot_general(
+                query * half.astype(bf16),
+                keyed,
+                (((1,), (1,)), ((), ())),
+                preferred_element_type=f32,
+            ) * HD ** (-0.5)
+            scores = jnp.where(valid, scores, -1e30)
+            spread = jnp.exp(scores - jnp.max(scores, -1, keepdims=True))
+            probs = spread * (1.0 / jnp.sum(spread, -1, keepdims=True))
+            total += half * product(probs.astype(bf16), valued)
+        ctx[:, at : at + 2 * HD] = total.astype(bf16)
+    second = normed(first + product(ctx[...], w_out[...]), *scale(1))
+    low = second.astype(bf16)
+    ffn = jnp.zeros((span, width), f32)
+    for at in range(0, w_up.shape[1], width):
+        pre = product(low, w_up[:, at : at + width])
+        active = (0.5 * pre * (1.0 + lax.erf(pre * (0.5**0.5)))).astype(bf16)
+        ffn += product(active, w_down[at : at + width, :])
+    final = normed(second + ffn, *scale(2))
+    out[0] = product(pick(picks[0], span), final.astype(bf16)).astype(bf16)
+
+
+def teacher_rows(lengths, slot, picks, got, extra, pos, norms, w_qkv, w_out, w_up, w_down):
+    count, picked = picks.shape
+    span, width = pos.shape
+
+    def whole(array, *shape):
+        shape = shape or array.shape
+        return pl.BlockSpec(shape, lambda i: (0,) * len(shape), pipeline_mode=pl.Buffered(1))
+
+    def each(*shape):
+        return pl.BlockSpec((1,) + shape, lambda i: (i, 0, 0))
+
+    return pl.pallas_call(
+        teacher_kernel,
+        grid=(count,),
+        out_shape=jax.ShapeDtypeStruct((count, picked, width), jnp.bfloat16),
+        in_specs=[
+            pl.BlockSpec(memory_space=pltpu.SMEM),
+            each(span, 1),
+            each(picked, 1),
+            whole(got, got.shape[0], width),
+            each(span, width),
+            whole(pos),
+            whole(norms),
+            whole(w_qkv),
+            whole(w_out),
+            whole(w_up),
+            whole(w_down),
+        ],
+        out_specs=each(picked, width),
+        scratch_shapes=[
+            pltpu.VMEM((span, 3 * width), jnp.bfloat16),
+            pltpu.VMEM((span, width), jnp.bfloat16),
+        ],
+        compiler_params=pltpu.CompilerParams(vmem_limit_bytes=WIDE),
+    )(
+        lengths[None],
+        slot.reshape(count, span, 1),
+        picks[:, :, None],
+        got,
+        extra,
+        pos,
+        norms,
+        w_qkv,
+        w_out,
+        w_up,
+        w_down,
+    )
+
+
+DEEP = 64
+WING = 256
+
+
+def by_eight(value):
+    return value.reshape(value.shape[0] // 8, 8, value.shape[1])
+
+
+def logits_kernel(labels, rows, head, out, stats):
+    f32 = jnp.float32
+    taken = rows[...].reshape(-1, rows.shape[-1])
+    vocab = out.shape[1]
+    parts = []
+    for at in range(0, taken.shape[0], WING):
+        logits = lax.dot_general(
+            head[0], taken[at : at + WING], (((1,), (1,)), ((), ())), preferred_element_type=f32
+        )
+        out[0, :, at : at + WING] = logits
+        parts.append(logits)
+    for k, logits in enumerate(parts):
+        cols = slice(k * WING, (k + 1) * WING)
+        top = jnp.max(jnp.max(by_eight(logits), 0), 0, keepdims=True)
+        row = lax.broadcasted_iota(jnp.int32, (DEEP, WING), 0) - labels[:, cols]
+        totals = [jnp.zeros((8, WING), f32)] * 3
+        for deep in range(0, vocab, DEEP):
+            part = logits[deep : deep + DEEP]
+            spread = jnp.exp(part - top)
+            hit = jnp.where(row == -deep, part, 0.0)
+            totals = [
+                total + jnp.sum(by_eight(more), 0)
+                for total, more in zip(totals, (spread, spread * part, hit))
+            ]
+        lines = [top] + [jnp.sum(total, 0, keepdims=True) for total in totals]
+        stats[0, :, cols] = jnp.concatenate(lines, axis=0)
+
+
+def vocabulary_logits(labels, rows, heads):
+    devices, count, picked, width = rows.shape
+    vocab = heads.shape[1]
+    block = 2 * WING // picked
+    wide = block * picked
+    return pl.pallas_call(
+        logits_kernel,
+        grid=(count, devices // block),
+        out_shape=[
+            jax.ShapeDtypeStruct((count, vocab, devices * picked), jnp.float32),
+            jax.ShapeDtypeStruct((count, 4, devices * picked), jnp.float32),
+        ],
+        in_specs=[
+            pl.BlockSpec((1, wide), lambda k, j: (0, j)),
+            pl.BlockSpec((block, 1, picked, width), lambda k, j: (j, k, 0, 0)),
+            pl.BlockSpec((1, vocab, width), lambda k, j: (k, 0, 0)),
+        ],
+        out_specs=[
+            pl.BlockSpec((1, vocab, wide), lambda k, j: (k, 0, j)),
+            pl.BlockSpec((1, 4, wide), lambda k, j: (k, 0, j)),
+        ],
+        compiler_params=pltpu.CompilerParams(vmem_limit_bytes=WIDE),
+    )(labels, rows, heads)
+
+
+def blend_kernel(stats, counted_ref, shift, loss, seen, sends, arrivals, local):
+    f32, bf16 = jnp.float32, jnp.bfloat16
+    me = here()
+    greet([moved(me, *step) for step in AROUND])
+
+    def columns(place):
+        chip = place["y"] * 4 + place["x"]
+        return stats.at[:, :, pl.ds(pl.multiple_of(chip * 128, 128), 128)]
+
+    copies = []
+    for k, step in enumerate(AROUND):
+        place = moved(me, *step)
+        copies.append(remote(columns(place), seen.at[number(me)], sends, arrivals, k, place))
+    own = pltpu.make_async_copy(columns(me), seen.at[number(me)], local)
+    own.start()
+    own.wait()
+    for copy in copies:
+        copy.wait()
+
+    def over_parts(k):
+        tops = seen[:, k, 0, :]
+        best = jnp.max(tops, 0, keepdims=True)
+        scale = jnp.exp(tops - best)
+        total = jnp.sum(seen[:, k, 1, :] * scale, 0, keepdims=True)
+        return best + jnp.log(total), scale, total
+
+    counted = counted_ref[...]
+    lane = lax.broadcasted_iota(jnp.int32, (1, 128), 1)
+    left = lane < 64
+    totals, entropies, chances = [], [], []
+    for k in range(4):
+        lse, scale, total = over_parts(k)
+        entropies.append(jnp.sum(seen[:, k, 2, :] * scale, 0, keepdims=True) / total - lse)
+        chances.append(counted * (jnp.sum(seen[:, k, 3, :], 0, keepdims=True) - lse))
+        totals.append(lse)
+    student, _, _ = over_parts(4)
+
+    def of_sequence(values):
+        first = jnp.sum(jnp.where(left, values, 0.0), -1, keepdims=True)
+        second = jnp.sum(jnp.where(left, 0.0, values), -1, keepdims=True)
+        return jnp.where(left, first, second)
+
+    hits = jnp.maximum(of_sequence(counted), 1.0)
+    gains = [of_sequence(chance) / hits for chance in chances]
+    best = functools.reduce(jnp.maximum, gains)
+    powers = [jnp.exp(gain - best) for gain in gains]
+    power = functools.reduce(jnp.add, powers)
+    entropy = jnp.zeros((1, 128), f32)
+    lines = []
+    for k in range(4):
+        lines.append(gains[k] - best - jnp.log(power) - totals[k])
+        entropy += (powers[k] / power * entropies[k]).astype(bf16).astype(f32)
+    lines += [student, counted, jnp.zeros((2, 128), f32)]
+    chip = me["y"] * 4 + me["x"]
+    shift[chip] = jnp.concatenate(lines, axis=0)
+    ours = jnp.where(left, 0, 1) == me["c"]
+    loss[...] = jnp.where(ours, counted * (entropy + student), 0.0)
+    copies = []
+    for k in range(1, 16):
+        place = moved(me, (7 * k) % 16 // 4, (7 * k) % 4, 0)
+        copies.append(remote(shift.at[chip], shift.at[chip], sends, arrivals, 30 + k, place))
+    for copy in copies:
+        copy.wait()
+
+
+def blend(stats, counted, collective):
+    return pl.pallas_call(
+        blend_kernel,
+        out_shape=[
+            jax.ShapeDtypeStruct((16, 8, 128), jnp.float32),
+            jax.ShapeDtypeStruct((1, 128), jnp.float32),
+        ],
+        in_specs=[VMEM, VMEM],
+        out_specs=[VMEM, VMEM],
+        scratch_shapes=[
+            pltpu.VMEM((32, 5, 4, 128), jnp.float32),
+            pltpu.SemaphoreType.DMA((46,)),
+            pltpu.SemaphoreType.DMA((46,)),
+            pltpu.SemaphoreType.DMA,
+        ],
+        compiler_params=pltpu.CompilerParams(collective_id=collective, has_side_effects=True),
+    )(stats, counted)
+
+
+def head_grads_kernel(logits, z, shift, h, table, head_grad, grad_rows, crossed, low):
+    f32, bf16 = jnp.float32, jnp.bfloat16
+    grad = jnp.zeros(head_grad.shape, f32)
+    for at in range(0, z.shape[2], WING):
+        cols = slice(at, at + WING)
+        lines = jnp.concatenate([shift[at // 128], shift[at // 128 + 1]], axis=1)
+        lse, counted = lines[4:5], lines[5:6]
+        total = jnp.zeros((8, WING), f32)
+        for deep in range(0, z.shape[1], DEEP):
+            rows = slice(deep, deep + DEEP)
+            target = jnp.zeros((DEEP, WING), f32)
+            for t in range(4):
+                share = jnp.exp(logits[t, rows, cols] + lines[t : t + 1])
+                target += share.astype(bf16).astype(f32)
+            student = z[0, rows, cols]
+            low[rows, cols] = (counted * (jnp.exp(student - lse) - target)).astype(bf16)
+            total += jnp.sum(by_eight(target * student), 0)
+        crossed[:, cols] = counted * jnp.sum(total, 0, keepdims=True)
+        grad_rows[cols] = lax.dot_general(
+            low[:, cols], table[...], (((0,), (0,)), ((), ())), preferred_element_type=f32
+        ).astype(bf16)
+        grad += product(low[:, cols], h[cols])
+
+    @pl.when(pl.program_id(0) == 0)
+    def _():
+        head_grad[...] = grad
+
+    @pl.when(pl.program_id(0) > 0)
+    def _():
+        head_grad[...] += grad
+
+
+def head_grads(logits, z, shift, h, table):
+    teachers, vocab, rows = logits.shape
+    width = table.shape[1]
+    wide = 2 * WING
+    return pl.pallas_call(
+        head_grads_kernel,
+        grid=(rows // wide,),
+        out_shape=[
+            jax.ShapeDtypeStruct((vocab, width), jnp.float32),
+            jax.ShapeDtypeStruct((rows, width), jnp.bfloat16),
+            jax.ShapeDtypeStruct((1, rows), jnp.float32),
+        ],
+        in_specs=[
+            pl.BlockSpec((teachers, vocab, wide), lambda j: (0, 0, j)),
+            pl.BlockSpec((1, vocab, wide), lambda j: (0, 0, j)),
+            pl.BlockSpec((wide // 128, 8, 128), lambda j: (j, 0, 0)),
+            pl.BlockSpec((wide, width), lambda j: (j, 0)),
+            pl.BlockSpec((vocab, width), lambda j: (0, 0)),
+        ],
+        out_specs=[
+            pl.BlockSpec((vocab, width), lambda j: (0, 0)),
+            pl.BlockSpec((wide, width), lambda j: (j, 0)),
+            pl.BlockSpec((1, wide), lambda j: (0, j)),
+        ],
+        scratch_shapes=[pltpu.VMEM((vocab, wide), jnp.bfloat16)],
+        compiler_params=pltpu.CompilerParams(vmem_limit_bytes=WIDE),
+    )(logits, z, shift, h, table)
 
 
 def scatter_sum_kernel(plan, *refs):
@@ -323,7 +706,7 @@
             pltpu.SemaphoreType.DMA((pieces,)),
         ],
         compiler_params=pltpu.CompilerParams(
-            collective_id=collective, has_side_effects=True, vmem_limit_bytes=40 * 2**20
+            collective_id=collective, has_side_effects=True, vmem_limit_bytes=WIDE
         ),
     )(*[part.reshape(16, 2, *part.shape[1:]) for part in parts])
 
@@ -690,7 +1073,7 @@
         turn, t_emb, s_emb = state
         t_slot, s_slot, t_want, s_want = ask_again(turn)
         t_more, s_more = placed(swap(answer(t_want, s_want)), t_slot, s_slot)
-        return turn + 1, t_emb + t_more, s_emb + s_more
+        return turn + 1, t_emb + t_more.astype(bf16), s_emb + s_more.astype(bf16)
 
     t_slot, s_slot, t_ask, s_ask = asked(0)
     line = jnp.concatenate(
@@ -702,14 +1085,14 @@
         jnp.broadcast_to(lengths[:, None], (fsdp, 128)),
     ]
     notes = jnp.stack(lines + [jnp.zeros((fsdp, 128), jnp.int32)] * 5, axis=1)
-    notes = exchange(notes, 1)
-    t_want, s_want = notes[:, 0, :T_ROOM], notes[:, 0, T_ROOM : T_ROOM + S_ROOM]
+    notes, got = route(notes, t_table[0], own_table, 1)
+    s_want = notes[:, 0, T_ROOM : T_ROOM + S_ROOM]
     rounds = jnp.max(notes[:, 0, T_ROOM + S_ROOM])
     plane_picks, plane_labels = notes[:, 1, :picked], notes[:, 1, picked : 2 * picked]
     plane_lengths = notes[:, 2, 0]
-    t_emb, s_emb = placed(exchange(answer(t_want, s_want), 2), t_slot, s_slot)
-    _, t_emb, s_emb = lax.while_loop(
-        lambda state: state[0] < rounds, more_rows, (jnp.int32(1), t_emb, s_emb)
+    nothing = (jnp.zeros((t_slot.shape[0], t_width), bf16), jnp.zeros((span, width), bf16))
+    _, t_extra, s_extra = lax.while_loop(
+        lambda state: state[0] < rounds, more_rows, (jnp.int32(1), *nothing)
     )
 
     def pieces(blocks, qkv, out, up, down, pos, norms):
@@ -758,73 +1141,43 @@
     student = (w_qkv, w_out, w_up, w_down, norms)
     heads = lax.all_gather(t_table[0], "grp", axis=0, tiled=False)
 
-    teacher = (t_qkv[0], t_out[0], t_up[0], t_down[0], t_norms[0])
-    t_embedded = t_emb.reshape(-1, span, t_width) + t_pos[0].astype(f32)[None]
-    teacher_final, _ = forward(t_embedded, group_lengths, teacher)
-    taken = jnp.take_along_axis(teacher_final, group_picks[:, :, None], axis=1).astype(bf16)
+    taken = teacher_rows(
+        group_lengths,
+        t_slot,
+        group_picks,
+        got.reshape(-1, got.shape[2]),
+        t_extra.reshape(-1, span, t_width),
+        t_pos[0],
+        t_norms[0].astype(f32).T,
+        t_qkv[0],
+        t_out[0],
+        t_up[0],
+        t_down[0],
+    )
     taken, heads = lax.optimization_barrier((taken, heads))
     rows = exchange_groups(taken, 10)
-    s_emb, rows = lax.optimization_barrier((s_emb, rows))
+    s_extra, got, rows = lax.optimization_barrier((s_extra, got, rows))
     rows = lax.all_gather(rows, FSDP, axis=0, tiled=False)
 
+    s_got = unfolded(got[:, :, t_width:]).reshape(-1, width)
+    s_emb = product(one_hot(s_slot, fsdp * S_ROOM), s_got) + s_extra.astype(f32)
     embedded = s_emb[None] + positions.astype(f32)[None]
     final, saved = forward(embedded, lengths, student)
     own_rows = jnp.take_along_axis(final, picks[:, :, None], axis=1).astype(bf16)[0]
     h = gather_plane(own_rows, 11)
-    z = jnp.einsum("rd,vd->rv", h, own_table, preferred_element_type=f32)
-
-    logits = jnp.einsum("fkpd,kvd->kfpv", rows, heads, preferred_element_type=f32)
-    logits = logits.reshape(logits.shape[0], -1, vocab_own)
     base = lax.axis_index(FSDP) * vocab_own
-    column = lax.broadcasted_iota(jnp.int32, (1, 1, vocab_own), 2) + base
-    at_label = column == plane_labels.reshape(1, -1, 1)
-    top = jnp.max(logits, -1)
-    spread = jnp.exp(logits - top[..., None])
-    stats = [
-        top,
-        jnp.sum(spread, -1),
-        jnp.sum(spread * logits, -1),
-        jnp.sum(jnp.where(at_label, logits, 0.0), -1),
-    ]
-    z_top = jnp.max(z, -1)
-    z_stats = [z_top, jnp.sum(jnp.exp(z - z_top[:, None]), -1)]
-    sent = jnp.concatenate(stats + [s[None] for s in z_stats], axis=0)
-    sent = jnp.moveaxis(sent.reshape(-1, fsdp, picked), 1, 0)
-    sent = jnp.pad(sent, ((0, 0), (0, 24 - sent.shape[1]), (0, 128 - picked)))
-    seen = exchange(sent, 3)[:, :, :picked]
-    tops, sums, dots, hits = [seen[:, 4 * j : 4 * j + 4] for j in range(4)]
-
-    def log_sum(tops, sums):
-        best = jnp.max(tops, 0)
-        scale = jnp.exp(tops - best)
-        return best, scale, jnp.sum(sums * scale, 0)
-
-    best, scale, total = log_sum(tops, sums)
-    t_lse = best + jnp.log(total)
-    t_ent = jnp.sum(dots * scale, 0) / total - t_lse
-    label_logp = jnp.sum(hits, 0) - t_lse
-    s_best, _, s_total = log_sum(seen[:, 16], seen[:, 17])
-    s_lse = s_best + jnp.log(s_total)
-    counted = (picks < lengths[:, None]).astype(f32)[0]
-    count_local = jnp.sum(counted)
-    label_loss = -jnp.sum(counted[None] * label_logp, -1) / jnp.maximum(count_local, 1.0)
-    log_blend = jax.nn.log_softmax(-label_loss)
-    blend = jax.nn.softmax(-label_loss)
-    entropy = jnp.sum((blend[:, None] * t_ent).astype(bf16).astype(f32), 0)
-    shift = jnp.concatenate([log_blend[:, None] - t_lse, s_lse[None]], axis=0)
-    shift = jnp.pad(shift, ((0, 3), (0, 128 - picked)))
-    shift = exchange(jnp.broadcast_to(shift, (fsdp, 8, 128)), 4)[:, :5, :picked]
-    shift = jnp.moveaxis(shift, 0, 1).reshape(5, -1)
-
-    plane_counted = (plane_picks < plane_lengths[:, None]).astype(f32).reshape(-1)
-    target = jnp.sum(jnp.exp(logits + shift[:4, :, None]).astype(bf16).astype(f32), 0)
-    loss_local = jnp.sum(counted * (entropy + s_lse)) - jnp.sum(
-        plane_counted * jnp.sum(target * z, -1)
-    )
-    grad_logits = (plane_counted[:, None] * (jnp.exp(z - shift[4][:, None]) - target)).astype(bf16)
-    grad_rows = jnp.einsum("rv,vd->rd", grad_logits, own_table, preferred_element_type=f32)
-    grad_rows = sum_and_scatter([grad_rows.astype(bf16).reshape(fsdp, picked, width)], width, f32, 5)
-    head_grad = jnp.einsum("rv,rd->vd", grad_logits, h, preferred_element_type=f32)
+    labels_here = plane_labels.reshape(1, -1) - base
+    z, z_stats = vocabulary_logits(labels_here, h.reshape(fsdp, 1, picked, width), own_table[None])
+    logits, stats = vocabulary_logits(labels_here, rows, heads)
+    stats = jnp.concatenate([stats, z_stats], axis=0)
+    plane_counted = (plane_picks < plane_lengths[:, None]).astype(f32).reshape(-1, 1, 2 * picked)
+    chip = lax.axis_index(("y", "x"))
+    chip_counted = lax.dynamic_index_in_dim(plane_counted, chip, 0, keepdims=False)
+    shift, own_loss = blend(stats, chip_counted, 3)
+    head_grad, grad_rows, crossed = head_grads(logits, z, shift, h, own_table)
+    count_local = jnp.sum((picks < lengths[:, None]).astype(f32))
+    loss_local = jnp.sum(own_loss) - jnp.sum(crossed)
+    grad_rows = sum_and_scatter([grad_rows.reshape(fsdp, picked, width)], width, f32, 5)
 
     grad_final = jnp.zeros(final.shape, f32).at[0, picks[0]].add(grad_rows)
     terms = backward(lengths, student, saved, grad_final)
@@ -859,12 +1212,13 @@
     seen = seen.sum(0)
     squares, loss_sum, count = jnp.sum(seen[:8]), seen[8, 0], seen[9, 0]
     at_norms = rest_sum.shape[0] - 8
-    norms_sum = rest_sum[at_norms, : s_norms.size].astype(f32).reshape(s_norms.shape)
+    norms_sum = rest_sum[at_norms, : s_norms.size].astype(f32).reshape(s_norms.shape).T
+    turned = [group[:6] + (group[6].T,) for group in (masters, momenta, averages)]
     clip_norm = jnp.sqrt(squares) / count
     factor = jnp.minimum(1.0, clip_limit / clip_norm) / count
-    return (loss_sum, count, clip_norm) + update(
-        factor, table_sum, rest_sum, norms_sum, masters, momenta, averages
-    )
+    outs = update(factor, table_sum, rest_sum, norms_sum, *turned)
+    outs = tuple(out.T if k % 7 == 6 else out for k, out in enumerate(outs))
+    return (loss_sum, count, clip_norm) + outs
 
 
 def solution(mesh):

time: 661 us -> 471 us (0.71)
  matrix products: 154 us -> 33.4 us
  Pallas kernels: 241 us -> 335 us
  other arithmetic: 115 us -> 25 us
  local copies, waits for them, and re-layouts: 109 us -> 32.9 us
  loops' own time: 1.92 us -> 10.3 us
    pallas_call x0 -> x6, Pallas kernels: none -> 169 us  [the longest x1 56.7 us: route(): pl.pallas_call(route_kernel, out_shape=[jax.ShapeDtypeStruct(notes.shape,...]
    pallas_call x5 -> x1, Pallas kernels: 98.8 us -> 17.2 us  [exchange(): pl.pallas_call(exchange_kernel, out_shape=jax.ShapeDtypeStruct(value.shap...]
    dot_general x8 -> x4, matrix products: 63.6 us -> 9.11 us  [project(): jnp.einsum('blk,kn->bln', left, right, preferred_element_type=jnp.float32)]
    reduce_sum x14 -> x3, other arithmetic: 56.1 us -> 1.82 us  [the longest x2 1.22 us: per_device(): loss_local = jnp.sum(own_loss) - jnp.sum(crossed)]
    dot_general x4 -> x0, matrix products: 35.8 us -> none  [the longest x1 22.6 us: per_device(): jnp.einsum('fkpd,kvd->kfpv', rows, heads, preferred_element_type=f32)]
    unnamed x330 -> x112, local copies, waits for them, and re-layouts: 46 us -> 10.8 us
    dot_general x6 -> x3, matrix products: 16.5 us -> 3.57 us  [product(): return jnp.dot(left, right, preferred_element_type=jnp.float32)]
    sub x2 -> x1, matrix products: 13.7 us -> 2.19 us  [forward(): probs = (jnp.exp(scores - top) / total).astype(jnp.bfloat16)]
  transfers between devices with their start and end apart: 3 -> 3, of which waited for: 0 -> 1; matrix products, arithmetic and copies ran while one was open for 32% -> 11% of each run, Pallas kernels for 16% -> 33%
where the time goes in v3:
time: 471 us; the launch traced here: 463 us
  Pallas kernels  335 us (71%)
  matrix products  33.4 us (7%)
  local copies, waits for them, and re-layouts  32.9 us (7%)
  other arithmetic  25 us (5%)
  between operations  25 us (5%)
  loops' own time  10.3 us (2%)
    pallas_call x1, Pallas kernels, route(): pl.pallas_call(route_kernel, out_shape=[jax.ShapeDtypeStruct(notes.shape,...  56.7 us
    pallas_call x2, Pallas kernels, sum_and_scatter(): pl.pallas_call(partial(scatter_sum_kernel, plan), out_shape=jax.ShapeDtyp...  55.9 us
    pallas_call x1, Pallas kernels, teacher_rows(): pl.pallas_call(teacher_kernel, grid=(count,), out_shape=jax.ShapeDtypeStr...  39.7 us
    pallas_call x2, Pallas kernels, vocabulary_logits(): pl.pallas_call(logits_kernel, grid=(count, devices // block), out_shape=[...  36.2 us
    pallas_call x1, Pallas kernels, sum_of_groups(): pl.pallas_call(group_sum_kernel, out_shape=[jax.ShapeDtypeStruct(table.sh...  35.6 us
    pallas_call x1, Pallas kernels, gather_plane(): pl.pallas_call(gather_kernel, out_shape=jax.ShapeDtypeStruct((16, 2, rows...  32.8 us
    pallas_call x1, Pallas kernels, head_grads(): pl.pallas_call(head_grads_kernel, grid=(rows // wide,), out_shape=[jax.Sh...  18.6 us
    pallas_call x1, Pallas kernels, blend(): pl.pallas_call(blend_kernel, out_shape=[jax.ShapeDtypeStruct((16, 8, 128)...  18.1 us
  transfers between devices with their start and end apart: 3, of which 1 were waited for; matrix products, arithmetic and copies ran while one was open for 11% of the time, Pallas kernels for 33%

profile of v3, /device:TPU:1, one launch (start us, length us, event | category | flops | bytes accessed | tf_op | source)
XLA Modules:
  0.0 462.9 jit_solution(4647357519857075253)
XLA Ops:
  8.9 0.7 convert_bitcast_fusion.3
  9.7 0.9 convert_bitcast_fusion.1
  10.6 0.8 constant_dynamic-update-slice_fusion.5
  11.3 0.9 convert_bitcast_fusion
  14.5 7.2 %shard_map.487 = s32[4,8,128]{2,1,0:T(8,128)} custom-call(s32[4,8,128]{2,1,0:T(8,128)} %broadcast_in_dim.296.source), custom_call_target="tpu_custom_call" | custom-call | tf_op jit(solution)/shard_map/pallas_call | solution.py:186
  21.7 0.7 slice_bitcast_fusion.1
  22.9 1.2 convert_reduce_fusion
  30.9 0.8 select_reduce_fusion.4
  32.4 56.7 %shard_map.488 = (s32[32,8,128]{2,1,0:T(8,128)S(1)}, bf16[32,48,1024]{2,1,0:T(8,128)(2,1)S(1)}) custom-call(s32[32,8,128]{2,1,0:T(8,128)S(1)} %stack.39.notes, bf16[960,768]{1,0:T(8,128)(2,1)} %bitcast.273, bf16[960,512]{1,0:T(8,128)(2,1)S(1)} %convert_element_type.212.s_table.table), custom_call_target="tpu_custom_call" | custom-call | tf_op jit(solution)/shard_map/pallas_call | solution.py:150
  89.2 1.7 copy-done
  90.9 1.2 slice_reduce_fusion.7
  92.2 1.0 copy.119.slot
  93.2 0.8 copy.120.picks
  94.6 1.2 broadcast_in_dim.304
  95.8 0.7 broadcast_in_dim.305
  96.5 9.4 %while.28 = (s32[]{:T(128)}, bf16[1024,768]{1,0:T(8,128)(2,1)}, bf16[256,512]{1,0:T(8,128)(2,1)}, s32[]{:T(128)}, s32[1024]{0:T(1024)S(1)}, /*index=5*/s32[1024]...) while((s32[]{:T(128)}, bf16[1024,768]{1,0:T(8,128)(2,1)}, ...), condition=%wide.region_12.13_spmd, body=%wide.region_9.12_spmd.sunk | while | flops 5660866048 | bytes 47710796 | solution.py:1094
  106.0 0.9 copy-done.8
  106.9 39.7 %shard_map.489.source = bf16[4,64,768]{2,1,0:T(8,128)(2,1)} custom-call(s32[1,4]{1,0:T(1,128)} %bitcast.342, s32[4,256,1]{2,1,0:T(8,128)} %copy.119.slot, s32[4,64,1]{2,1,0:T(8,128)} %copy.120.picks, bf16[1536,1024]{1,0:T(8,128)(2,1)} %bitcast.261, bf16[4,256,768]{2,1,0:T(8,128)(2,1)} %bitcast.21.extra, bf16[256,768]{1,0:T(8,128)(2,1)} %bitcast.313, ...), custom_call_target="tpu_custom_call" | custom-call | tf_op jit(solution)/shard_map/pallas_call | solution.py:359
  146.6 8.3 %shard_map.490 = bf16[4,64,768]{2,1,0:T(8,128)(2,1)} custom-call(bf16[4,64,768]{2,1,0:T(8,128)(2,1)} %shard_map.489.source), custom_call_target="tpu_custom_call" | custom-call | tf_op jit(solution)/shard_map/pallas_call | solution.py:186
  157.4 1.1 convert_bitcast_fusion.4.head
  158.5 1.2 fusion.101
  159.8 0.9 fusion.62
  160.9 1.5 fusion.108
  162.6 0.8 slice_reduce_fusion.1
  163.4 4.1 fusion.100
  167.5 0.8 copy-done.27
  169.5 3.3 slice.235
  172.7 2.2 fusion.109
  174.9 1.9 convolution_convert_fusion.10
  178.5 7.3 %multiply_convert_fusion.1 = (bf16[256,2048]{1,0:T(8,128)(2,1)S(1)}, f32[256,2048]{1,0:T(8,128)}, f32[256,2048]{1,0:T(8,128)}) fusion(bf16[512,512]{1,0:T(8,128)(2,1)S(1)} %bitcast.305, bf16[512,512]{1,0:T(8,128)(2,1)S(1)} %bitcast.307, bf16[512,512]{1,0:T(8,128)(2,1)S(1)} %bitcast.309, bf16[512,512]{1,0:T(8,128)(2,1)S(1)} %bitcast.311, ...), kind=kOutput, calls=%fused_computation.76 | convolution fusion | flops 579993600 | bytes 7870464 | tf_op jit(solution)/shard_map/blk,kn->bln/dot_general | solution.py:854
  185.8 0.8 fusion.111
  187.2 0.7 gather_fusion
  187.9 0.7 select_convert_fusion.source
  188.6 32.8 %shard_map.492 = bf16[16,2,64,512]{3,2,1,0:T(8,128)(2,1)} custom-call(bf16[64,512]{1,0:T(8,128)(2,1)} %select_convert_fusion.source), custom_call_target="tpu_custom_call" | custom-call | tf_op jit(solution)/shard_map/pallas_call | solution.py:220
  221.3 7.7 %shard_map.493 = (f32[1,960,2048]{2,1,0:T(8,128)}, f32[1,4,2048]{2,1,0:T(4,128)}) custom-call(s32[1,2048]{1,0:T(1,128)} %sub.231.labels, bf16[32,1,64,512]{3,2,1,0:T(8,128)(2,1)} %bitcast.268, bf16[1,960,512]{2,1,0:T(8,128)(2,1)} %convert_bitcast_fusion.4.head), custom_call_target="tpu_custom_call" | custom-call | tf_op jit(solution)/shard_map/pallas_call | solution.py:438
  229.0 0.8 all-gather.9.cloned.1.call-done
  229.8 28.5 %shard_map.491 = (f32[4,960,2048]{2,1,0:T(8,128)}, f32[4,4,2048]{2,1,0:T(4,128)}) custom-call(s32[1,2048]{1,0:T(1,128)} %sub.231.labels, bf16[32,4,64,768]{3,2,1,0:T(8,128)(2,1)} %bitcast.270, bf16[4,960,768]{2,1,0:T(8,128)(2,1)} %all-gather.5.cloned.1.call-done.head), custom_call_target="tpu_custom_call" | custom-call | tf_op jit(solution)/shard_map/pallas_call | solution.py:438
  258.4 1.6 pad_maximum_fusion.15.stats
  260.0 18.1 %shard_map.494 = (f32[16,8,128]{2,1,0:T(8,128)}, f32[1,128]{1,0:T(1,128)}) custom-call(f32[5,4,2048]{2,1,0:T(4,128)} %pad_maximum_fusion.15.stats, f32[1,128]{1,0:T(1,128)} %fusion.70.counted_ref), custom_call_target="tpu_custom_call" | custom-call | tf_op jit(solution)/shard_map/pallas_call | solution.py:524
  278.1 18.6 %shard_map.495 = (f32[960,512]{1,0:T(8,128)}, bf16[2048,512]{1,0:T(8,128)(2,1)}, f32[1,2048]{1,0:T(1,128)}) custom-call(f32[4,960,2048]{2,1,0:T(8,128)} %get-tuple-element.466.logits, f32[1,960,2048]{2,1,0:T(8,128)} %get-tuple-element.469.z, f32[16,8,128]{2,1,0:T(8,128)} %get-tuple-element.472.shift, bf16[2048,512]{1,0:T(8,128)(2,1)} %bitcast.269, ...), custom_call_target="tpu_custom_call" | custom-call | tf_op jit(solution)/shard_map/pallas_call | solution.py:578
  296.7 18.4 %shard_map.496 = f32[64,512]{1,0:T(8,128)} custom-call(bf16[16,2,64,512]{3,2,1,0:T(8,128)(2,1)} %bitcast.284), custom_call_target="tpu_custom_call" | custom-call | tf_op jit(solution)/shard_map/pallas_call | solution.py:689
  315.0 1.7 scatter_custom_fusion
  317.3 1.2 copy-done.14
  318.5 3.6 add_convert_fusion
  322.2 0.9 fusion.42
  324.0 2.2 convolution_convert_fusion.8
  328.6 0.8 fusion.43
  330.4 1.9 convolution_convert_fusion.4
  332.3 1.2 convolution_convert_fusion.7
  333.5 2.2 convolution_convert_fusion.3
  335.7 2.1 convolution_convert_fusion.2
  337.9 0.8 fusion.139
  338.7 0.9 pad_maximum_fusion.7.source
  339.7 17.2 %shard_map.497 = bf16[32,48,256]{2,1,0:T(8,128)(2,1)} custom-call(bf16[32,48,256]{2,1,0:T(8,128)(2,1)} %pad_maximum_fusion.7.source), custom_call_target="tpu_custom_call" | custom-call | tf_op jit(solution)/shard_map/pallas_call | solution.py:86
  356.9 1.3 fusion.102
  358.7 1.6 fusion.29
  360.3 0.9 while.29
  362.3 1.1 copy.133
  365.9 37.6 %shard_map.498.rest = bf16[208,512]{1,0:T(8,128)(2,1)} custom-call(bf16[16,2,16,1536]{3,2,1,0:T(8,128)(2,1)} %bitcast.289, bf16[16,2,16,512]{3,2,1,0:T(8,128)(2,1)} %bitcast.285, bf16[16,2,16,2048]{3,2,1,0:T(8,128)(2,1)} %bitcast.271, bf16[16,2,64,512]{3,2,1,0:T(8,128)(2,1)} %bitcast.272, bf16[16,2,16,512]{3,2,1,0:T(8,128)(2,1)} %bitcast.286), custom_call_target="tpu_custom_call" | custom-call | tf_op jit(solution)/shard_map/pallas_call | solution.py:689
  403.4 0.7 select_add_fusion.facts
  404.2 0.9 copy-done.2
  405.1 35.6 %shard_map.499 = (bf16[960,512]{1,0:T(8,128)(2,1)S(1)}, bf16[208,512]{1,0:T(8,128)(2,1)S(1)}, f32[32,16,128]{2,1,0:T(8,128)S(1)}) custom-call(bf16[960,512]{1,0:T(8,128)(2,1)S(1)} %convert_element_type.243.table, bf16[208,512]{1,0:T(8,128)(2,1)S(1)} %copy-done.2, f32[8,128]{1,0:T(8,128)S(1)} %select_add_fusion.facts), custom_call_target="tpu_custom_call" | custom-call | tf_op jit(solution)/shard_map/pallas_call | solution.py:782
  440.7 0.9 copy-done.1
  446.4 8.4 %shard_map.500 = (f32[960,512]{1,0:T(8,128)}, f32[8,512]{1,0:T(8,128)}, f32[16,1536]{1,0:T(8,128)}, f32[16,512]{1,0:T(8,128)}, f32[16,2048]{1,0:T(8,128)}, /*ind...) custom-call(f32[1,1]{1,0:T(1,128)} %bitcast.99.factor_ref, ...), custom_call_target="tpu_custom_call" | custom-call | tf_op jit(solution)/shard_map/pallas_call | solution.py:274
  (232 shorter events, 23.3 us)
Async XLA Ops:
  7.2 5.1 %copy-start.26 = (f32[64,512]{1,0:T(8,128)S(1)}, f32[64,512]{1,0:T(8,128)}, u32[]{:S(2)}) copy-start(f32[64,512]{1,0:T(8,128)} %refs_5_.1) | copy-start | bytes 393220
  7.2 6.6 %copy-start.51 = (s32[1,64]{1,0:T(1,128)S(1)}, s32[1,64]{1,0:T(1,128)}, u32[]{:S(2)}) copy-start(s32[1,64]{1,0:T(1,128)} %param.38) | copy-start | bytes 772
  7.2 6.6 %copy-start.50 = (s32[1,256]{1,0:T(1,128)S(1)}, s32[1,256]{1,0:T(1,128)}, u32[]{:S(2)}) copy-start(s32[1,256]{1,0:T(1,128)} %param.36) | copy-start | bytes 3076
  7.2 24.7 %copy-start.53 = (s32[1,64]{1,0:T(1,128)S(1)}, s32[1,64]{1,0:T(1,128)}, u32[]{:S(2)}) copy-start(s32[1,64]{1,0:T(1,128)} %param.39) | copy-start | bytes 772
  7.2 24.8 %copy-start.4 = (f32[960,512]{1,0:T(8,128)S(1)}, f32[960,512]{1,0:T(8,128)}, u32[]{:S(2)}) copy-start(f32[960,512]{1,0:T(8,128)} %refs_0_.1) | copy-start | bytes 5898244
  7.2 139.3 %all-gather.5.cloned.1.call-start = ((), (), s32[]{:S(2)}) async-start(), calls=%async_computation.4 | async-start | bytes 7372800 | tf_op jit(solution)/shard_map/all_gather | solution.py:1142
  8.0 151.8 %all-gather.7.cloned.1.call-start = ((), (), s32[]{:S(2)}) async-start(), calls=%async_computation.5 | async-start | bytes 7028736 | tf_op jit(solution)/shard_map/all_gather | solution.py:1139
  12.3 0.7 copy-start.46
  13.0 216.8 %all-gather.9.cloned.1.call-start = ((), (), s32[]{:S(2)}) async-start(), calls=%async_computation.6 | async-start | bytes 12976128 | tf_op jit(solution)/shard_map/all_gather | solution.py:1160
  32.1 61.8 %copy-start.48 = (bf16[1,768,6]{1,2,0:T(8,128)(2,1)S(1)}, bf16[1,768,6]{1,2,0:T(8,128)(2,1)}, u32[]{:S(2)}) copy-start(bf16[1,768,6]{1,2,0:T(8,128)(2,1)} %param.67) | copy-start | bytes 27652
  89.2 1.7 copy-start
  105.9 0.9 copy-start.8
  106.9 50.5 %copy-start.5 = (f32[960,512]{1,0:T(8,128)S(1)}, f32[960,512]{1,0:T(8,128)}, u32[]{:S(2)}) copy-start(f32[960,512]{1,0:T(8,128)} %refs_0_.1) | copy-start | bytes 5898244
  158.5 2.4 copy-start.45
  162.3 14.6 %copy-start.10 = (f32[256,512]{1,0:T(8,128)}, f32[256,512]{1,0:T(8,128)S(1)}, u32[]{:S(2)}) copy-start(f32[256,512]{1,0:T(8,128)S(1)} %get-tuple-element.637) | copy-start | bytes 1572868
  167.5 0.8 copy-start.27
  167.5 1.4 copy-start.29
  167.5 1.4 copy-start.31
  169.2 5.8 %copy-start.41 = (bf16[1,256,512]{1,2,0:T(8,128)(2,1)}, bf16[1,256,512]{1,2,0:T(8,128)(2,1)S(1)}, u32[]{:S(2)}) copy-start(bf16[1,256,512]{1,2,0:T(8,128)(2,1)S(1)} %copy.122) | copy-start | bytes 786436
  169.5 3.3 copy-start.18
  176.9 8.9 %copy-start.24 = (bf16[8,64,256]{2,1,0:T(8,128)(2,1)}, bf16[8,64,256]{2,1,0:T(8,128)(2,1)S(1)}, u32[]{:S(2)}) copy-start(bf16[8,64,256]{2,1,0:T(8,128)(2,1)S(1)} %convolution_convert_fusion.10) | copy-start | bytes 786436
  176.9 1.1 copy-start.33
  176.9 1.3 copy-start.35
  176.9 1.4 copy-start.37
  176.9 1.6 copy-start.39
  178.5 7.3 %copy-start.13 = (bf16[32,64,512]{2,1,0:T(8,128)(2,1)S(1)}, bf16[32,64,512]{2,1,0:T(8,128)(2,1)}, u32[]{:S(2)}) copy-start(bf16[32,64,512]{2,1,0:T(8,128)(2,1)} %slice.235) | copy-start | bytes 6291460
  185.8 1.0 copy-start.20
  229.8 28.5 %copy-start.47 = (f32[1,4,2048]{2,1,0:T(4,128)S(1)}, f32[1,4,2048]{2,1,0:T(4,128)}, u32[]{:S(2)}) copy-start(f32[1,4,2048]{2,1,0:T(4,128)} %get-tuple-element.471) | copy-start | bytes 98308
  229.8 48.2 %copy-start.9 = (bf16[960,512]{1,0:T(8,128)(2,1)S(1)}, bf16[960,512]{1,0:T(8,128)(2,1)}, u32[]{:S(2)}) copy-start(bf16[960,512]{1,0:T(8,128)(2,1)} %copy-done.8) | copy-start | bytes 2949124
  316.7 1.8 copy-start.14
  317.3 4.9 %copy-start.15 = (f32[1,256,512]{2,1,0:T(8,128)}, f32[1,256,512]{2,1,0:T(8,128)S(1)}, u32[]{:S(2)}) copy-start(f32[1,256,512]{2,1,0:T(8,128)S(1)} %get-tuple-element.583) | copy-start | bytes 1572868
  318.5 3.6 copy-start.34
  318.5 3.6 copy-start.36
  318.5 3.6 copy-start.38
  318.5 3.7 copy-start.40
  322.2 1.0 copy-start.22
  323.9 2.2 copy-start.12
  324.0 2.2 copy-start.42
  326.7 1.0 copy-start.19
  327.1 1.1 copy-start.11
  327.1 1.2 copy-start.28
  327.1 1.4 copy-start.30
  327.1 1.5 copy-start.32
  330.2 2.1 copy-start.25
  330.4 3.1 copy-start.23
  333.5 2.2 copy-start.16
  333.5 2.2 copy-start.21
  356.9 1.8 copy-start.52
  361.2 1.0 copy-start.17
  361.2 2.2 copy-start.54
  361.2 2.8 copy-start.49
  404.2 0.9 copy-start.2
  440.7 1.0 copy-start.1
  441.7 4.7 %copy-start.3 = (bf16[208,512]{1,0:T(8,128)(2,1)}, bf16[208,512]{1,0:T(8,128)(2,1)S(1)}, u32[]{:S(2)}) copy-start(bf16[208,512]{1,0:T(8,128)(2,1)S(1)} %get-tuple-element.480.rest_grad) | copy-start | bytes 638980
Sparse Core Ops, SparseCore 0:
  9.7 65.8 all-gather.4
  77.9 50.7 all-gather.6
  155.0 74.7 all-gather.8

commit v4 on v3

--- a/solution.py
+++ b/solution.py
@@ -1,4 +1,5 @@
 import functools
+import math
 from functools import partial
 
 import jax
@@ -14,6 +15,7 @@
 GRP_FSDP = ("grp", "y", "x", "c")
 T_ROOM = 48
 S_ROOM = 24
+S_APART = 32
 WIDE = 56 * 2**20
 
 norm_eps = 1e-12
@@ -66,38 +68,7 @@
     return copy
 
 
-def exchange_kernel(source, target, sends, arrivals, local):
-    me = here()
-    greet([moved(me, *step) for step in AROUND])
-    copies = []
-    for k, step in enumerate(AROUND):
-        place = moved(me, *step)
-        copies.append(
-            remote(source.at[number(place)], target.at[number(me)], sends, arrivals, k, place)
-        )
-    own = pltpu.make_async_copy(source.at[number(me)], target.at[number(me)], local)
-    own.start()
-    own.wait()
-    for copy in copies:
-        copy.wait()
-
-
-def exchange(value, collective):
-    return pl.pallas_call(
-        exchange_kernel,
-        out_shape=jax.ShapeDtypeStruct(value.shape, value.dtype),
-        in_specs=[ANY],
-        out_specs=ANY,
-        scratch_shapes=[
-            pltpu.SemaphoreType.DMA((len(AROUND),)),
-            pltpu.SemaphoreType.DMA((len(AROUND),)),
-            pltpu.SemaphoreType.DMA,
-        ],
-        compiler_params=pltpu.CompilerParams(collective_id=collective, has_side_effects=True),
-    )(value)
-
-
-def route_kernel(notes, t_table, s_table, heard, got, sent, sends, arrivals, local):
+def route_kernel(notes, t_table, s_table, heard, got, sent, wants, sends, arrivals, local):
     f32, bf16 = jnp.float32, jnp.bfloat16
     me = here()
     greet([moved(me, *step) for step in AROUND])
@@ -110,26 +81,32 @@
     heard[number(me)] = notes[number(me)]
     for copy in copies:
         copy.wait()
-    wants = heard[:, 0, :].astype(f32).T
+    all_wants = heard[:, 0, :].astype(f32).T
     vocab, t_width = t_table.shape
     half = s_table.shape[1] // 2
-    batch = 8
-
-    def rows_of(at, room, peers, table):
-        index = jnp.concatenate([wants[at : at + room, p : p + 1] for p in peers], axis=0)
+    batch = wants.shape[2]
+    for k in range(wants.shape[0]):
+        wants[k] = all_wants[:, k * batch : (k + 1) * batch]
+
+    def rows_of(k, at, room, table):
+        index = jnp.concatenate(
+            [wants[k, at : at + room, p : p + 1] for p in range(batch)], axis=0
+        )
         entry = lax.broadcasted_iota(jnp.int32, (index.shape[0], vocab), 1).astype(f32)
         hot = jnp.where(entry == index, 1.0, 0.0).astype(bf16)
         return product(hot, table[...])
 
-    for first in range(0, 32, batch):
-        peers = range(first, first + batch)
-        t_rows = rows_of(0, T_ROOM, peers, t_table)
-        s_rows = rows_of(T_ROOM, S_ROOM, peers, s_table)
-        for j, p in enumerate(peers):
+    @pl.loop(0, wants.shape[0])
+    def _(k):
+        t_rows = rows_of(k, 0, T_ROOM, t_table)
+        s_rows = rows_of(k, T_ROOM, S_ROOM, s_table)
+        for j in range(batch):
+            p = k * batch + j
             sent[p, :, :t_width] = t_rows[j * T_ROOM : (j + 1) * T_ROOM].astype(bf16)
             own = s_rows[j * S_ROOM : (j + 1) * S_ROOM]
             own = jnp.concatenate([own[:, :half], own[:, half:]], axis=0)
             sent[p, :, t_width:] = own.astype(bf16)
+
     copies = []
     for k, step in enumerate(AROUND):
         place = moved(me, *step)
@@ -157,6 +134,7 @@
         out_specs=[VMEM, ANY],
         scratch_shapes=[
             pltpu.VMEM((32, T_ROOM, width), jnp.bfloat16),
+            pltpu.VMEM((4, 128, 8), jnp.float32),
             pltpu.SemaphoreType.DMA((2 * len(AROUND),)),
             pltpu.SemaphoreType.DMA((2 * len(AROUND),)),
             pltpu.SemaphoreType.DMA,
@@ -316,11 +294,11 @@
     lane = lax.broadcasted_iota(jnp.int32, (span, 2 * HD), 1)
     halves = [jnp.where(lane < HD, 1.0, 0.0), jnp.where(lane < HD, 0.0, 1.0)]
     valid = lax.broadcasted_iota(jnp.int32, (span, span), 1) < length
-    for pair in range(width // (2 * HD)):
-        at = 2 * HD * pair
-        query = qkv[:, at : at + 2 * HD]
-        keyed = qkv[:, width + at : width + at + 2 * HD]
-        valued = qkv[:, 2 * width + at : 2 * width + at + 2 * HD]
+
+    def heads_at(at):
+        query = qkv[:, pl.ds(at, 2 * HD)]
+        keyed = qkv[:, pl.ds(width + at, 2 * HD)]
+        valued = qkv[:, pl.ds(2 * width + at, 2 * HD)]
         total = jnp.zeros((span, 2 * HD), f32)
         for half in halves:
             scores = lax.dot_general(
@@ -333,7 +311,11 @@
             spread = jnp.exp(scores - jnp.max(scores, -1, keepdims=True))
             probs = spread * (1.0 / jnp.sum(spread, -1, keepdims=True))
             total += half * product(probs.astype(bf16), valued)
-        ctx[:, at : at + 2 * HD] = total.astype(bf16)
+        ctx[:, pl.ds(at, 2 * HD)] = total.astype(bf16)
+
+    for at in range(0, width, 2 * HD):
+        heads_at(at)
+
     second = normed(first + product(ctx[...], w_out[...]), *scale(1))
     low = second.astype(bf16)
     ffn = jnp.zeros((span, width), f32)
@@ -539,7 +521,9 @@
     )(stats, counted)
 
 
-def head_grads_kernel(logits, z, shift, h, table, head_grad, grad_rows, crossed, low):
+def head_grads_kernel(
+    logits, z, shift, h, table, head_grad, head_low, grad_rows, crossed, low
+):
     f32, bf16 = jnp.float32, jnp.bfloat16
     grad = jnp.zeros(head_grad.shape, f32)
     for at in range(0, z.shape[2], WING):
@@ -570,6 +554,10 @@
     def _():
         head_grad[...] += grad
 
+    @pl.when(pl.program_id(0) == pl.num_programs(0) - 1)
+    def _():
+        head_low[...] = head_grad[...].astype(bf16)
+
 
 def head_grads(logits, z, shift, h, table):
     teachers, vocab, rows = logits.shape
@@ -580,6 +568,7 @@
         grid=(rows // wide,),
         out_shape=[
             jax.ShapeDtypeStruct((vocab, width), jnp.float32),
+            jax.ShapeDtypeStruct((vocab, width), jnp.bfloat16),
             jax.ShapeDtypeStruct((rows, width), jnp.bfloat16),
             jax.ShapeDtypeStruct((1, rows), jnp.float32),
         ],
@@ -592,24 +581,36 @@
         ],
         out_specs=[
             pl.BlockSpec((vocab, width), lambda j: (0, 0)),
+            pl.BlockSpec((vocab, width), lambda j: (0, 0)),
             pl.BlockSpec((wide, width), lambda j: (j, 0)),
             pl.BlockSpec((1, wide), lambda j: (0, j)),
         ],
         scratch_shapes=[pltpu.VMEM((vocab, wide), jnp.bfloat16)],
-        compiler_params=pltpu.CompilerParams(vmem_limit_bytes=WIDE),
+        compiler_params=pltpu.CompilerParams(vmem_limit_bytes=40 * 2**20),
     )(logits, z, shift, h, table)
 
 
-def scatter_sum_kernel(plan, *refs):
+def quarter(group):
+    return pl.ds(pl.multiple_of(group * 128, 128), 128)
+
+
+def scatter_sum_kernel(plan, side, *refs):
     f32, bf16 = jnp.float32, jnp.bfloat16
     parts, refs = refs[: len(plan)], refs[len(plan) :]
-    out, own, other, both, in_a, in_b, mid_a, mid_b, end_a, end_b, sends, arrivals, local = refs
+    if side == "head":
+        exact, sided, out, side_out, mine_exact, side_in, *refs = refs
+    else:
+        sided, out, side_out, side_in, *refs = refs
+    own, other, both, in_a, in_b, mid_a, mid_b, end_a, end_b, sends, arrivals, local = refs
     me = here()
+    group = lax.axis_index("grp")
+    groups = [{"grp": lax.rem(group + d, 4)} for d in (1, 2, 3)]
     steps_x = [moved(me, 0, d, 0) for d in (1, 2, 3)]
     steps_y = [moved(me, d, 0, 0) for d in (1, 2, 3)]
     sibling = moved(me, 0, 0, 1)
-    greet([sibling] + steps_x + steps_y)
-    copies, at, k = [], 0, 13
+    plane = [moved(me, *step) for step in AROUND]
+    greet(groups + (plane if side == "rows" else [sibling] + steps_x + steps_y))
+    copies, at, k = [], 0, 16
     width = own.shape[-1]
     for part, (rows, columns) in zip(parts, plan):
         for column in range(0, columns, width):
@@ -626,12 +627,30 @@
                 )
             )
             mine = pltpu.make_async_copy(
-                part.at[:, me["c"], :, cols], own.at[span], local.at[k - 13]
+                part.at[:, me["c"], :, cols], own.at[span], local.at[k - 15]
             )
             mine.start()
             copies.append(mine)
             at += rows
             k += 1
+    over = [
+        remote(
+            sided.at[:, quarter(place["grp"])],
+            side_in.at[group] if side == "rows" else side_in.at[d],
+            sends,
+            arrivals,
+            13 + d,
+            place,
+        )
+        for d, place in enumerate(groups)
+    ]
+    kept = pltpu.make_async_copy(
+        (sided if side == "rows" else exact).at[:, quarter(group)],
+        side_in.at[group] if side == "rows" else mine_exact,
+        local.at[0],
+    )
+    kept.start()
+    over.append(kept)
     for copy in copies:
         copy.wait()
 
@@ -650,6 +669,20 @@
         copies.append(
             remote(both.at[to_y["y"], :, :, right], in_b.at[d], sends, arrivals, 4 + d, to_y)
         )
+    last = []
+    if side == "rows":
+        for copy in over:
+            copy.wait()
+        room = side_in.shape[1] // 32
+
+        def of(place):
+            return side_in.at[:, pl.ds(pl.multiple_of(number(place) * room, room), room)]
+
+        for j, place in enumerate(plane):
+            last.append(remote(of(place), side_out.at[number(me)], sends, arrivals, k + j, place))
+        kept = pltpu.make_async_copy(of(me), side_out.at[number(me)], local.at[0])
+        kept.start()
+        last.append(kept)
     for copy in copies:
         copy.wait()
 
@@ -668,6 +701,13 @@
         to_x, to_y = steps_x[d], steps_y[d]
         copies.append(remote(mid_a.at[to_y["y"]], end_a.at[d], sends, arrivals, 7 + d, to_y))
         copies.append(remote(mid_b.at[to_x["x"]], end_b.at[d], sends, arrivals, 10 + d, to_x))
+    if side == "head":
+        for copy in over:
+            copy.wait()
+        total = mine_exact[...]
+        for d in range(3):
+            total += side_in[d].astype(f32)
+        side_out[...] = total
     for copy in copies:
         copy.wait()
     total_a = mid_a[me["y"]].astype(f32)
@@ -677,21 +717,33 @@
         total_b += end_b[d].astype(f32)
     out[:, left] = total_a.astype(out.dtype)
     out[:, right] = total_b.astype(out.dtype)
-
-
-def sum_and_scatter(parts, width, dtype, collective):
+    for copy in last:
+        copy.wait()
+
+
+def sum_and_scatter(parts, width, dtype, side, sided, collective):
     plan = [part.shape[1:] for part in parts]
     rows = sum(r * (c // width) for r, c in plan)
     pieces = sum(c // width for _, c in plan)
     cut = width // 2
     rest = width - cut
     bf16 = jnp.bfloat16
+    room = (12 if side == "head" else 28) * 2**20
+    tall = sided[0].shape[0]
+    if side == "head":
+        side_out = jax.ShapeDtypeStruct((tall, 128), jnp.float32)
+        side_scratch = [pltpu.VMEM((tall, 128), jnp.float32), pltpu.VMEM((3, tall, 128), bf16)]
+    else:
+        side_out = jax.ShapeDtypeStruct((32, 4, tall // 32, 128), bf16)
+        side_scratch = [pltpu.VMEM((4, tall, 128), bf16)]
+    semaphores = 16 + pieces + (len(AROUND) if side == "rows" else 0)
     return pl.pallas_call(
-        partial(scatter_sum_kernel, plan),
-        out_shape=jax.ShapeDtypeStruct((rows, width), dtype),
-        in_specs=[ANY] * len(parts),
-        out_specs=VMEM,
-        scratch_shapes=[
+        partial(scatter_sum_kernel, plan, side),
+        out_shape=[jax.ShapeDtypeStruct((rows, width), dtype), side_out],
+        in_specs=[ANY] * (len(parts) + len(sided)),
+        out_specs=[VMEM, VMEM],
+        scratch_shapes=side_scratch
+        + [
             pltpu.VMEM((16, rows, width), bf16),
             pltpu.VMEM((16, rows, width), bf16),
             pltpu.VMEM((4, 4, rows, width), bf16),
@@ -701,18 +753,18 @@
             pltpu.VMEM((4, rows, rest), bf16),
             pltpu.VMEM((3, rows, cut), bf16),
             pltpu.VMEM((3, rows, rest), bf16),
-            pltpu.SemaphoreType.DMA((13 + pieces,)),
-            pltpu.SemaphoreType.DMA((13 + pieces,)),
-            pltpu.SemaphoreType.DMA((pieces,)),
+            pltpu.SemaphoreType.DMA((semaphores,)),
+            pltpu.SemaphoreType.DMA((semaphores,)),
+            pltpu.SemaphoreType.DMA((1 + pieces,)),
         ],
         compiler_params=pltpu.CompilerParams(
-            collective_id=collective, has_side_effects=True, vmem_limit_bytes=WIDE
+            collective_id=collective, has_side_effects=True, vmem_limit_bytes=room
         ),
-    )(*[part.reshape(16, 2, *part.shape[1:]) for part in parts])
+    )(*[part.reshape(16, 2, *part.shape[1:]) for part in parts], *sided)
 
 
 def group_sum_kernel(
-    table, rest, facts, table_out, rest_out, seen, table_in, rest_in, told, sends, arrivals, local
+    head, wants, given, rest, facts, table_out, rest_out, seen, total, rest_in, told, sends, arrivals
 ):
     f32, bf16 = jnp.float32, jnp.bfloat16
     me = here()
@@ -720,50 +772,43 @@
     groups = [{"grp": lax.rem(group + d, 4)} for d in (1, 2, 3)]
     plane = [moved(me, *step) for step in AROUND]
     greet(groups + plane)
-
-    def quarter(g):
-        return pl.ds(pl.multiple_of(g * 128, 128), 128)
-
     mine = quarter(group)
-    copies = []
+    early = [
+        remote(rest.at[:, quarter(groups[d]["grp"])], rest_in.at[d], sends, arrivals, d, groups[d])
+        for d in range(3)
+    ]
+    total[...] = head[...]
+
+    @pl.loop(0, wants.shape[0])
+    def _(k):
+        row = lax.broadcasted_iota(jnp.int32, (head.shape[0], wants.shape[1]), 0)
+        hot = jnp.where(row == wants[pl.ds(k, 1), :], 1.0, 0.0).astype(bf16)
+        total[...] += product(hot, given[k])
+
+    rounded = total[...].astype(bf16)
+    table_out[:, mine] = rounded
+    rounded = rounded.astype(f32)
+    squares = jnp.sum(by_eight(rounded * rounded), 0)
+    wide = [
+        remote(table_out.at[:, mine], table_out.at[:, mine], sends, arrivals, 3 + d, groups[d])
+        for d in range(3)
+    ]
+    for copy in early:
+        copy.wait()
+    summed = rest[:, mine].astype(f32)
     for d in range(3):
-        theirs = quarter(groups[d]["grp"])
-        copies.append(remote(table.at[:, theirs], table_in.at[d], sends, arrivals, d, groups[d]))
-        copies.append(remote(rest.at[:, theirs], rest_in.at[d], sends, arrivals, 3 + d, groups[d]))
-    for copy in copies:
-        copy.wait()
-
-    def summed(source, arrived, target):
-        rows = 16
-
-        def body(k, squares):
-            at = pl.ds(pl.multiple_of(k * rows, rows), rows)
-            total = source[at, mine].astype(f32)
-            for d in range(3):
-                total += arrived[d, at].astype(f32)
-            total = total.astype(bf16)
-            target[at, mine] = total
-            total = total.astype(f32)
-            total = total * total
-            return squares + total[:8] + total[8:]
-
-        return lax.fori_loop(0, source.shape[0] // rows, body, jnp.zeros((8, 128), f32))
-
-    squares = summed(table, table_in, table_out) + summed(rest, rest_in, rest_out)
+        summed += rest_in[d].astype(f32)
+    summed = summed.astype(bf16)
+    rest_out[:, mine] = summed
+    summed = summed.astype(f32)
+    squares += jnp.sum(by_eight(summed * summed), 0)
     told[group, 0:8] = squares
     told[group, 8:16] = facts[...]
     copies = []
     for d in range(3):
-        copies.append(
-            remote(told.at[group], told.at[group], sends, arrivals, 6 + d, groups[d])
-        )
-    wide = []
-    for d in range(3):
+        copies.append(remote(told.at[group], told.at[group], sends, arrivals, 6 + d, groups[d]))
         wide.append(
-            remote(table_out.at[:, mine], table_out.at[:, mine], sends, arrivals, 9 + d, groups[d])
-        )
-        wide.append(
-            remote(rest_out.at[:, mine], rest_out.at[:, mine], sends, arrivals, 12 + d, groups[d])
+            remote(rest_out.at[:, mine], rest_out.at[:, mine], sends, arrivals, 9 + d, groups[d])
         )
     for copy in copies:
         copy.wait()
@@ -771,35 +816,35 @@
     copies = []
     for k, place in enumerate(plane):
         copies.append(
-            remote(seen.at[number(me)], seen.at[number(me)], sends, arrivals, 15 + k, place)
+            remote(seen.at[number(me)], seen.at[number(me)], sends, arrivals, 12 + k, place)
         )
     for copy in copies + wide:
         copy.wait()
 
 
-def sum_of_groups(table, rest, facts, collective):
-    count = 15 + len(AROUND)
+def sum_of_groups(head, wants, given, rest, facts, collective):
+    count = 12 + len(AROUND)
+    bf16 = jnp.bfloat16
     return pl.pallas_call(
         group_sum_kernel,
         out_shape=[
-            jax.ShapeDtypeStruct(table.shape, table.dtype),
+            jax.ShapeDtypeStruct((head.shape[0], 512), bf16),
             jax.ShapeDtypeStruct(rest.shape, rest.dtype),
             jax.ShapeDtypeStruct((32, 16, 128), jnp.float32),
         ],
-        in_specs=[VMEM, VMEM, VMEM],
+        in_specs=[VMEM] * 5,
         out_specs=[VMEM, VMEM, VMEM],
         scratch_shapes=[
-            pltpu.VMEM((3, table.shape[0], 128), table.dtype),
+            pltpu.VMEM(head.shape, jnp.float32),
             pltpu.VMEM((3, rest.shape[0], 128), rest.dtype),
             pltpu.VMEM((4, 16, 128), jnp.float32),
             pltpu.SemaphoreType.DMA((count,)),
             pltpu.SemaphoreType.DMA((count,)),
-            pltpu.SemaphoreType.DMA,
         ],
         compiler_params=pltpu.CompilerParams(
             collective_id=collective, has_side_effects=True, vmem_limit_bytes=40 * 2**20
         ),
-    )(table, rest, facts)
+    )(head, wants, given, rest, facts)
 
 
 def slots(tokens, own_rows):
@@ -812,9 +857,9 @@
     return owner, ~repeated, jnp.sum(counts.astype(jnp.int32), axis=0)
 
 
-def slot_in_round(owner, rank, room, turn):
+def slot_in_round(owner, rank, room, turn, apart=None):
     at = rank - turn * room
-    return jnp.where((at >= 0) & (at < room), owner * room + at, -1)
+    return jnp.where((at >= 0) & (at < room), owner * (apart or room) + at, -1)
 
 
 def wanted_rows(slot, first, local, places):
@@ -845,21 +890,8 @@
     return centred * lax.rsqrt(var + norm_eps) * gain + shift
 
 
-def norm_back(value, gain, shift, grad):
-    _, pull = jax.vjp(layer_norm, value, gain, shift)
-    return pull(grad)
-
-
 def project(left, right):
     return jnp.einsum("blk,kn->bln", left, right, preferred_element_type=jnp.float32)
-
-
-def project_back(grad, right):
-    return jnp.einsum("bln,kn->blk", grad, right, preferred_element_type=jnp.float32)
-
-
-def weight_grad(left, grad):
-    return jnp.einsum("blk,bln->kn", left, grad, preferred_element_type=jnp.float32)
 
 
 def split_heads(packed, width):
@@ -903,8 +935,6 @@
         embedded,
         first_low,
         packed,
-        top,
-        total,
         context,
         joined,
         second_low,
@@ -915,66 +945,161 @@
     return (final, saved)
 
 
-def backward(lengths, weights, saved, grad_final):
+def norm_back(value, gain, grad):
+    mean = jnp.mean(value, -1, keepdims=True)
+    centred = value - mean
+    scale = lax.rsqrt(jnp.mean(centred * centred, -1, keepdims=True) + norm_eps)
+    unit = centred * scale
+    scaled = grad * gain
+    back = scaled - jnp.mean(scaled, -1, keepdims=True)
+    back = scale * (back - unit * jnp.mean(scaled * unit, -1, keepdims=True))
+    return back, jnp.sum(grad * unit, 0, keepdims=True), jnp.sum(grad, 0, keepdims=True)
+
+
+def product_of(left, right, dims):
+    return lax.dot_general(left, right, (dims, ((), ())), preferred_element_type=jnp.float32)
+
+
+def backward_kernel(
+    lengths,
+    picks,
+    slot,
+    grad_rows,
+    embedded,
+    first_low,
+    packed,
+    context,
+    joined,
+    second_low,
+    hidden_pre,
+    active,
+    summed,
+    norms,
+    w_qkv,
+    w_out,
+    w_up,
+    w_down,
+    g_qkv,
+    g_out,
+    g_up,
+    g_down,
+    g_emb,
+    g_norms,
+    given,
+    d_packed,
+    d_context,
+    carried,
+):
+    f32, bf16 = jnp.float32, jnp.bfloat16
+    span, width = embedded.shape
+    rows, columns, both = ((0,), (0,)), ((1,), (1,)), ((1,), (0,))
+    row = lax.broadcasted_iota(jnp.int32, (span, picks.shape[1]), 0)
+    hot = jnp.where(row == picks[...], 1.0, 0.0)
+    d_final = jnp.dot(
+        hot, grad_rows[...], preferred_element_type=f32, precision=lax.Precision.HIGHEST
+    )
+    d_summed, gain_c, shift_c = norm_back(summed[...], norms[4:5], d_final)
+    d_ffn = d_summed.astype(bf16)
+    carried[...] = d_summed
+
+    @pl.loop(0, w_up.shape[1] // width)
+    def _(k):
+        cols = pl.ds(pl.multiple_of(k * width, width), width)
+        g_down[cols] = product_of(active[:, cols], d_ffn, rows).astype(bf16)
+        pre = hidden_pre[:, cols]
+        slope = 0.5 * (1.0 + lax.erf(pre * (0.5**0.5)))
+        slope += pre * (jnp.exp(-0.5 * pre * pre) * (0.5 / math.pi) ** 0.5)
+        d_up = (slope * product_of(d_ffn, w_down[cols], columns)).astype(bf16)
+        g_up[:, cols] = product_of(second_low[...], d_up, rows).astype(bf16)
+        carried[...] += product_of(d_up, w_up[:, cols], columns)
+
+    d_joined, gain_b, shift_b = norm_back(joined[...], norms[2:3], carried[...])
+    d_attn = d_joined.astype(bf16)
+    g_out[...] = product_of(context[...], d_attn, rows).astype(bf16)
+    d_context[...] = product_of(d_attn, w_out[...], columns).astype(bf16)
+    lane = lax.broadcasted_iota(jnp.int32, (span, 2 * HD), 1)
+    halves = [jnp.where(lane < HD, 1.0, 0.0), jnp.where(lane < HD, 0.0, 1.0)]
+    valid = lax.broadcasted_iota(jnp.int32, (span, span), 1) < lengths[0, 0]
+
+    @pl.loop(0, width // (2 * HD))
+    def _(k):
+        at = pl.multiple_of(k * 2 * HD, 2 * HD)
+        query, keyed, valued = [
+            packed[:, pl.ds(piece * width + at, 2 * HD)] for piece in range(3)
+        ]
+        d_heads = d_context[:, pl.ds(at, 2 * HD)]
+        d_query, d_keyed, d_valued = [jnp.zeros((span, 2 * HD), f32)] * 3
+        for half in halves:
+            low = half.astype(bf16)
+            scores = product_of(query * low, keyed, columns) * HD ** (-0.5)
+            scores = jnp.where(valid, scores, -1e30)
+            spread = jnp.exp(scores - jnp.max(scores, -1, keepdims=True))
+            probs = spread * (1.0 / jnp.sum(spread, -1, keepdims=True))
+            d_valued += half * product_of(probs.astype(bf16), d_heads, rows)
+            d_probs = product_of(d_heads * low, valued, columns)
+            d_scores = probs * (d_probs - jnp.sum(probs * d_probs, -1, keepdims=True))
+            d_scores = d_scores.astype(bf16)
+            d_query += half * product_of(d_scores, keyed, both)
+            d_keyed += half * product_of(d_scores, query, rows)
+        for piece, value in enumerate((d_query * HD ** (-0.5), d_keyed * HD ** (-0.5), d_valued)):
+            d_packed[:, pl.ds(piece * width + at, 2 * HD)] = value.astype(bf16)
+
+    carried[...] = d_joined
+
+    @pl.loop(0, 3)
+    def _(k):
+        cols = pl.ds(pl.multiple_of(k * width, width), width)
+        g_qkv[:, cols] = product_of(first_low[...], d_packed[:, cols], rows).astype(bf16)
+        carried[...] += product_of(d_packed[:, cols], w_qkv[:, cols], columns)
+
+    d_emb, gain_a, shift_a = norm_back(embedded[...], norms[0:1], carried[...])
+    g_emb[...] = d_emb
+    lines = [gain_a, shift_a, gain_b, shift_b, gain_c, shift_c, jnp.zeros((2, width), f32)]
+    g_norms[...] = jnp.concatenate(lines, axis=0)
+    low = d_emb.astype(bf16)
+
+    @pl.loop(0, given.shape[0] // span)
+    def _(k):
+        place = lax.broadcasted_iota(jnp.int32, (span, span), 0) + k * span
+        place = jnp.where(place == slot[...], 1.0, 0.0).astype(bf16)
+        given[pl.ds(pl.multiple_of(k * span, span), span)] = product(place, low).astype(bf16)
+
+
+def backward(lengths, picks, slot, places, weights, saved, grad_rows):
     w_qkv, w_out, w_up, w_down, norms = weights
-    norms = norms.astype(jnp.float32)
-    (
-        embedded,
-        first_low,
-        packed,
-        top,
-        total,
-        context,
-        joined,
-        second_low,
-        hidden_pre,
-        active,
-        summed,
-    ) = saved
-    width = w_out.shape[1]
-    grad_summed, gain_c, shift_c = norm_back(summed, norms[:, 4], norms[:, 5], grad_final)
-    grad_ffn = grad_summed.astype(jnp.bfloat16)
-    g_down = weight_grad(active, grad_ffn)
-    _, gelu_pull = jax.vjp(partial(jax.nn.gelu, approximate=False), hidden_pre)
-    grad_up = gelu_pull(project_back(grad_ffn, w_down))[0].astype(jnp.bfloat16)
-    g_up = weight_grad(second_low, grad_up)
-    grad_second = grad_summed + project_back(grad_up, w_up)
-    grad_joined, gain_b, shift_b = norm_back(joined, norms[:, 2], norms[:, 3], grad_second)
-    grad_attn = grad_joined.astype(jnp.bfloat16)
-    g_out = weight_grad(context, grad_attn)
-    grad_context = project_back(grad_attn, w_out).astype(jnp.bfloat16)
-    query, keyed, valued = split_heads(packed, width)
-    scores = masked_scores(query, keyed, lengths)
-    probs = jnp.exp(scores - top) / total
-    grad_heads = grad_context.reshape(query.shape)
-    grad_valued = jnp.einsum(
-        "bhqk,bqhd->bkhd",
-        probs.astype(jnp.bfloat16),
-        grad_heads,
-        preferred_element_type=jnp.float32,
-    )
-    grad_probs = jnp.einsum(
-        "bqhd,bkhd->bhqk", grad_heads, valued, preferred_element_type=jnp.float32
-    )
-    grad_scores = (probs * (grad_probs - jnp.sum(probs * grad_probs, -1, keepdims=True))).astype(
-        jnp.bfloat16
-    )
-    grad_query = jnp.einsum(
-        "bhqk,bkhd->bqhd", grad_scores, keyed, preferred_element_type=jnp.float32
-    ) * HD ** (-0.5)
-    grad_keyed = jnp.einsum(
-        "bhqk,bqhd->bkhd", grad_scores, query, preferred_element_type=jnp.float32
-    ) * HD ** (-0.5)
-    grad_packed = jnp.concatenate(
-        [piece.reshape(first_low.shape) for piece in (grad_query, grad_keyed, grad_valued)], -1
-    )
-    grad_packed = grad_packed.astype(jnp.bfloat16)
-    g_qkv = weight_grad(first_low, grad_packed)
-    grad_first = grad_joined + project_back(grad_packed, w_qkv)
-    grad_embedded, gain_a, shift_a = norm_back(embedded, norms[:, 0], norms[:, 1], grad_first)
-    g_positions = jnp.sum(grad_embedded, 0)
-    g_norms = jnp.stack([gain_a, shift_a, gain_b, shift_b, gain_c, shift_c], -1)
-    return (grad_embedded, g_positions, g_qkv, g_out, g_up, g_down, g_norms)
+    span, width = saved[0].shape[1:]
+    f32, bf16 = jnp.float32, jnp.bfloat16
+    return pl.pallas_call(
+        backward_kernel,
+        out_shape=[
+            jax.ShapeDtypeStruct(w_qkv.shape, bf16),
+            jax.ShapeDtypeStruct(w_out.shape, bf16),
+            jax.ShapeDtypeStruct(w_up.shape, bf16),
+            jax.ShapeDtypeStruct(w_down.shape, bf16),
+            jax.ShapeDtypeStruct((span, width), f32),
+            jax.ShapeDtypeStruct((8, width), f32),
+            jax.ShapeDtypeStruct((places, width), bf16),
+        ],
+        in_specs=[pl.BlockSpec(memory_space=pltpu.SMEM)] + [VMEM] * 17,
+        out_specs=[VMEM] * 7,
+        scratch_shapes=[
+            pltpu.VMEM((span, 3 * width), bf16),
+            pltpu.VMEM((span, width), bf16),
+            pltpu.VMEM((span, width), f32),
+        ],
+        compiler_params=pltpu.CompilerParams(vmem_limit_bytes=32 * 2**20),
+    )(
+        lengths[None],
+        picks,
+        slot[None],
+        grad_rows,
+        *[value[0] for value in saved],
+        norms.astype(f32).T,
+        w_qkv,
+        w_out,
+        w_up,
+        w_down,
+    )
 
 
 def per_device(
@@ -1030,20 +1155,23 @@
     t_owner, t_first, t_rank = slots(group_ids.reshape(-1), vocab_own)
     s_owners, s_firsts, s_ranks = jax.vmap(lambda one: slots(one, vocab_own))(group_ids)
     my_group = lax.axis_index("grp")
-    s_owner, s_first, s_rank = (
-        lax.dynamic_index_in_dim(v, my_group, 0, keepdims=False)
-        for v in (s_owners, s_firsts, s_ranks)
+    s_owner, s_rank = (
+        lax.dynamic_index_in_dim(v, my_group, 0, keepdims=False) for v in (s_owners, s_ranks)
     )
     most = jnp.maximum(jnp.max(t_rank) // T_ROOM, jnp.max(s_ranks) // S_ROOM) + 1
     t_local = group_ids.reshape(-1) - t_owner * vocab_own
-    s_local = ids[0] - s_owner * vocab_own
+    s_locals = group_ids - s_owners * vocab_own
 
     def asked(turn):
         t_slot = slot_in_round(t_owner, t_rank, T_ROOM, turn)
         s_slot = slot_in_round(s_owner, s_rank, S_ROOM, turn)
         t_ask = wanted_rows(t_slot, t_first, t_local, fsdp * T_ROOM).reshape(fsdp, T_ROOM)
-        s_ask = wanted_rows(s_slot, s_first, s_local, fsdp * S_ROOM).reshape(fsdp, S_ROOM)
-        return t_slot, s_slot, t_ask, s_ask
+        s_asks = jax.vmap(partial(wanted_rows, places=fsdp * S_APART))(
+            slot_in_round(s_owners, s_ranks, S_ROOM, turn, S_APART), s_firsts, s_locals
+        ).reshape(-1, fsdp, S_APART)
+        s_ask = lax.dynamic_index_in_dim(s_asks, my_group, 0, keepdims=False)[:, :S_ROOM]
+        s_asks = jnp.moveaxis(s_asks, 0, 1).reshape(fsdp, -1)
+        return t_slot, s_slot, t_ask, s_ask, s_asks
 
     def answer(t_want, s_want):
         t_sent = product(one_hot(t_want.reshape(-1), vocab_own), t_table[0]).astype(bf16)
@@ -1065,17 +1193,18 @@
         return lax.all_to_all(value, FSDP, split_axis=0, concat_axis=0, tiled=True)
 
     def ask_again(turn):
-        t_slot, s_slot, t_ask, s_ask = asked(turn)
-        wants = swap(jnp.concatenate([t_ask, s_ask], axis=1))
-        return t_slot, s_slot, wants[:, :T_ROOM], wants[:, T_ROOM:]
+        t_slot, s_slot, t_ask, s_ask, s_asks = asked(turn)
+        wants = swap(jnp.concatenate([t_ask, s_ask, s_asks], axis=1))
+        both = T_ROOM + S_ROOM
+        return t_slot, s_slot, wants[:, :T_ROOM], wants[:, T_ROOM:both], wants[:, both:]
 
     def more_rows(state):
         turn, t_emb, s_emb = state
-        t_slot, s_slot, t_want, s_want = ask_again(turn)
+        t_slot, s_slot, t_want, s_want, _ = ask_again(turn)
         t_more, s_more = placed(swap(answer(t_want, s_want)), t_slot, s_slot)
         return turn + 1, t_emb + t_more.astype(bf16), s_emb + s_more.astype(bf16)
 
-    t_slot, s_slot, t_ask, s_ask = asked(0)
+    t_slot, s_slot, t_ask, s_ask, s_asks = asked(0)
     line = jnp.concatenate(
         [t_ask, s_ask, jnp.broadcast_to(most, (fsdp, 128 - T_ROOM - S_ROOM))], axis=1
     )
@@ -1083,10 +1212,11 @@
         line,
         jnp.broadcast_to(jnp.concatenate([picks, labels], axis=1), (fsdp, 2 * picked)),
         jnp.broadcast_to(lengths[:, None], (fsdp, 128)),
+        s_asks,
     ]
-    notes = jnp.stack(lines + [jnp.zeros((fsdp, 128), jnp.int32)] * 5, axis=1)
+    notes = jnp.stack(lines + [jnp.zeros((fsdp, 128), jnp.int32)] * 4, axis=1)
     notes, got = route(notes, t_table[0], own_table, 1)
-    s_want = notes[:, 0, T_ROOM : T_ROOM + S_ROOM]
+    wants = notes[:, 3]
     rounds = jnp.max(notes[:, 0, T_ROOM + S_ROOM])
     plane_picks, plane_labels = notes[:, 1, :picked], notes[:, 1, picked : 2 * picked]
     plane_lengths = notes[:, 2, 0]
@@ -1174,41 +1304,46 @@
     chip = lax.axis_index(("y", "x"))
     chip_counted = lax.dynamic_index_in_dim(plane_counted, chip, 0, keepdims=False)
     shift, own_loss = blend(stats, chip_counted, 3)
-    head_grad, grad_rows, crossed = head_grads(logits, z, shift, h, own_table)
+    head_grad, head_low, grad_rows, crossed = head_grads(logits, z, shift, h, own_table)
     count_local = jnp.sum((picks < lengths[:, None]).astype(f32))
     loss_local = jnp.sum(own_loss) - jnp.sum(crossed)
-    grad_rows = sum_and_scatter([grad_rows.reshape(fsdp, picked, width)], width, f32, 5)
-
-    grad_final = jnp.zeros(final.shape, f32).at[0, picks[0]].add(grad_rows)
-    terms = backward(lengths, student, saved, grad_final)
-    grad_embedded = terms[0]
-    low_embedded = grad_embedded[0].astype(bf16)
-
-    def given(s_slot):
-        rows = product(one_hot(s_slot, fsdp * S_ROOM).T, low_embedded).astype(bf16)
-        return folded(rows.reshape(fsdp, S_ROOM, width))
-
-    def taken_in(got, s_want):
-        rows = unfolded(got).reshape(-1, width)
-        return product(one_hot(s_want.reshape(-1), vocab_own).T, rows)
+    grad_rows, head_grad = sum_and_scatter(
+        [grad_rows.reshape(fsdp, picked, width)], width, f32, "head", [head_grad, head_low], 5
+    )
+
+    g_slot = slot_in_round(s_owner, s_rank, S_ROOM, 0, S_APART)
+    g_qkv, g_out, g_up, g_down, g_pos, g_norms, given_rows = backward(
+        lengths, picks, g_slot, fsdp * S_APART, student, saved, grad_rows
+    )
+    low_embedded = g_pos.astype(bf16)
+
+    def given(turn):
+        slot = slot_in_round(s_owner, s_rank, S_ROOM, turn, S_APART)
+        hot = (jnp.arange(fsdp * S_APART)[:, None] == slot[None, :]).astype(bf16)
+        return product(hot, low_embedded).astype(bf16)
 
     def more_grads(state):
         turn, total = state
-        _, s_slot, _, s_want = ask_again(turn)
-        return turn + 1, total + taken_in(swap(given(s_slot)), s_want)
-
-    g_lookup = taken_in(exchange(given(s_slot), 6), s_want)
-    _, g_table = lax.while_loop(
-        lambda state: state[0] < rounds, more_grads, (jnp.int32(1), head_grad + g_lookup)
-    )
-    g_pos, g_qkv, g_out, g_up, g_down, g_norms = terms[1:]
+        wants = ask_again(turn)[4]
+        rows = jnp.stack(jnp.split(given(turn), 4, axis=1))
+        rows = lax.all_to_all(rows, "grp", split_axis=0, concat_axis=0, tiled=True)
+        rows = swap(jnp.moveaxis(rows.reshape(4, fsdp, S_APART, -1), 0, 1))
+        hot = one_hot(wants.reshape(-1), vocab_own).T
+        return turn + 1, total + product(hot, rows.reshape(-1, rows.shape[3]))
+
+    _, head_grad = lax.while_loop(
+        lambda state: state[0] < rounds, more_grads, (jnp.int32(1), head_grad)
+    )
+    g_norms = g_norms[:6].T
     parts = pieces(fsdp, g_qkv, g_out, g_up, g_down, g_pos, g_norms)
-    rest = sum_and_scatter(parts, width, bf16, 7)
+    rest, got = sum_and_scatter(parts, width, bf16, "rows", [given_rows], 7)
     row = jnp.arange(8)[:, None]
     column_of = jnp.arange(128)[None, :]
     told = jnp.where((row == 0) & (column_of == 0), loss_local, 0.0)
     told += jnp.where((row == 1) & (column_of == 0), count_local, 0.0)
-    table_sum, rest_sum, seen = sum_of_groups(g_table.astype(bf16), rest, told, 8)
+    table_sum, rest_sum, seen = sum_of_groups(
+        head_grad, wants.reshape(4, -1), got.reshape(4, -1, got.shape[3]), rest, told, 8
+    )
     seen = seen.sum(0)
     squares, loss_sum, count = jnp.sum(seen[:8]), seen[8, 0], seen[9, 0]
     at_norms = rest_sum.shape[0] - 8

time: 471 us -> 453 us (0.962)
  matrix products: 33.4 us -> 14.2 us
  local copies, waits for them, and re-layouts: 32.9 us -> 38.6 us
    dot_general x12 -> x0, matrix products: 16.6 us -> none  [the longest x4 7.42 us: weight_grad(): jnp.einsum('blk,bln->kn', left, grad, preferred_element_type=jnp.float32)]
    unnamed x112 -> x116, local copies, waits for them, and re-layouts: 10.8 us -> 17.9 us
  transfers between devices with their start and end apart: 3 -> 3, of which waited for: 1 -> 0; matrix products, arithmetic and copies ran while one was open for 11% -> 12% of each run, Pallas kernels for 33% -> 34%
where the time goes in v4:
time: 453 us; the launch traced here: 446 us
  Pallas kernels  338 us (75%)
  local copies, waits for them, and re-layouts  38.6 us (9%)
  between operations  24.7 us (5%)
  other arithmetic  22.9 us (5%)
  matrix products  14.2 us (3%)
  loops' own time  6.92 us (2%)
    pallas_call x2, Pallas kernels, sum_and_scatter(): pl.pallas_call(partial(scatter_sum_kernel, plan, side), out_shape=[jax.Sh...  67.1 us
    pallas_call x1, Pallas kernels, route(): pl.pallas_call(route_kernel, out_shape=[jax.ShapeDtypeStruct(notes.shape,...  57.9 us
    pallas_call x1, Pallas kernels, teacher_rows(): pl.pallas_call(teacher_kernel, grid=(count,), out_shape=jax.ShapeDtypeStr...  40 us
    pallas_call x2, Pallas kernels, vocabulary_logits(): pl.pallas_call(logits_kernel, grid=(count, devices // block), out_shape=[...  36.3 us
    pallas_call x1, Pallas kernels, gather_plane(): pl.pallas_call(gather_kernel, out_shape=jax.ShapeDtypeStruct((16, 2, rows...  32.3 us
    pallas_call x1, Pallas kernels, sum_of_groups(): pl.pallas_call(group_sum_kernel, out_shape=[jax.ShapeDtypeStruct((head.sh...  29.2 us
    pallas_call x1, Pallas kernels, blend(): pl.pallas_call(blend_kernel, out_shape=[jax.ShapeDtypeStruct((16, 8, 128)...  19.3 us
    unnamed x116, local copies, waits for them, and re-layouts  17.9 us
  transfers between devices with their start and end apart: 3, of which 0 were waited for; matrix products, arithmetic and copies ran while one was open for 12% of the time, Pallas kernels for 34%

profile of v4, /device:TPU:1, one launch (start us, length us, event | category | flops | bytes accessed | tf_op | source)
XLA Modules:
  0.0 446.2 jit_solution(933498172651609181)
XLA Ops:
  7.3 0.7 all-gather.5.cloned.1.call-update
  8.0 0.7 convert.27
  8.9 0.7 convert_bitcast_fusion.3
  9.7 0.9 convert_bitcast_fusion.1
  10.6 0.8 constant_dynamic-update-slice_fusion.5
  11.3 0.9 convert_bitcast_fusion
  12.3 0.7 copy-done.55
  14.5 7.2 %shard_map.487 = s32[4,8,128]{2,1,0:T(8,128)} custom-call(s32[4,8,128]{2,1,0:T(8,128)} %broadcast_in_dim.270.source), custom_call_target="tpu_custom_call" | custom-call | tf_op jit(solution)/shard_map/pallas_call | solution.py:164
  21.7 0.7 slice_bitcast_fusion.6
  22.9 1.2 convert_reduce_fusion
  30.0 0.7 slice_reduce_fusion.11
  31.4 0.8 select_reduce_fusion.4
  33.1 57.9 %shard_map.488 = (s32[32,8,128]{2,1,0:T(8,128)S(1)}, bf16[32,48,1024]{2,1,0:T(8,128)(2,1)S(1)}) custom-call(s32[32,8,128]{2,1,0:T(8,128)S(1)} %stack.46.notes, bf16[960,768]{1,0:T(8,128)(2,1)} %bitcast.245, bf16[960,512]{1,0:T(8,128)(2,1)S(1)} %convert_element_type.167.s_table.table), custom_call_target="tpu_custom_call" | custom-call | tf_op jit(solution)/shard_map/pallas_call | solution.py:127
  91.0 1.7 copy-done.6
  92.7 1.2 slice_reduce_fusion.7
  94.0 1.0 copy.125.slot
  95.0 0.8 copy.126.picks
  96.4 1.2 broadcast_in_dim.278
  97.6 0.7 broadcast_in_dim.279
  98.4 6.2 %while.28 = (s32[]{:T(128)}, bf16[1024,768]{1,0:T(8,128)(2,1)}, bf16[256,512]{1,0:T(8,128)(2,1)}, s32[]{:T(128)}, s32[1024]{0:T(1024)S(1)}, /*index=5*/s32[1024]...) while((s32[]{:T(128)}, bf16[1024,768]{1,0:T(8,128)(2,1)}, ...), condition=%wide.region_12.13_spmd, body=%wide.region_9.12_spmd.sunk | while | flops 5663440896 | bytes 60638628 | solution.py:1224
  104.6 0.9 copy-done.37
  105.5 40.0 %shard_map.489.source = bf16[4,64,768]{2,1,0:T(8,128)(2,1)} custom-call(s32[1,4]{1,0:T(1,128)} %bitcast.292, s32[4,256,1]{2,1,0:T(8,128)} %copy.125.slot, s32[4,64,1]{2,1,0:T(8,128)} %copy.126.picks, bf16[1536,1024]{1,0:T(8,128)(2,1)} %bitcast.223, bf16[4,256,768]{2,1,0:T(8,128)(2,1)} %bitcast.244, bf16[256,768]{1,0:T(8,128)(2,1)} %bitcast.268, ...), custom_call_target="tpu_custom_call" | custom-call | tf_op jit(solution)/shard_map/pallas_call | solution.py:341
  145.6 8.4 %shard_map.490 = bf16[4,64,768]{2,1,0:T(8,128)(2,1)} custom-call(bf16[4,64,768]{2,1,0:T(8,128)(2,1)} %shard_map.489.source), custom_call_target="tpu_custom_call" | custom-call | tf_op jit(solution)/shard_map/pallas_call | solution.py:164
  154.1 0.7 sub.214.labels
  156.4 1.1 convert_bitcast_fusion.5.head
  157.5 1.2 fusion.60
  158.8 0.9 fusion.44
  160.0 1.5 fusion.66
  161.7 0.9 slice_reduce_fusion.1
  162.7 4.1 fusion.59
  167.9 0.9 copy.128
  168.9 0.9 copy.130
  169.7 3.1 fusion.67
  172.8 2.0 convolution_convert_fusion.3
  174.8 0.8 copy.134.context
  175.6 1.8 slice.253
  180.2 5.9 %fusion.22 = (bf16[256,2048]{1,0:T(8,128)(2,1)S(1)}, f32[256,2048]{1,0:T(8,128)}) fusion(bf16[256,512]{1,0:T(8,128)(2,1)S(1)} %fusion.38.second_low, bf16[512,2048]{1,0:T(8,128)(2,1)S(1)} %pad_maximum_fusion.2.w_up), kind=kOutput, calls=%fused_computation.77 | convolution fusion | flops 570949632 | bytes 5505024 | tf_op jit(solution)/shard_map/blk,kn->bln/dot_general | solution.py:894
  186.0 0.8 fusion.69
  188.0 0.7 gather_fusion
  188.7 0.7 select_convert_fusion.source
  189.4 32.3 %shard_map.492 = bf16[16,2,64,512]{3,2,1,0:T(8,128)(2,1)} custom-call(bf16[64,512]{1,0:T(8,128)(2,1)} %select_convert_fusion.source), custom_call_target="tpu_custom_call" | custom-call | tf_op jit(solution)/shard_map/pallas_call | solution.py:198
  221.7 7.5 %shard_map.493 = (f32[1,960,2048]{2,1,0:T(8,128)}, f32[1,4,2048]{2,1,0:T(4,128)}) custom-call(s32[1,2048]{1,0:T(1,128)} %sub.214.labels, bf16[32,1,64,512]{3,2,1,0:T(8,128)(2,1)} %bitcast.219, bf16[1,960,512]{2,1,0:T(8,128)(2,1)} %convert_bitcast_fusion.5.head), custom_call_target="tpu_custom_call" | custom-call | tf_op jit(solution)/shard_map/pallas_call | solution.py:420
  229.2 1.2 pad_maximum_fusion.3.w_qkv
  230.5 28.7 %shard_map.491 = (f32[4,960,2048]{2,1,0:T(8,128)}, f32[4,4,2048]{2,1,0:T(4,128)}) custom-call(s32[1,2048]{1,0:T(1,128)} %sub.214.labels, bf16[32,4,64,768]{3,2,1,0:T(8,128)(2,1)} %bitcast.241, bf16[4,960,768]{2,1,0:T(8,128)(2,1)} %all-gather.5.cloned.1.call-done.head), custom_call_target="tpu_custom_call" | custom-call | tf_op jit(solution)/shard_map/pallas_call | solution.py:420
  259.2 1.6 pad_maximum_fusion.5.stats
  260.8 19.3 %shard_map.494 = (f32[16,8,128]{2,1,0:T(8,128)}, f32[1,128]{1,0:T(1,128)}) custom-call(f32[5,4,2048]{2,1,0:T(4,128)} %pad_maximum_fusion.5.stats, f32[1,128]{1,0:T(1,128)} %fusion.50.counted_ref), custom_call_target="tpu_custom_call" | custom-call | tf_op jit(solution)/shard_map/pallas_call | solution.py:506
  280.2 0.8 copy-done.31
  281.0 17.8 %shard_map.495 = (f32[960,512]{1,0:T(8,128)S(1)}, bf16[960,512]{1,0:T(8,128)(2,1)S(1)}, bf16[2048,512]{1,0:T(8,128)(2,1)S(1)}, f32[1,2048]{1,0:T(1,128)S(1)}) custom-call(f32[4,960,2048]{2,1,0:T(8,128)} %get-tuple-element.582.logits, f32[1,960,2048]{2,1,0:T(8,128)} %get-tuple-element.585.z, f32[16,8,128]{2,1,0:T(8,128)S(1)} %copy-done.31, ...), custom_call_target="tpu_custom_call" | custom-call | tf_op jit(solution)/shard_map/pallas_call | solution.py:566
  298.9 18.4 %shard_map.496 = (f32[64,512]{1,0:T(8,128)S(1)}, f32[960,128]{1,0:T(8,128)}) custom-call(bf16[16,2,64,512]{3,2,1,0:T(8,128)(2,1)S(1)} %bitcast.227, f32[960,512]{1,0:T(8,128)S(1)} %get-tuple-element.590.refs_1_, bf16[960,512]{1,0:T(8,128)(2,1)S(1)} %get-tuple-element.591.refs_2_), custom_call_target="tpu_custom_call" | custom-call | tf_op jit(solution)/shard_map/pallas_call | solution.py:740
  317.4 14.2 %shard_map.497 = (bf16[512,1536]{1,0:T(8,128)(2,1)S(1)}, bf16[512,512]{1,0:T(8,128)(2,1)S(1)}, bf16[512,2048]{1,0:T(8,128)(2,1)S(1)}, bf16[2048,512]{1,0:T(8,128...) custom-call(s32[1,1]{1,0:T(1,128)} %bitcast.218.lengths, ...), custom_call_target="tpu_custom_call" | custom-call | tf_op jit(solution)/shard_map/pallas_call | solution.py:1072
  331.6 1.3 copy-done.14
  332.9 1.0 copy-done.18
  333.9 0.8 copy-done.28
  334.7 0.8 convert_element_type.190
  339.2 0.7 select_add_fusion.facts
  339.9 1.6 copy-done.15
  341.5 1.4 copy-done.17
  342.9 1.2 copy-done.19
  344.2 48.6 %shard_map.498 = (bf16[208,512]{1,0:T(8,128)(2,1)S(1)}, bf16[32,4,32,128]{3,2,1,0:T(8,128)(2,1)S(1)}) custom-call(bf16[16,2,16,1536]{3,2,1,0:T(8,128)(2,1)S(1)} %bitcast.231, bf16[16,2,16,512]{3,2,1,0:T(8,128)(2,1)S(1)} %bitcast.233, bf16[16,2,16,2048]{3,2,1,0:T(8,128)(2,1)S(1)} %bitcast.228, bf16[16,2,64,512]{3,2,1,0:T(8,128)(2,1)S(1)} %bitcast.229, ...), custom_call_target="tpu_custom_call" | custom-call | tf_op jit(solution)/shard_map/pallas_call | solution.py:740
  392.8 1.0 copy-done.20
  393.8 0.7 while.29
  395.0 29.2 %shard_map.499 = (bf16[960,512]{1,0:T(8,128)(2,1)S(1)}, bf16[208,512]{1,0:T(8,128)(2,1)S(1)}, f32[32,16,128]{2,1,0:T(8,128)S(1)}) custom-call(f32[960,128]{1,0:T(8,128)} %get-tuple-element.595.head, s32[4,1024]{1,0:T(4,128)S(1)} %reshape_squeeze.2.wants, bf16[4,1024,128]{2,1,0:T(8,128)(2,1)S(1)} %bitcast.232, bf16[208,512]{1,0:T(8,128)(2,1)S(1)} %get-tuple-element.603.rest, ...), custom_call_target="tpu_custom_call" | custom-call | tf_op jit(solution)/shard_map/pallas_call | solution.py:828
  424.2 0.9 copy-done.27
  429.9 8.4 %shard_map.500 = (f32[960,512]{1,0:T(8,128)}, f32[8,512]{1,0:T(8,128)}, f32[16,1536]{1,0:T(8,128)}, f32[16,512]{1,0:T(8,128)}, f32[16,2048]{1,0:T(8,128)}, /*ind...) custom-call(f32[1,1]{1,0:T(1,128)} %bitcast.85.factor_ref, ...), custom_call_target="tpu_custom_call" | custom-call | tf_op jit(solution)/shard_map/pallas_call | solution.py:252
  (204 shorter events, 17.9 us)
Async XLA Ops:
  7.2 5.1 %copy-start.48 = (f32[64,512]{1,0:T(8,128)S(1)}, f32[64,512]{1,0:T(8,128)}, u32[]{:S(2)}) copy-start(f32[64,512]{1,0:T(8,128)} %refs_5_.1) | copy-start | bytes 393220
  7.2 6.6 %copy-start.32 = (s32[1,64]{1,0:T(1,128)S(1)}, s32[1,64]{1,0:T(1,128)}, u32[]{:S(2)}) copy-start(s32[1,64]{1,0:T(1,128)} %picks.1) | copy-start | bytes 772
  7.2 6.6 %copy-start.58 = (s32[1,256]{1,0:T(1,128)S(1)}, s32[1,256]{1,0:T(1,128)}, u32[]{:S(2)}) copy-start(s32[1,256]{1,0:T(1,128)} %param.36) | copy-start | bytes 3076
  7.2 25.2 %copy-start.59 = (s32[1,64]{1,0:T(1,128)S(1)}, s32[1,64]{1,0:T(1,128)}, u32[]{:S(2)}) copy-start(s32[1,64]{1,0:T(1,128)} %param.39) | copy-start | bytes 772
  7.2 25.4 %copy-start.33 = (f32[960,512]{1,0:T(8,128)S(1)}, f32[960,512]{1,0:T(8,128)}, u32[]{:S(2)}) copy-start(f32[960,512]{1,0:T(8,128)} %refs_0_.1) | copy-start | bytes 5898244
  7.2 138.3 %all-gather.5.cloned.1.call-start = ((), (), s32[]{:S(2)}) async-start(), calls=%async_computation.5 | async-start | bytes 7372800 | tf_op jit(solution)/shard_map/all_gather | solution.py:1272
  8.0 150.8 %all-gather.7.cloned.1.call-start = ((), (), s32[]{:S(2)}) async-start(), calls=%async_computation.6 | async-start | bytes 7028736 | tf_op jit(solution)/shard_map/all_gather | solution.py:1269
  12.3 0.7 copy-start.55
  13.1 217.4 %all-gather.9.cloned.1.call-start = ((), (), s32[]{:S(2)}) async-start(), calls=%async_computation.7 | async-start | bytes 12976128 | tf_op jit(solution)/shard_map/all_gather | solution.py:1290
  32.8 63.0 %copy-start.57 = (bf16[1,768,6]{1,2,0:T(8,128)(2,1)S(1)}, bf16[1,768,6]{1,2,0:T(8,128)(2,1)}, u32[]{:S(2)}) copy-start(bf16[1,768,6]{1,2,0:T(8,128)(2,1)} %param.67) | copy-start | bytes 27652
  91.0 1.7 copy-start.6
  104.6 0.9 copy-start.37
  105.5 50.9 %copy-start.34 = (f32[960,512]{1,0:T(8,128)S(1)}, f32[960,512]{1,0:T(8,128)}, u32[]{:S(2)}) copy-start(f32[960,512]{1,0:T(8,128)} %refs_0_.1) | copy-start | bytes 5898244
  157.5 2.5 copy-start.54
  166.8 0.8 copy-start.40
  166.8 1.0 copy-start.42
  166.8 10.7 %copy-start.7 = (bf16[32,16,512]{2,1,0:T(8,128)(2,1)}, bf16[32,16,512]{2,1,0:T(8,128)(2,1)S(1)}, u32[]{:S(2)}) copy-start(bf16[32,16,512]{2,1,0:T(8,128)(2,1)S(1)} %get-tuple-element.734) | copy-start | bytes 1572868
  167.8 5.1 %copy-start.11 = (bf16[256,1536]{1,0:T(8,128)(2,1)}, bf16[256,1536]{1,0:T(8,128)(2,1)S(1)}, u32[]{:S(2)}) copy-start(bf16[256,1536]{1,0:T(8,128)(2,1)S(1)} %convolution_convert_fusion.2.packed) | copy-start | bytes 2359300
  168.9 4.0 copy-start.51
  177.5 8.6 %copy-start.1 = (bf16[32,64,512]{2,1,0:T(8,128)(2,1)}, bf16[32,64,512]{2,1,0:T(8,128)(2,1)S(1)}, u32[]{:S(2)}) copy-start(bf16[32,64,512]{2,1,0:T(8,128)(2,1)S(1)} %slice.253) | copy-start | bytes 6291460
  177.5 1.4 copy-start.44
  177.5 1.9 copy-start.45
  177.5 2.2 copy-start.46
  177.5 2.3 copy-start.47
  178.3 1.8 copy-start.24
  180.1 5.9 %copy-start.3 = (bf16[512,2048]{1,0:T(8,128)(2,1)}, bf16[512,2048]{1,0:T(8,128)(2,1)S(1)}, u32[]{:S(2)}) copy-start(bf16[512,2048]{1,0:T(8,128)(2,1)S(1)} %pad_maximum_fusion.2.w_up) | copy-start | bytes 6291460
  186.0 1.0 copy-start.22
  187.0 0.8 copy-start.9
  189.4 39.8 %copy-start.41 = (bf16[32,16,512]{2,1,0:T(8,128)(2,1)S(1)}, bf16[32,16,512]{2,1,0:T(8,128)(2,1)}, u32[]{:S(2)}) copy-start(bf16[32,16,512]{2,1,0:T(8,128)(2,1)} %copy-done.40) | copy-start | bytes 1572868
  189.4 39.8 %copy-start.43 = (bf16[32,16,512]{2,1,0:T(8,128)(2,1)S(1)}, bf16[32,16,512]{2,1,0:T(8,128)(2,1)}, u32[]{:S(2)}) copy-start(bf16[32,16,512]{2,1,0:T(8,128)(2,1)} %copy-done.42) | copy-start | bytes 1572868
  230.5 28.8 %copy-start.56 = (f32[1,4,2048]{2,1,0:T(4,128)S(1)}, f32[1,4,2048]{2,1,0:T(4,128)}, u32[]{:S(2)}) copy-start(f32[1,4,2048]{2,1,0:T(4,128)} %get-tuple-element.587) | copy-start | bytes 98308
  230.5 49.7 %copy-start = (bf16[16,2,64,512]{3,2,1,0:T(8,128)(2,1)S(1)}, bf16[16,2,64,512]{3,2,1,0:T(8,128)(2,1)}, u32[]{:S(2)}) copy-start(bf16[16,2,64,512]{3,2,1,0:T(8,128)(2,1)} %shard_map.492) | copy-start | bytes 6291460
  280.2 0.8 copy-start.31
  281.0 36.3 %copy-start.5 = (bf16[512,1536]{1,0:T(8,128)(2,1)S(1)}, bf16[512,1536]{1,0:T(8,128)(2,1)}, u32[]{:S(2)}) copy-start(bf16[512,1536]{1,0:T(8,128)(2,1)} %pad_maximum_fusion.3.w_qkv) | copy-start | bytes 4718596
  281.0 36.3 %copy-start.10 = (f32[256,512]{1,0:T(8,128)S(1)}, f32[256,512]{1,0:T(8,128)}, u32[]{:S(2)}) copy-start(f32[256,512]{1,0:T(8,128)} %copy-done.9) | copy-start | bytes 1572868
  281.0 36.3 %copy-start.12 = (bf16[256,1536]{1,0:T(8,128)(2,1)S(1)}, bf16[256,1536]{1,0:T(8,128)(2,1)}, u32[]{:S(2)}) copy-start(bf16[256,1536]{1,0:T(8,128)(2,1)} %copy-done.11) | copy-start | bytes 2359300
  281.0 36.3 %copy-start.13 = (f32[256,2048]{1,0:T(8,128)S(1)}, f32[256,2048]{1,0:T(8,128)}, u32[]{:S(2)}) copy-start(f32[256,2048]{1,0:T(8,128)} %get-tuple-element.764.hidden_pre) | copy-start | bytes 6291460
  281.0 36.3 %copy-start.23 = (bf16[256,2048]{1,0:T(8,128)(2,1)S(1)}, bf16[256,2048]{1,0:T(8,128)(2,1)}, u32[]{:S(2)}) copy-start(bf16[256,2048]{1,0:T(8,128)(2,1)} %copy-done.22) | copy-start | bytes 3145732
  281.0 36.3 %copy-start.26 = (bf16[256,512]{1,0:T(8,128)(2,1)S(1)}, bf16[256,512]{1,0:T(8,128)(2,1)}, u32[]{:S(2)}) copy-start(bf16[256,512]{1,0:T(8,128)(2,1)} %copy.134.context) | copy-start | bytes 786436
  298.8 18.5 %copy-start.2 = (bf16[32,64,512]{2,1,0:T(8,128)(2,1)S(1)}, bf16[32,64,512]{2,1,0:T(8,128)(2,1)}, u32[]{:S(2)}) copy-start(bf16[32,64,512]{2,1,0:T(8,128)(2,1)} %copy-done.1) | copy-start | bytes 6291460
  298.8 18.5 %copy-start.4 = (bf16[512,2048]{1,0:T(8,128)(2,1)S(1)}, bf16[512,2048]{1,0:T(8,128)(2,1)}, u32[]{:S(2)}) copy-start(bf16[512,2048]{1,0:T(8,128)(2,1)} %copy-done.3) | copy-start | bytes 6291460
  298.8 18.5 %copy-start.8 = (bf16[32,16,512]{2,1,0:T(8,128)(2,1)S(1)}, bf16[32,16,512]{2,1,0:T(8,128)(2,1)}, u32[]{:S(2)}) copy-start(bf16[32,16,512]{2,1,0:T(8,128)(2,1)} %copy-done.7) | copy-start | bytes 1572868
  298.9 18.5 %copy-start.25 = (bf16[256,512]{1,0:T(8,128)(2,1)S(1)}, bf16[256,512]{1,0:T(8,128)(2,1)}, u32[]{:S(2)}) copy-start(bf16[256,512]{1,0:T(8,128)(2,1)} %copy-done.24) | copy-start | bytes 786436
  331.5 1.4 copy-start.14
  332.9 1.0 copy-start.18
  333.9 0.8 copy-start.28
  334.7 1.2 copy-start.16
  334.7 2.0 copy-start.60
  334.7 5.3 %copy-start.29 = (bf16[512,512]{1,0:T(8,128)(2,1)S(1)}, bf16[512,512]{1,0:T(8,128)(2,1)}, u32[]{:S(2)}) copy-start(bf16[512,512]{1,0:T(8,128)(2,1)} %copy-done.28) | copy-start | bytes 1572868
  339.9 1.6 copy-start.15
  341.5 1.4 copy-start.17
  342.9 1.2 copy-start.19
  392.8 1.0 copy-start.20
  393.8 1.2 copy-start.21
  424.2 1.0 copy-start.27
  425.2 4.7 %copy-start.30 = (bf16[208,512]{1,0:T(8,128)(2,1)}, bf16[208,512]{1,0:T(8,128)(2,1)S(1)}, u32[]{:S(2)}) copy-start(bf16[208,512]{1,0:T(8,128)(2,1)S(1)} %get-tuple-element.608.rest_grad) | copy-start | bytes 638980
Sparse Core Ops, SparseCore 0:
  9.7 65.8 all-gather.4
  77.9 50.7 all-gather.6
  154.1 74.5 all-gather.8

commit v5 on v4

--- a/solution.py
+++ b/solution.py
@@ -210,10 +210,14 @@
     return out.reshape(32 * rows, width)
 
 
-def update_kernel(factor_ref, table_grad, rest_grad, norms_grad, *refs):
+def update_kernel(seen, table_grad, rest_grad, *refs):
     masters, momenta, averages = refs[:7], refs[7:14], refs[14:21]
-    outs = refs[21:]
-    factor = factor_ref[0, 0]
+    loss_sum, count_out, clip_out = refs[21:24]
+    outs = refs[24:]
+    facts = jnp.sum(seen[...], 0)
+    squares, loss, count = [jnp.sum(line) for line in (facts[:8], facts[8:9], facts[9:10])]
+    clip = jnp.sqrt(jnp.full((8, 128), squares)) / count
+    factor = (jnp.minimum(1.0, clip_limit / clip) / count)[0:1, 0:1]
 
     def step(k, grad):
         clipped = grad * factor
@@ -227,6 +231,9 @@
 
     @pl.when(pl.program_id(0) == 0)
     def _():
+        loss_sum[0, 0] = loss
+        count_out[0, 0] = count
+        clip_out[...] = clip
         width = rest_grad.shape[1]
         at = 0
         for k in (2, 3, 4, 5):
@@ -236,34 +243,32 @@
                 blocks.append(rest_grad[at : at + rows].astype(jnp.float32))
                 at += rows
             step(k, blocks[0] if len(blocks) == 1 else jnp.concatenate(blocks, axis=1))
-        step(1, rest_grad[at : at + 16].astype(jnp.float32)[: masters[1].shape[0]])
-        step(6, norms_grad[...])
-
-
-def update(factor, table_grad, rest_grad, norms_grad, masters, momenta, averages):
+        small = rest_grad[at : at + 16].astype(jnp.float32)
+        step(1, small[:8])
+        step(6, small[8 : 8 + masters[6].shape[0], : masters[6].shape[1]])
+
+
+def update(seen, table_grad, rest_grad, masters, momenta, averages):
     steps = 5
     rows, width = table_grad.shape
 
     def whole(shape):
-        return pl.BlockSpec(shape, lambda i: (0, 0))
+        return pl.BlockSpec(shape, lambda i: (0,) * len(shape))
 
     tall = pl.BlockSpec((rows // steps, width), lambda i: (i, 0))
     states = [tall] + [whole(m.shape) for m in masters[1:]]
-    outs = pl.pallas_call(
+    scalar = pl.BlockSpec(memory_space=pltpu.SMEM)
+    one = jax.ShapeDtypeStruct((1, 1), jnp.float32)
+    tile = jax.ShapeDtypeStruct((8, 128), jnp.float32)
+    return pl.pallas_call(
         update_kernel,
         grid=(steps,),
-        out_shape=[jax.ShapeDtypeStruct(m.shape, m.dtype) for m in masters] * 3,
-        in_specs=[
-            pl.BlockSpec(memory_space=pltpu.SMEM),
-            tall,
-            whole(rest_grad.shape),
-            whole(norms_grad.shape),
-        ]
-        + states * 3,
-        out_specs=states * 3,
+        out_shape=[one, one, tile]
+        + [jax.ShapeDtypeStruct(m.shape, m.dtype) for m in masters] * 3,
+        in_specs=[whole(seen.shape), tall, whole(rest_grad.shape)] + states * 3,
+        out_specs=[scalar, scalar, whole(tile.shape)] + states * 3,
         compiler_params=pltpu.CompilerParams(vmem_limit_bytes=WIDE),
-    )(factor.reshape(1, 1), table_grad, rest_grad, norms_grad, *masters, *momenta, *averages)
-    return tuple(outs)
+    )(seen, table_grad, rest_grad, *masters, *momenta, *averages)
 
 
 def normed(value, gain, shift):
@@ -284,8 +289,10 @@
         wide = lax.broadcasted_iota(jnp.int32, (index.shape[0], count), 1)
         return jnp.where(wide == index, 1.0, 0.0).astype(bf16)
 
+    lines = norms[...].astype(f32)
+
     def scale(k):
-        return norms[2 * k : 2 * k + 1], norms[2 * k + 1 : 2 * k + 2]
+        return lines[2 * k : 2 * k + 1], lines[2 * k + 1 : 2 * k + 2]
 
     emb = product(pick(slot[0], got.shape[0]), got[...])
     emb = emb + extra[0].astype(f32) + pos[...].astype(f32)
@@ -493,7 +500,9 @@
     chip = me["y"] * 4 + me["x"]
     shift[chip] = jnp.concatenate(lines, axis=0)
     ours = jnp.where(left, 0, 1) == me["c"]
-    loss[...] = jnp.where(ours, counted * (entropy + student), 0.0)
+    lines = [counted * (entropy + student), counted]
+    lines = [jnp.where(ours, line, 0.0) for line in lines] + [jnp.zeros((6, 128), f32)]
+    loss[...] = jnp.concatenate(lines, axis=0)
     copies = []
     for k in range(1, 16):
         place = moved(me, (7 * k) % 16 // 4, (7 * k) % 4, 0)
@@ -507,7 +516,7 @@
         blend_kernel,
         out_shape=[
             jax.ShapeDtypeStruct((16, 8, 128), jnp.float32),
-            jax.ShapeDtypeStruct((1, 128), jnp.float32),
+            jax.ShapeDtypeStruct((8, 128), jnp.float32),
         ],
         in_specs=[VMEM, VMEM],
         out_specs=[VMEM, VMEM],
@@ -526,6 +535,7 @@
 ):
     f32, bf16 = jnp.float32, jnp.bfloat16
     grad = jnp.zeros(head_grad.shape, f32)
+    cross = jnp.zeros((1, WING), f32)
     for at in range(0, z.shape[2], WING):
         cols = slice(at, at + WING)
         lines = jnp.concatenate([shift[at // 128], shift[at // 128 + 1]], axis=1)
@@ -540,7 +550,7 @@
             student = z[0, rows, cols]
             low[rows, cols] = (counted * (jnp.exp(student - lse) - target)).astype(bf16)
             total += jnp.sum(by_eight(target * student), 0)
-        crossed[:, cols] = counted * jnp.sum(total, 0, keepdims=True)
+        cross += counted * jnp.sum(total, 0, keepdims=True)
         grad_rows[cols] = lax.dot_general(
             low[:, cols], table[...], (((0,), (0,)), ((), ())), preferred_element_type=f32
         ).astype(bf16)
@@ -549,10 +559,12 @@
     @pl.when(pl.program_id(0) == 0)
     def _():
         head_grad[...] = grad
+        crossed[...] = cross
 
     @pl.when(pl.program_id(0) > 0)
     def _():
         head_grad[...] += grad
+        crossed[...] += cross
 
     @pl.when(pl.program_id(0) == pl.num_programs(0) - 1)
     def _():
@@ -570,7 +582,7 @@
             jax.ShapeDtypeStruct((vocab, width), jnp.float32),
             jax.ShapeDtypeStruct((vocab, width), jnp.bfloat16),
             jax.ShapeDtypeStruct((rows, width), jnp.bfloat16),
-            jax.ShapeDtypeStruct((1, rows), jnp.float32),
+            jax.ShapeDtypeStruct((1, WING), jnp.float32),
         ],
         in_specs=[
             pl.BlockSpec((teachers, vocab, wide), lambda j: (0, 0, j)),
@@ -583,7 +595,7 @@
             pl.BlockSpec((vocab, width), lambda j: (0, 0)),
             pl.BlockSpec((vocab, width), lambda j: (0, 0)),
             pl.BlockSpec((wide, width), lambda j: (j, 0)),
-            pl.BlockSpec((1, wide), lambda j: (0, j)),
+            pl.BlockSpec((1, WING), lambda j: (0, 0)),
         ],
         scratch_shapes=[pltpu.VMEM((vocab, wide), jnp.bfloat16)],
         compiler_params=pltpu.CompilerParams(vmem_limit_bytes=40 * 2**20),
@@ -728,7 +740,7 @@
     cut = width // 2
     rest = width - cut
     bf16 = jnp.bfloat16
-    room = (12 if side == "head" else 28) * 2**20
+    room = (12 if side == "head" else 36) * 2**20
     tall = sided[0].shape[0]
     if side == "head":
         side_out = jax.ShapeDtypeStruct((tall, 128), jnp.float32)
@@ -740,7 +752,7 @@
     return pl.pallas_call(
         partial(scatter_sum_kernel, plan, side),
         out_shape=[jax.ShapeDtypeStruct((rows, width), dtype), side_out],
-        in_specs=[ANY] * (len(parts) + len(sided)),
+        in_specs=[VMEM if side == "rows" else ANY] * (len(parts) + len(sided)),
         out_specs=[VMEM, VMEM],
         scratch_shapes=side_scratch
         + [
@@ -764,7 +776,7 @@
 
 
 def group_sum_kernel(
-    head, wants, given, rest, facts, table_out, rest_out, seen, total, rest_in, told, sends, arrivals
+    head, wants, given, rest, facts, crossed, table_out, rest_out, seen, total, rest_in, told, sends, arrivals
 ):
     f32, bf16 = jnp.float32, jnp.bfloat16
     me = here()
@@ -803,7 +815,9 @@
     summed = summed.astype(f32)
     squares += jnp.sum(by_eight(summed * summed), 0)
     told[group, 0:8] = squares
-    told[group, 8:16] = facts[...]
+    first = lax.broadcasted_iota(jnp.int32, (8, 128), 0) == 0
+    cross = crossed[:, :128] + crossed[:, 128:]
+    told[group, 8:16] = facts[...] - jnp.where(first, cross, 0.0)
     copies = []
     for d in range(3):
         copies.append(remote(told.at[group], told.at[group], sends, arrivals, 6 + d, groups[d]))
@@ -822,7 +836,7 @@
         copy.wait()
 
 
-def sum_of_groups(head, wants, given, rest, facts, collective):
+def sum_of_groups(head, wants, given, rest, facts, crossed, collective):
     count = 12 + len(AROUND)
     bf16 = jnp.bfloat16
     return pl.pallas_call(
@@ -832,7 +846,7 @@
             jax.ShapeDtypeStruct(rest.shape, rest.dtype),
             jax.ShapeDtypeStruct((32, 16, 128), jnp.float32),
         ],
-        in_specs=[VMEM] * 5,
+        in_specs=[VMEM] * 6,
         out_specs=[VMEM, VMEM, VMEM],
         scratch_shapes=[
             pltpu.VMEM(head.shape, jnp.float32),
@@ -844,7 +858,7 @@
         compiler_params=pltpu.CompilerParams(
             collective_id=collective, has_side_effects=True, vmem_limit_bytes=40 * 2**20
         ),
-    )(head, wants, given, rest, facts)
+    )(head, wants, given, rest, facts, crossed)
 
 
 def slots(tokens, own_rows):
@@ -1226,8 +1240,9 @@
     )
 
     def pieces(blocks, qkv, out, up, down, pos, norms):
-        tail = norms.astype(f32).reshape(blocks, 1, -1)
-        tail = jnp.pad(tail, ((0, 0), (0, 7), (0, width - tail.shape[2])))
+        lines = norms.shape[0]
+        tail = jnp.moveaxis(norms.astype(f32).reshape(lines, blocks, -1), 1, 0)
+        tail = jnp.pad(tail, ((0, 0), (0, 8 - lines), (0, width - tail.shape[2])))
         small = jnp.concatenate([pos.reshape(blocks, -1, width).astype(f32), tail], axis=1)
         big = [part.astype(bf16).reshape(blocks, -1, part.shape[1]) for part in (qkv, out, up, down)]
         return big + [lax.optimization_barrier(small.astype(bf16))]
@@ -1261,14 +1276,16 @@
             across(at_up, s_up.shape[1] // width),
             packed[:, at_down:at_pos].reshape(-1, width),
             packed[:, at_pos:at_norms].reshape(-1, width),
-            packed[:, at_norms, : s_norms.size].reshape(-1, s_norms.shape[1]),
+            jnp.moveaxis(
+                packed[:, at_norms : at_norms + s_norms.shape[1], :lead], 1, 0
+            ).reshape(s_norms.shape[1], -1),
         )
 
-    own_packed = pack(pieces(1, s_qkv, s_out, s_up, s_down, s_pos, s_norms))
+    own_packed = pack(pieces(1, s_qkv, s_out, s_up, s_down, s_pos, s_norms.T))
     w_qkv, w_out, w_up, w_down, positions, norms = unpack(
         lax.all_gather(own_packed, FSDP, axis=0, tiled=True)
     )
-    student = (w_qkv, w_out, w_up, w_down, norms)
+    student = (w_qkv, w_out, w_up, w_down, norms.T)
     heads = lax.all_gather(t_table[0], "grp", axis=0, tiled=False)
 
     taken = teacher_rows(
@@ -1278,7 +1295,7 @@
         got.reshape(-1, got.shape[2]),
         t_extra.reshape(-1, span, t_width),
         t_pos[0],
-        t_norms[0].astype(f32).T,
+        t_norms[0].T,
         t_qkv[0],
         t_out[0],
         t_up[0],
@@ -1305,8 +1322,6 @@
     chip_counted = lax.dynamic_index_in_dim(plane_counted, chip, 0, keepdims=False)
     shift, own_loss = blend(stats, chip_counted, 3)
     head_grad, head_low, grad_rows, crossed = head_grads(logits, z, shift, h, own_table)
-    count_local = jnp.sum((picks < lengths[:, None]).astype(f32))
-    loss_local = jnp.sum(own_loss) - jnp.sum(crossed)
     grad_rows, head_grad = sum_and_scatter(
         [grad_rows.reshape(fsdp, picked, width)], width, f32, "head", [head_grad, head_low], 5
     )
@@ -1334,26 +1349,15 @@
     _, head_grad = lax.while_loop(
         lambda state: state[0] < rounds, more_grads, (jnp.int32(1), head_grad)
     )
-    g_norms = g_norms[:6].T
     parts = pieces(fsdp, g_qkv, g_out, g_up, g_down, g_pos, g_norms)
     rest, got = sum_and_scatter(parts, width, bf16, "rows", [given_rows], 7)
-    row = jnp.arange(8)[:, None]
-    column_of = jnp.arange(128)[None, :]
-    told = jnp.where((row == 0) & (column_of == 0), loss_local, 0.0)
-    told += jnp.where((row == 1) & (column_of == 0), count_local, 0.0)
     table_sum, rest_sum, seen = sum_of_groups(
-        head_grad, wants.reshape(4, -1), got.reshape(4, -1, got.shape[3]), rest, told, 8
-    )
-    seen = seen.sum(0)
-    squares, loss_sum, count = jnp.sum(seen[:8]), seen[8, 0], seen[9, 0]
-    at_norms = rest_sum.shape[0] - 8
-    norms_sum = rest_sum[at_norms, : s_norms.size].astype(f32).reshape(s_norms.shape).T
+        head_grad, wants.reshape(4, -1), got.reshape(4, -1, got.shape[3]), rest, own_loss, crossed, 8
+    )
     turned = [group[:6] + (group[6].T,) for group in (masters, momenta, averages)]
-    clip_norm = jnp.sqrt(squares) / count
-    factor = jnp.minimum(1.0, clip_limit / clip_norm) / count
-    outs = update(factor, table_sum, rest_sum, norms_sum, *turned)
+    loss_sum, count, clip_norm, *outs = update(seen, table_sum, rest_sum, *turned)
     outs = tuple(out.T if k % 7 == 6 else out for k, out in enumerate(outs))
-    return (loss_sum, count, clip_norm) + outs
+    return (loss_sum.reshape(()), count.reshape(()), clip_norm[0, 0]) + outs
 
 
 def solution(mesh):

time: 453 us -> 447 us (0.987)
  between operations: 24.7 us -> 19.5 us
  transfers between devices with their start and end apart: 3 -> 3, of which waited for: 0 -> 0; matrix products, arithmetic and copies ran while one was open for 12% -> 11% of each run, Pallas kernels for 34% -> 35%
where the time goes in v5:
time: 447 us; the launch traced here: 440 us
  Pallas kernels  339 us (76%)
  local copies, waits for them, and re-layouts  37.4 us (8%)
  other arithmetic  19.7 us (4%)
  between operations  19.5 us (4%)
  matrix products  14.6 us (3%)
  loops' own time  9.94 us (2%)
    pallas_call x2, Pallas kernels, sum_and_scatter(): pl.pallas_call(partial(scatter_sum_kernel, plan, side), out_shape=[jax.Sh...  67.5 us
    pallas_call x1, Pallas kernels, route(): pl.pallas_call(route_kernel, out_shape=[jax.ShapeDtypeStruct(notes.shape,...  57.8 us
    pallas_call x1, Pallas kernels, teacher_rows(): pl.pallas_call(teacher_kernel, grid=(count,), out_shape=jax.ShapeDtypeStr...  39.6 us
    pallas_call x2, Pallas kernels, vocabulary_logits(): pl.pallas_call(logits_kernel, grid=(count, devices // block), out_shape=[...  36.2 us
    pallas_call x1, Pallas kernels, gather_plane(): pl.pallas_call(gather_kernel, out_shape=jax.ShapeDtypeStruct((16, 2, rows...  32.9 us
    pallas_call x1, Pallas kernels, sum_of_groups(): pl.pallas_call(group_sum_kernel, out_shape=[jax.ShapeDtypeStruct((head.sh...  28.8 us
    pallas_call x1, Pallas kernels, blend(): pl.pallas_call(blend_kernel, out_shape=[jax.ShapeDtypeStruct((16, 8, 128)...  18.8 us
    pallas_call x1, Pallas kernels, head_grads(): pl.pallas_call(head_grads_kernel, grid=(rows // wide,), out_shape=[jax.Sh...  17.8 us
  transfers between devices with their start and end apart: 3, of which 0 were waited for; matrix products, arithmetic and copies ran while one was open for 11% of the time, Pallas kernels for 35%

profile of v5, /device:TPU:1, one launch (start us, length us, event | category | flops | bytes accessed | tf_op | source)
XLA Modules:
  0.0 440.5 jit_solution(10940832219115649512)
XLA Ops:
  7.3 0.7 all-gather.5.cloned.1.call-update
  8.0 0.7 convert_bitcast_fusion.4
  8.7 0.7 convert_bitcast_fusion.3
  9.4 0.9 convert_bitcast_fusion.2
  10.4 0.8 constant_dynamic-update-slice_fusion.5
  11.1 0.9 convert_bitcast_fusion.1
  14.3 7.2 %shard_map.487 = s32[4,8,128]{2,1,0:T(8,128)} custom-call(s32[4,8,128]{2,1,0:T(8,128)} %broadcast_in_dim.255.source), custom_call_target="tpu_custom_call" | custom-call | tf_op jit(solution)/shard_map/pallas_call | solution.py:164
  21.5 0.7 slice_bitcast_fusion.6
  22.7 1.2 convert_reduce_fusion
  29.7 0.7 slice_reduce_fusion.4
  31.2 0.8 select_reduce_fusion.4
  32.8 57.8 %shard_map.488 = (s32[32,8,128]{2,1,0:T(8,128)S(1)}, bf16[32,48,1024]{2,1,0:T(8,128)(2,1)S(1)}) custom-call(s32[32,8,128]{2,1,0:T(8,128)S(1)} %stack.46.notes, bf16[960,768]{1,0:T(8,128)(2,1)} %bitcast.251, bf16[960,512]{1,0:T(8,128)(2,1)S(1)} %convert_element_type.166.s_table.table), custom_call_target="tpu_custom_call" | custom-call | tf_op jit(solution)/shard_map/pallas_call | solution.py:127
  90.7 1.8 copy-done.6
  92.5 1.2 slice_reduce_fusion.1
  93.7 1.0 copy.116.slot
  94.7 0.8 copy.117.picks
  95.5 1.2 broadcast_in_dim.263
  96.8 0.7 broadcast_in_dim.264
  97.5 9.2 %while.28 = (s32[]{:T(128)}, bf16[1024,768]{1,0:T(8,128)(2,1)}, bf16[256,512]{1,0:T(8,128)(2,1)}, s32[]{:T(128)}, s32[1024]{0:T(1024)S(1)}, /*index=5*/s32[1024]...) while((s32[]{:T(128)}, bf16[1024,768]{1,0:T(8,128)(2,1)}, ...), condition=%wide.region_12.13_spmd, body=%wide.region_9.12_spmd.sunk | while | flops 5663440896 | bytes 60638628 | solution.py:1238
  106.7 0.9 copy-done.39
  107.6 39.6 %shard_map.489.source = bf16[4,64,768]{2,1,0:T(8,128)(2,1)} custom-call(s32[1,4]{1,0:T(1,128)} %bitcast.309, s32[4,256,1]{2,1,0:T(8,128)} %copy.116.slot, s32[4,64,1]{2,1,0:T(8,128)} %copy.117.picks, bf16[1536,1024]{1,0:T(8,128)(2,1)} %bitcast.229, bf16[4,256,768]{2,1,0:T(8,128)(2,1)} %bitcast.250, bf16[256,768]{1,0:T(8,128)(2,1)} %bitcast.274, ...), custom_call_target="tpu_custom_call" | custom-call | tf_op jit(solution)/shard_map/pallas_call | solution.py:348
  147.2 8.2 %shard_map.490 = bf16[4,64,768]{2,1,0:T(8,128)(2,1)} custom-call(bf16[4,64,768]{2,1,0:T(8,128)(2,1)} %shard_map.489.source), custom_call_target="tpu_custom_call" | custom-call | tf_op jit(solution)/shard_map/pallas_call | solution.py:164
  157.2 1.1 convert_bitcast_fusion.6.head
  158.3 1.2 fusion.58
  159.6 0.9 convert_bitcast_fusion
  160.6 1.5 fusion.64
  162.5 3.8 fusion.57
  167.4 0.9 copy.119
  168.5 0.8 copy.121
  169.3 3.1 fusion.65
  172.4 2.0 convolution_convert_fusion.3
  174.4 0.8 copy.124.context
  175.2 1.8 slice.236
  179.8 6.3 %fusion.22 = (bf16[256,2048]{1,0:T(8,128)(2,1)S(1)}, f32[256,2048]{1,0:T(8,128)}) fusion(bf16[256,512]{1,0:T(8,128)(2,1)S(1)} %fusion.38.second_low, bf16[512,2048]{1,0:T(8,128)(2,1)S(1)} %pad_maximum_fusion.2.w_up), kind=kOutput, calls=%fused_computation.77 | convolution fusion | flops 570949632 | bytes 5505024 | tf_op jit(solution)/shard_map/blk,kn->bln/dot_general | solution.py:908
  186.0 0.8 fusion.67
  187.9 0.7 gather_fusion
  188.7 0.7 select_convert_fusion.source
  189.4 32.9 %shard_map.492 = bf16[16,2,64,512]{3,2,1,0:T(8,128)(2,1)} custom-call(bf16[64,512]{1,0:T(8,128)(2,1)} %select_convert_fusion.source), custom_call_target="tpu_custom_call" | custom-call | tf_op jit(solution)/shard_map/pallas_call | solution.py:198
  222.3 7.6 %shard_map.493 = (f32[1,960,2048]{2,1,0:T(8,128)}, f32[1,4,2048]{2,1,0:T(4,128)}) custom-call(s32[1,2048]{1,0:T(1,128)} %sub.211.labels, bf16[32,1,64,512]{3,2,1,0:T(8,128)(2,1)} %bitcast.225, bf16[1,960,512]{2,1,0:T(8,128)(2,1)} %convert_bitcast_fusion.6.head), custom_call_target="tpu_custom_call" | custom-call | tf_op jit(solution)/shard_map/pallas_call | solution.py:427
  229.9 1.2 pad_maximum_fusion.3.w_qkv
  231.2 28.6 %shard_map.491 = (f32[4,960,2048]{2,1,0:T(8,128)}, f32[4,4,2048]{2,1,0:T(4,128)}) custom-call(s32[1,2048]{1,0:T(1,128)} %sub.211.labels, bf16[32,4,64,768]{3,2,1,0:T(8,128)(2,1)} %bitcast.247, bf16[4,960,768]{2,1,0:T(8,128)(2,1)} %all-gather.5.cloned.1.call-done.head), custom_call_target="tpu_custom_call" | custom-call | tf_op jit(solution)/shard_map/pallas_call | solution.py:427
  259.8 1.6 pad_maximum_fusion.5.stats
  261.4 18.8 %shard_map.494 = (f32[16,8,128]{2,1,0:T(8,128)}, f32[8,128]{1,0:T(8,128)}) custom-call(f32[5,4,2048]{2,1,0:T(4,128)} %pad_maximum_fusion.5.stats, f32[1,128]{1,0:T(1,128)} %fusion.48.counted_ref), custom_call_target="tpu_custom_call" | custom-call | tf_op jit(solution)/shard_map/pallas_call | solution.py:515
  280.2 0.8 copy-done.32
  281.1 17.8 %shard_map.495 = (f32[960,512]{1,0:T(8,128)S(1)}, bf16[960,512]{1,0:T(8,128)(2,1)S(1)}, bf16[2048,512]{1,0:T(8,128)(2,1)S(1)}, f32[1,256]{1,0:T(1,128)S(1)}) custom-call(f32[4,960,2048]{2,1,0:T(8,128)} %get-tuple-element.585.logits, f32[1,960,2048]{2,1,0:T(8,128)} %get-tuple-element.588.z, f32[16,8,128]{2,1,0:T(8,128)S(1)} %copy-done.32, ...), custom_call_target="tpu_custom_call" | custom-call | tf_op jit(solution)/shard_map/pallas_call | solution.py:578
  299.0 18.4 %shard_map.496 = (f32[64,512]{1,0:T(8,128)S(1)}, f32[960,128]{1,0:T(8,128)}) custom-call(bf16[16,2,64,512]{3,2,1,0:T(8,128)(2,1)S(1)} %bitcast.233, f32[960,512]{1,0:T(8,128)S(1)} %get-tuple-element.593.refs_1_, bf16[960,512]{1,0:T(8,128)(2,1)S(1)} %get-tuple-element.594.refs_2_), custom_call_target="tpu_custom_call" | custom-call | tf_op jit(solution)/shard_map/pallas_call | solution.py:752
  317.5 14.4 %shard_map.497 = (bf16[512,1536]{1,0:T(8,128)(2,1)S(1)}, bf16[512,512]{1,0:T(8,128)(2,1)S(1)}, bf16[512,2048]{1,0:T(8,128)(2,1)S(1)}, bf16[2048,512]{1,0:T(8,128...) custom-call(s32[1,1]{1,0:T(1,128)} %bitcast.224.lengths, ...), custom_call_target="tpu_custom_call" | custom-call | tf_op jit(solution)/shard_map/pallas_call | solution.py:1086
  331.9 1.3 copy-done.14
  333.2 1.0 copy-done.18
  334.2 0.8 copy-done.28
  335.0 0.7 convert_element_type.191
  335.7 0.8 convert_bitcast_fusion.5
  336.6 1.2 copy.125
  338.4 1.4 copy-done.17
  339.8 1.0 copy-done.29
  340.8 49.1 %shard_map.498 = (bf16[208,512]{1,0:T(8,128)(2,1)S(1)}, bf16[32,4,32,128]{3,2,1,0:T(8,128)(2,1)S(1)}) custom-call(bf16[16,2,16,1536]{3,2,1,0:T(8,128)(2,1)S(1)} %bitcast.237, bf16[16,2,16,512]{3,2,1,0:T(8,128)(2,1)S(1)} %bitcast.239, bf16[16,2,16,2048]{3,2,1,0:T(8,128)(2,1)S(1)} %bitcast.234, bf16[16,2,64,512]{3,2,1,0:T(8,128)(2,1)S(1)} %bitcast.235, ...), custom_call_target="tpu_custom_call" | custom-call | tf_op jit(solution)/shard_map/pallas_call | solution.py:752
  389.9 1.0 copy-done.20
  390.9 0.7 while.29
  392.1 28.8 %shard_map.499 = (bf16[960,512]{1,0:T(8,128)(2,1)S(1)}, bf16[208,512]{1,0:T(8,128)(2,1)S(1)}, f32[32,16,128]{2,1,0:T(8,128)S(1)}) custom-call(f32[960,128]{1,0:T(8,128)} %get-tuple-element.598.head, s32[4,1024]{1,0:T(4,128)S(1)} %reshape_squeeze.4.wants, bf16[4,1024,128]{2,1,0:T(8,128)(2,1)S(1)} %bitcast.238, bf16[208,512]{1,0:T(8,128)(2,1)S(1)} %get-tuple-element.606.rest, ...), custom_call_target="tpu_custom_call" | custom-call | tf_op jit(solution)/shard_map/pallas_call | solution.py:842
  421.0 0.9 copy-done.27
  421.9 0.7 copy-done.30
  422.6 0.7 copy-done.31
  423.3 9.3 %shard_map.500 = (f32[1,1]{1,0:T(1,128)}, f32[1,1]{1,0:T(1,128)}, f32[8,128]{1,0:T(8,128)}, f32[960,512]{1,0:T(8,128)}, f32[8,512]{1,0:T(8,128)}, /*index=5*/f32...) custom-call(f32[32,16,128]{2,1,0:T(8,128)} %copy-done.30, ...), custom_call_target="tpu_custom_call" | custom-call | tf_op jit(solution)/shard_map/pallas_call | solution.py:263
  432.6 1.2 slice.199
  (190 shorter events, 13.9 us)
Async XLA Ops:
  7.2 4.9 %copy-start.50 = (f32[64,512]{1,0:T(8,128)S(1)}, f32[64,512]{1,0:T(8,128)}, u32[]{:S(2)}) copy-start(f32[64,512]{1,0:T(8,128)} %refs_5_.1) | copy-start | bytes 393220
  7.2 6.4 %copy-start.34 = (s32[1,64]{1,0:T(1,128)S(1)}, s32[1,64]{1,0:T(1,128)}, u32[]{:S(2)}) copy-start(s32[1,64]{1,0:T(1,128)} %picks.1) | copy-start | bytes 772
  7.2 6.4 %copy-start.59 = (s32[1,256]{1,0:T(1,128)S(1)}, s32[1,256]{1,0:T(1,128)}, u32[]{:S(2)}) copy-start(s32[1,256]{1,0:T(1,128)} %param.36) | copy-start | bytes 3076
  7.2 25.0 %copy-start.60 = (s32[1,64]{1,0:T(1,128)S(1)}, s32[1,64]{1,0:T(1,128)}, u32[]{:S(2)}) copy-start(s32[1,64]{1,0:T(1,128)} %param.39) | copy-start | bytes 772
  7.2 25.2 %copy-start.35 = (f32[960,512]{1,0:T(8,128)S(1)}, f32[960,512]{1,0:T(8,128)}, u32[]{:S(2)}) copy-start(f32[960,512]{1,0:T(8,128)} %refs_0_.1) | copy-start | bytes 5898244
  7.2 140.0 %all-gather.5.cloned.1.call-start = ((), (), s32[]{:S(2)}) async-start(), calls=%async_computation.5 | async-start | bytes 7372800 | tf_op jit(solution)/shard_map/all_gather | solution.py:1289
  8.0 151.6 %all-gather.7.cloned.1.call-start = ((), (), s32[]{:S(2)}) async-start(), calls=%async_computation.6 | async-start | bytes 7028736 | tf_op jit(solution)/shard_map/all_gather | solution.py:1286
  12.1 0.7 copy-start.57
  12.8 218.3 %all-gather.9.cloned.1.call-start = ((), (), s32[]{:S(2)}) async-start(), calls=%async_computation.7 | async-start | bytes 12976128 | tf_op jit(solution)/shard_map/all_gather | solution.py:1307
  90.7 1.8 copy-start.6
  106.7 0.9 copy-start.39
  107.6 49.6 %copy-start.36 = (f32[960,512]{1,0:T(8,128)S(1)}, f32[960,512]{1,0:T(8,128)}, u32[]{:S(2)}) copy-start(f32[960,512]{1,0:T(8,128)} %refs_0_.1) | copy-start | bytes 5898244
  158.3 2.3 copy-start.56
  166.3 0.8 copy-start.42
  166.3 1.0 copy-start.44
  166.3 10.8 %copy-start.7 = (bf16[32,16,512]{2,1,0:T(8,128)(2,1)}, bf16[32,16,512]{2,1,0:T(8,128)(2,1)S(1)}, u32[]{:S(2)}) copy-start(bf16[32,16,512]{2,1,0:T(8,128)(2,1)S(1)} %get-tuple-element.734) | copy-start | bytes 1572868
  167.3 5.1 %copy-start.11 = (bf16[256,1536]{1,0:T(8,128)(2,1)}, bf16[256,1536]{1,0:T(8,128)(2,1)S(1)}, u32[]{:S(2)}) copy-start(bf16[256,1536]{1,0:T(8,128)(2,1)S(1)} %convolution_convert_fusion.2.packed) | copy-start | bytes 2359300
  168.4 4.0 copy-start.53
  177.1 9.0 %copy-start.1 = (bf16[32,64,512]{2,1,0:T(8,128)(2,1)}, bf16[32,64,512]{2,1,0:T(8,128)(2,1)S(1)}, u32[]{:S(2)}) copy-start(bf16[32,64,512]{2,1,0:T(8,128)(2,1)S(1)} %slice.236) | copy-start | bytes 6291460
  177.1 1.4 copy-start.46
  177.1 2.0 copy-start.47
  177.1 2.2 copy-start.48
  177.1 2.3 copy-start.49
  177.9 1.8 copy-start.24
  179.7 6.3 %copy-start.3 = (bf16[512,2048]{1,0:T(8,128)(2,1)}, bf16[512,2048]{1,0:T(8,128)(2,1)S(1)}, u32[]{:S(2)}) copy-start(bf16[512,2048]{1,0:T(8,128)(2,1)S(1)} %pad_maximum_fusion.2.w_up) | copy-start | bytes 6291460
  186.0 1.0 copy-start.22
  187.0 0.8 copy-start.9
  189.4 40.6 %copy-start.43 = (bf16[32,16,512]{2,1,0:T(8,128)(2,1)S(1)}, bf16[32,16,512]{2,1,0:T(8,128)(2,1)}, u32[]{:S(2)}) copy-start(bf16[32,16,512]{2,1,0:T(8,128)(2,1)} %copy-done.42) | copy-start | bytes 1572868
  189.4 40.6 %copy-start.45 = (bf16[32,16,512]{2,1,0:T(8,128)(2,1)S(1)}, bf16[32,16,512]{2,1,0:T(8,128)(2,1)}, u32[]{:S(2)}) copy-start(bf16[32,16,512]{2,1,0:T(8,128)(2,1)} %copy-done.44) | copy-start | bytes 1572868
  231.2 28.6 %copy-start.58 = (f32[1,4,2048]{2,1,0:T(4,128)S(1)}, f32[1,4,2048]{2,1,0:T(4,128)}, u32[]{:S(2)}) copy-start(f32[1,4,2048]{2,1,0:T(4,128)} %get-tuple-element.590) | copy-start | bytes 98308
  231.2 49.0 %copy-start = (bf16[16,2,64,512]{3,2,1,0:T(8,128)(2,1)S(1)}, bf16[16,2,64,512]{3,2,1,0:T(8,128)(2,1)}, u32[]{:S(2)}) copy-start(bf16[16,2,64,512]{3,2,1,0:T(8,128)(2,1)} %shard_map.492) | copy-start | bytes 6291460
  280.2 0.8 copy-start.32
  281.1 36.3 %copy-start.5 = (bf16[512,1536]{1,0:T(8,128)(2,1)S(1)}, bf16[512,1536]{1,0:T(8,128)(2,1)}, u32[]{:S(2)}) copy-start(bf16[512,1536]{1,0:T(8,128)(2,1)} %pad_maximum_fusion.3.w_qkv) | copy-start | bytes 4718596
  281.1 36.4 %copy-start.10 = (f32[256,512]{1,0:T(8,128)S(1)}, f32[256,512]{1,0:T(8,128)}, u32[]{:S(2)}) copy-start(f32[256,512]{1,0:T(8,128)} %copy-done.9) | copy-start | bytes 1572868
  281.1 36.4 %copy-start.12 = (bf16[256,1536]{1,0:T(8,128)(2,1)S(1)}, bf16[256,1536]{1,0:T(8,128)(2,1)}, u32[]{:S(2)}) copy-start(bf16[256,1536]{1,0:T(8,128)(2,1)} %copy-done.11) | copy-start | bytes 2359300
  281.1 36.4 %copy-start.13 = (f32[256,2048]{1,0:T(8,128)S(1)}, f32[256,2048]{1,0:T(8,128)}, u32[]{:S(2)}) copy-start(f32[256,2048]{1,0:T(8,128)} %get-tuple-element.768.hidden_pre) | copy-start | bytes 6291460
  281.1 36.4 %copy-start.23 = (bf16[256,2048]{1,0:T(8,128)(2,1)S(1)}, bf16[256,2048]{1,0:T(8,128)(2,1)}, u32[]{:S(2)}) copy-start(bf16[256,2048]{1,0:T(8,128)(2,1)} %copy-done.22) | copy-start | bytes 3145732
  281.1 36.4 %copy-start.26 = (bf16[256,512]{1,0:T(8,128)(2,1)S(1)}, bf16[256,512]{1,0:T(8,128)(2,1)}, u32[]{:S(2)}) copy-start(bf16[256,512]{1,0:T(8,128)(2,1)} %copy.124.context) | copy-start | bytes 786436
  298.9 18.5 %copy-start.2 = (bf16[32,64,512]{2,1,0:T(8,128)(2,1)S(1)}, bf16[32,64,512]{2,1,0:T(8,128)(2,1)}, u32[]{:S(2)}) copy-start(bf16[32,64,512]{2,1,0:T(8,128)(2,1)} %copy-done.1) | copy-start | bytes 6291460
  298.9 18.5 %copy-start.4 = (bf16[512,2048]{1,0:T(8,128)(2,1)S(1)}, bf16[512,2048]{1,0:T(8,128)(2,1)}, u32[]{:S(2)}) copy-start(bf16[512,2048]{1,0:T(8,128)(2,1)} %copy-done.3) | copy-start | bytes 6291460
  299.0 18.5 %copy-start.8 = (bf16[32,16,512]{2,1,0:T(8,128)(2,1)S(1)}, bf16[32,16,512]{2,1,0:T(8,128)(2,1)}, u32[]{:S(2)}) copy-start(bf16[32,16,512]{2,1,0:T(8,128)(2,1)} %copy-done.7) | copy-start | bytes 1572868
  299.0 18.5 %copy-start.25 = (bf16[256,512]{1,0:T(8,128)(2,1)S(1)}, bf16[256,512]{1,0:T(8,128)(2,1)}, u32[]{:S(2)}) copy-start(bf16[256,512]{1,0:T(8,128)(2,1)} %copy-done.24) | copy-start | bytes 786436
  331.9 1.4 copy-start.14
  333.2 1.0 copy-start.18
  334.2 0.8 copy-start.28
  335.0 1.5 copy-start.16
  335.0 3.2 copy-start.19
  336.6 1.7 copy-start.15
  338.4 1.4 copy-start.17
  339.8 1.0 copy-start.29
  389.9 1.0 copy-start.20
  390.9 1.2 copy-start.21
  390.9 1.2 copy-start.33
  420.9 1.0 copy-start.27
  421.9 0.7 copy-start.30
  422.6 0.7 copy-start.31
Sparse Core Ops, SparseCore 0:
  9.7 65.8 all-gather.4
  77.9 50.7 all-gather.6
  155.6 75.1 all-gather.8

commit v6 on v5

--- a/solution.py
+++ b/solution.py
@@ -48,10 +48,12 @@
     return (place["y"] * 4 + place["x"]) * 2 + place["c"]
 
 
-def greet(places):
+def greet(places, work=None):
     barrier = pltpu.get_barrier_semaphore()
     for place in places:
         pl.semaphore_signal(barrier, inc=1, device_id=place, device_id_type=MESH)
+    if work:
+        work()
     pl.semaphore_wait(barrier, len(places))
 
 
@@ -245,7 +247,12 @@
             step(k, blocks[0] if len(blocks) == 1 else jnp.concatenate(blocks, axis=1))
         small = rest_grad[at : at + 16].astype(jnp.float32)
         step(1, small[:8])
-        step(6, small[8 : 8 + masters[6].shape[0], : masters[6].shape[1]])
+        lines, columns = masters[6].shape
+        at = ((lax.axis_index("y") * 4 + lax.axis_index("x")) * 2 + lax.axis_index("c")) * columns
+        row = lax.broadcasted_iota(jnp.int32, (width, columns), 0) - at
+        own = lax.broadcasted_iota(jnp.int32, (width, columns), 1) == row
+        own = jnp.where(own, 1.0, 0.0).astype(jnp.bfloat16)
+        step(6, product(small.astype(jnp.bfloat16), own)[8 : 8 + lines])
 
 
 def update(seen, table_grad, rest_grad, masters, momenta, averages):
@@ -606,7 +613,7 @@
     return pl.ds(pl.multiple_of(group * 128, 128), 128)
 
 
-def scatter_sum_kernel(plan, side, *refs):
+def scatter_sum_kernel(plan, side, *refs, work=None):
     f32, bf16 = jnp.float32, jnp.bfloat16
     parts, refs = refs[: len(plan)], refs[len(plan) :]
     if side == "head":
@@ -621,7 +628,7 @@
     steps_y = [moved(me, d, 0, 0) for d in (1, 2, 3)]
     sibling = moved(me, 0, 0, 1)
     plane = [moved(me, *step) for step in AROUND]
-    greet(groups + (plane if side == "rows" else [sibling] + steps_x + steps_y))
+    greet(groups + (plane if side == "rows" else [sibling] + steps_x + steps_y), work)
     copies, at, k = [], 0, 16
     width = own.shape[-1]
     for part, (rows, columns) in zip(parts, plan):
@@ -733,46 +740,45 @@
         copy.wait()
 
 
-def sum_and_scatter(parts, width, dtype, side, sided, collective):
-    plan = [part.shape[1:] for part in parts]
-    rows = sum(r * (c // width) for r, c in plan)
-    pieces = sum(c // width for _, c in plan)
+def scatter_scratch(rows, width, pieces, more):
     cut = width // 2
     rest = width - cut
     bf16 = jnp.bfloat16
-    room = (12 if side == "head" else 36) * 2**20
-    tall = sided[0].shape[0]
-    if side == "head":
-        side_out = jax.ShapeDtypeStruct((tall, 128), jnp.float32)
-        side_scratch = [pltpu.VMEM((tall, 128), jnp.float32), pltpu.VMEM((3, tall, 128), bf16)]
-    else:
-        side_out = jax.ShapeDtypeStruct((32, 4, tall // 32, 128), bf16)
-        side_scratch = [pltpu.VMEM((4, tall, 128), bf16)]
-    semaphores = 16 + pieces + (len(AROUND) if side == "rows" else 0)
+    semaphores = 16 + pieces + more
+    return [
+        pltpu.VMEM((16, rows, width), bf16),
+        pltpu.VMEM((16, rows, width), bf16),
+        pltpu.VMEM((4, 4, rows, width), bf16),
+        pltpu.VMEM((3, 4, rows, cut), bf16),
+        pltpu.VMEM((3, 4, rows, rest), bf16),
+        pltpu.VMEM((4, rows, cut), bf16),
+        pltpu.VMEM((4, rows, rest), bf16),
+        pltpu.VMEM((3, rows, cut), bf16),
+        pltpu.VMEM((3, rows, rest), bf16),
+        pltpu.SemaphoreType.DMA((semaphores,)),
+        pltpu.SemaphoreType.DMA((semaphores,)),
+        pltpu.SemaphoreType.DMA((1 + pieces,)),
+    ]
+
+
+def scatter_head(part, exact, low, collective):
+    _, rows, width = part.shape
+    tall = low.shape[0]
+    f32, bf16 = jnp.float32, jnp.bfloat16
     return pl.pallas_call(
-        partial(scatter_sum_kernel, plan, side),
-        out_shape=[jax.ShapeDtypeStruct((rows, width), dtype), side_out],
-        in_specs=[VMEM if side == "rows" else ANY] * (len(parts) + len(sided)),
+        partial(scatter_sum_kernel, [(rows, width)], "head"),
+        out_shape=[
+            jax.ShapeDtypeStruct((rows, width), f32),
+            jax.ShapeDtypeStruct((tall, 128), f32),
+        ],
+        in_specs=[ANY] * 3,
         out_specs=[VMEM, VMEM],
-        scratch_shapes=side_scratch
-        + [
-            pltpu.VMEM((16, rows, width), bf16),
-            pltpu.VMEM((16, rows, width), bf16),
-            pltpu.VMEM((4, 4, rows, width), bf16),
-            pltpu.VMEM((3, 4, rows, cut), bf16),
-            pltpu.VMEM((3, 4, rows, rest), bf16),
-            pltpu.VMEM((4, rows, cut), bf16),
-            pltpu.VMEM((4, rows, rest), bf16),
-            pltpu.VMEM((3, rows, cut), bf16),
-            pltpu.VMEM((3, rows, rest), bf16),
-            pltpu.SemaphoreType.DMA((semaphores,)),
-            pltpu.SemaphoreType.DMA((semaphores,)),
-            pltpu.SemaphoreType.DMA((1 + pieces,)),
-        ],
+        scratch_shapes=[pltpu.VMEM((tall, 128), f32), pltpu.VMEM((3, tall, 128), bf16)]
+        + scatter_scratch(rows, width, 1, 0),
         compiler_params=pltpu.CompilerParams(
-            collective_id=collective, has_side_effects=True, vmem_limit_bytes=room
+            collective_id=collective, has_side_effects=True, vmem_limit_bytes=12 * 2**20
         ),
-    )(*[part.reshape(16, 2, *part.shape[1:]) for part in parts], *sided)
+    )(part.reshape(16, 2, rows, width), exact, low)
 
 
 def group_sum_kernel(
@@ -997,8 +1003,8 @@
     g_out,
     g_up,
     g_down,
-    g_emb,
-    g_norms,
+    small,
+    low_emb,
     given,
     d_packed,
     d_context,
@@ -1019,17 +1025,20 @@
     @pl.loop(0, w_up.shape[1] // width)
     def _(k):
         cols = pl.ds(pl.multiple_of(k * width, width), width)
-        g_down[cols] = product_of(active[:, cols], d_ffn, rows).astype(bf16)
+        blocks = g_down.shape[0] * width // w_up.shape[1]
+        piece = product_of(active[:, cols], d_ffn, rows)
+        g_down[pl.ds(k * blocks, blocks)] = piece.reshape(blocks, *g_down.shape[1:]).astype(bf16)
         pre = hidden_pre[:, cols]
         slope = 0.5 * (1.0 + lax.erf(pre * (0.5**0.5)))
         slope += pre * (jnp.exp(-0.5 * pre * pre) * (0.5 / math.pi) ** 0.5)
         d_up = (slope * product_of(d_ffn, w_down[cols], columns)).astype(bf16)
-        g_up[:, cols] = product_of(second_low[...], d_up, rows).astype(bf16)
+        piece = product_of(second_low[...], d_up, rows)
+        g_up[:, :, :, cols] = piece.reshape(*g_up.shape[:3], width).astype(bf16)
         carried[...] += product_of(d_up, w_up[:, cols], columns)
 
     d_joined, gain_b, shift_b = norm_back(joined[...], norms[2:3], carried[...])
     d_attn = d_joined.astype(bf16)
-    g_out[...] = product_of(context[...], d_attn, rows).astype(bf16)
+    g_out[...] = product_of(context[...], d_attn, rows).reshape(g_out.shape).astype(bf16)
     d_context[...] = product_of(d_attn, w_out[...], columns).astype(bf16)
     lane = lax.broadcasted_iota(jnp.int32, (span, 2 * HD), 1)
     halves = [jnp.where(lane < HD, 1.0, 0.0), jnp.where(lane < HD, 0.0, 1.0)]
@@ -1063,14 +1072,24 @@
     @pl.loop(0, 3)
     def _(k):
         cols = pl.ds(pl.multiple_of(k * width, width), width)
-        g_qkv[:, cols] = product_of(first_low[...], d_packed[:, cols], rows).astype(bf16)
+        piece = product_of(first_low[...], d_packed[:, cols], rows)
+        g_qkv[:, :, :, cols] = piece.reshape(*g_qkv.shape[:3], width).astype(bf16)
         carried[...] += product_of(d_packed[:, cols], w_qkv[:, cols], columns)
 
     d_emb, gain_a, shift_a = norm_back(embedded[...], norms[0:1], carried[...])
-    g_emb[...] = d_emb
+    carried[...] = d_emb
     lines = [gain_a, shift_a, gain_b, shift_b, gain_c, shift_c, jnp.zeros((2, width), f32)]
-    g_norms[...] = jnp.concatenate(lines, axis=0)
+    lines = jnp.concatenate(lines, axis=0)
+    owner = lax.broadcasted_iota(jnp.int32, lines.shape, 1)
+
+    @pl.loop(0, 32)
+    def _(k):
+        mine = (owner >= k * (width // 32)) & (owner < (k + 1) * (width // 32))
+        block = [carried[pl.ds(pl.multiple_of(k * 8, 8), 8)], jnp.where(mine, lines, 0.0)]
+        small[k // 2, lax.rem(k, 2)] = jnp.concatenate(block, axis=0).astype(bf16)
+
     low = d_emb.astype(bf16)
+    low_emb[...] = low
 
     @pl.loop(0, given.shape[0] // span)
     def _(k):
@@ -1079,29 +1098,55 @@
         given[pl.ds(pl.multiple_of(k * span, span), span)] = product(place, low).astype(bf16)
 
 
-def backward(lengths, picks, slot, places, weights, saved, grad_rows):
+def finish_kernel(plan, *refs):
+    inputs, (out, side_out, low_emb), refs = refs[:18], refs[18:21], refs[21:]
+    parts, (given, d_packed, d_context, carried), refs = refs[:5], refs[5:9], refs[9:]
+    g_qkv, g_out, g_up, g_down, small = parts
+    work = partial(
+        backward_kernel,
+        *inputs,
+        g_qkv,
+        g_out,
+        g_up,
+        g_down,
+        small,
+        low_emb,
+        given,
+        d_packed,
+        d_context,
+        carried,
+    )
+    scatter_sum_kernel(plan, "rows", *parts, given, out, side_out, *refs, work=work)
+
+
+def backward(lengths, picks, slot, places, weights, saved, grad_rows, collective):
     w_qkv, w_out, w_up, w_down, norms = weights
     span, width = saved[0].shape[1:]
     f32, bf16 = jnp.float32, jnp.bfloat16
+    plan = [(w.shape[0] // 32, w.shape[1]) for w in (w_qkv, w_out, w_up, w_down)] + [(16, width)]
+    rows = sum(r * (c // width) for r, c in plan)
+    pieces = sum(c // width for _, c in plan)
     return pl.pallas_call(
-        backward_kernel,
+        partial(finish_kernel, plan),
         out_shape=[
-            jax.ShapeDtypeStruct(w_qkv.shape, bf16),
-            jax.ShapeDtypeStruct(w_out.shape, bf16),
-            jax.ShapeDtypeStruct(w_up.shape, bf16),
-            jax.ShapeDtypeStruct(w_down.shape, bf16),
-            jax.ShapeDtypeStruct((span, width), f32),
-            jax.ShapeDtypeStruct((8, width), f32),
-            jax.ShapeDtypeStruct((places, width), bf16),
+            jax.ShapeDtypeStruct((rows, width), bf16),
+            jax.ShapeDtypeStruct((32, 4, places // 32, 128), bf16),
+            jax.ShapeDtypeStruct((span, width), bf16),
         ],
         in_specs=[pl.BlockSpec(memory_space=pltpu.SMEM)] + [VMEM] * 17,
-        out_specs=[VMEM] * 7,
-        scratch_shapes=[
+        out_specs=[VMEM] * 3,
+        scratch_shapes=[pltpu.VMEM((16, 2, *size), bf16) for size in plan]
+        + [
+            pltpu.VMEM((places, width), bf16),
             pltpu.VMEM((span, 3 * width), bf16),
             pltpu.VMEM((span, width), bf16),
             pltpu.VMEM((span, width), f32),
-        ],
-        compiler_params=pltpu.CompilerParams(vmem_limit_bytes=32 * 2**20),
+            pltpu.VMEM((4, places, 128), bf16),
+        ]
+        + scatter_scratch(rows, width, pieces, len(AROUND)),
+        compiler_params=pltpu.CompilerParams(
+            collective_id=collective, has_side_effects=True, vmem_limit_bytes=36 * 2**20
+        ),
     )(
         lengths[None],
         picks,
@@ -1322,15 +1367,14 @@
     chip_counted = lax.dynamic_index_in_dim(plane_counted, chip, 0, keepdims=False)
     shift, own_loss = blend(stats, chip_counted, 3)
     head_grad, head_low, grad_rows, crossed = head_grads(logits, z, shift, h, own_table)
-    grad_rows, head_grad = sum_and_scatter(
-        [grad_rows.reshape(fsdp, picked, width)], width, f32, "head", [head_grad, head_low], 5
+    grad_rows, head_grad = scatter_head(
+        grad_rows.reshape(fsdp, picked, width), head_grad, head_low, 5
     )
 
     g_slot = slot_in_round(s_owner, s_rank, S_ROOM, 0, S_APART)
-    g_qkv, g_out, g_up, g_down, g_pos, g_norms, given_rows = backward(
-        lengths, picks, g_slot, fsdp * S_APART, student, saved, grad_rows
-    )
-    low_embedded = g_pos.astype(bf16)
+    rest, got, low_embedded = backward(
+        lengths, picks, g_slot, fsdp * S_APART, student, saved, grad_rows, 7
+    )
 
     def given(turn):
         slot = slot_in_round(s_owner, s_rank, S_ROOM, turn, S_APART)
@@ -1349,8 +1393,6 @@
     _, head_grad = lax.while_loop(
         lambda state: state[0] < rounds, more_grads, (jnp.int32(1), head_grad)
     )
-    parts = pieces(fsdp, g_qkv, g_out, g_up, g_down, g_pos, g_norms)
-    rest, got = sum_and_scatter(parts, width, bf16, "rows", [given_rows], 7)
     table_sum, rest_sum, seen = sum_of_groups(
         head_grad, wants.reshape(4, -1), got.reshape(4, -1, got.shape[3]), rest, own_loss, crossed, 8
     )

time: 447 us -> 446 us (level)
    unnamed x116 -> x110, local copies, waits for them, and re-layouts: 17.3 us -> 9.2 us
    pallas_call x3 -> x2, Pallas kernels: 81.9 us -> 80.3 us  [the longest x1 62 us: backward(): pl.pallas_call(partial(finish_kernel, plan), out_shape=[jax.ShapeDtypeStr...]
  transfers between devices with their start and end apart: 3 -> 3, of which waited for: 0 -> 0; matrix products, arithmetic and copies ran while one was open for 11% -> 14% of each run, Pallas kernels for 35% -> 35%
where the time goes in v6:
time: 446 us; the launch traced here: 440 us
  Pallas kernels  338 us (76%)
  local copies, waits for them, and re-layouts  33.2 us (7%)
  other arithmetic  24 us (5%)
  between operations  19.4 us (4%)
  matrix products  14.4 us (3%)
  loops' own time  10.1 us (2%)
    pallas_call x1, Pallas kernels, backward(): pl.pallas_call(partial(finish_kernel, plan), out_shape=[jax.ShapeDtypeStr...  62 us
    pallas_call x1, Pallas kernels, route(): pl.pallas_call(route_kernel, out_shape=[jax.ShapeDtypeStruct(notes.shape,...  60.2 us
    pallas_call x1, Pallas kernels, teacher_rows(): pl.pallas_call(teacher_kernel, grid=(count,), out_shape=jax.ShapeDtypeStr...  39.7 us
    pallas_call x2, Pallas kernels, vocabulary_logits(): pl.pallas_call(logits_kernel, grid=(count, devices // block), out_shape=[...  36.1 us
    pallas_call x1, Pallas kernels, gather_plane(): pl.pallas_call(gather_kernel, out_shape=jax.ShapeDtypeStruct((16, 2, rows...  30.5 us
    pallas_call x1, Pallas kernels, sum_of_groups(): pl.pallas_call(group_sum_kernel, out_shape=[jax.ShapeDtypeStruct((head.sh...  28.8 us
    pallas_call x1, Pallas kernels, blend(): pl.pallas_call(blend_kernel, out_shape=[jax.ShapeDtypeStruct((16, 8, 128)...  19.2 us
    pallas_call x1, Pallas kernels, scatter_head(): pl.pallas_call(partial(scatter_sum_kernel, [(rows, width)], 'head'), out_...  18.3 us
  transfers between devices with their start and end apart: 3, of which 0 were waited for; matrix products, arithmetic and copies ran while one was open for 14% of the time, Pallas kernels for 35%

profile of v6, /device:TPU:1, one launch (start us, length us, event | category | flops | bytes accessed | tf_op | source)
XLA Modules:
  0.0 439.5 jit_solution(3081162777993226469)
XLA Ops:
  7.3 0.7 all-gather.5.cloned.1.call-update
  8.0 0.7 convert_bitcast_fusion.4
  8.7 0.7 convert_bitcast_fusion.3
  9.4 0.9 convert_bitcast_fusion.2
  10.4 0.8 constant_dynamic-update-slice_fusion.5
  11.1 0.9 convert_bitcast_fusion.1
  12.1 0.7 copy-done.44
  14.3 7.2 %shard_map.487 = s32[4,8,128]{2,1,0:T(8,128)} custom-call(s32[4,8,128]{2,1,0:T(8,128)} %broadcast_in_dim.255.source), custom_call_target="tpu_custom_call" | custom-call | tf_op jit(solution)/shard_map/pallas_call | solution.py:166
  21.5 0.7 slice_bitcast_fusion.6
  23.3 1.2 convert_reduce_fusion
  24.5 1.2 fusion.61
  28.9 0.6 fusion.60
  31.5 0.7 slice_reduce_fusion.4
  32.8 0.6 select_reduce_fusion.5
  34.0 0.8 sub.206
  35.5 1.5 select_reduce_fusion.4
  37.6 1.4 sub.202
  39.6 1.2 add_bitcast_fusion.2
  40.8 0.7 copy.108
  41.5 1.0 stack_reshape.3
  42.5 1.1 convert_element_type.160.s_table.table
  43.9 60.2 %shard_map.488 = (s32[32,8,128]{2,1,0:T(8,128)S(1)}, bf16[32,48,1024]{2,1,0:T(8,128)(2,1)S(1)}) custom-call(s32[32,8,128]{2,1,0:T(8,128)S(1)} %stack.46.notes, bf16[960,768]{1,0:T(8,128)(2,1)S(1)} %bitcast.237, bf16[960,512]{1,0:T(8,128)(2,1)} %convert_element_type.160.s_table.table), custom_call_target="tpu_custom_call" | custom-call | tf_op jit(solution)/shard_map/pallas_call | solution.py:129
  104.1 1.8 copy-done.6
  105.9 1.2 slice_reduce_fusion.1
  107.1 1.0 copy.109.slot
  108.1 0.8 copy.110.picks
  108.9 1.2 broadcast_in_dim.263
  110.2 0.7 broadcast_in_dim.264
  110.9 9.3 %while.28 = (s32[]{:T(128)}, bf16[1024,768]{1,0:T(8,128)(2,1)}, bf16[256,512]{1,0:T(8,128)(2,1)}, s32[]{:T(128)}, s32[1024]{0:T(1024)S(1)}, /*index=5*/s32[1024]...) while((s32[]{:T(128)}, bf16[1024,768]{1,0:T(8,128)(2,1)}, ...), condition=%wide.region_12.13_spmd, body=%wide.region_9.12_spmd.sunk | while | flops 5663440896 | bytes 46089560 | solution.py:1283
  120.2 39.7 %shard_map.489.source = bf16[4,64,768]{2,1,0:T(8,128)(2,1)} custom-call(s32[1,4]{1,0:T(1,128)} %bitcast.294, s32[4,256,1]{2,1,0:T(8,128)} %copy.109.slot, s32[4,64,1]{2,1,0:T(8,128)} %copy.110.picks, bf16[1536,1024]{1,0:T(8,128)(2,1)} %bitcast.221, bf16[4,256,768]{2,1,0:T(8,128)(2,1)} %bitcast.30.extra, bf16[256,768]{1,0:T(8,128)(2,1)} %bitcast.260, ...), custom_call_target="tpu_custom_call" | custom-call | tf_op jit(solution)/shard_map/pallas_call | solution.py:355
  159.9 8.5 %shard_map.490 = bf16[4,64,768]{2,1,0:T(8,128)(2,1)} custom-call(bf16[4,64,768]{2,1,0:T(8,128)(2,1)} %shard_map.489.source), custom_call_target="tpu_custom_call" | custom-call | tf_op jit(solution)/shard_map/pallas_call | solution.py:166
  168.5 0.7 sub.211.labels
  170.2 1.1 convert_bitcast_fusion.5.head
  171.3 1.2 fusion.56
  172.6 0.9 convert_bitcast_fusion
  173.6 1.5 fusion.62
  175.4 4.1 fusion.55
  180.6 0.9 copy.112
  181.6 0.9 copy.114
  182.5 3.1 fusion.63
  185.6 1.9 convolution_convert_fusion.3
  187.6 0.9 copy.117.refs_7_
  188.4 1.8 slice.236
  192.9 6.2 %fusion.22 = (bf16[256,2048]{1,0:T(8,128)(2,1)S(1)}, f32[256,2048]{1,0:T(8,128)}) fusion(bf16[256,512]{1,0:T(8,128)(2,1)S(1)} %fusion.36.refs_9_, bf16[512,2048]{1,0:T(8,128)(2,1)S(1)} %pad_maximum_fusion.2.refs_16_), kind=kOutput, calls=%fused_computation.77 | convolution fusion | flops 570949632 | bytes 5505024 | tf_op jit(solution)/shard_map/blk,kn->bln/dot_general | solution.py:914
  199.1 0.8 fusion.65
  201.0 0.7 gather_fusion
  201.7 0.7 select_convert_fusion.source
  202.4 30.5 %shard_map.492 = bf16[16,2,64,512]{3,2,1,0:T(8,128)(2,1)} custom-call(bf16[64,512]{1,0:T(8,128)(2,1)} %select_convert_fusion.source), custom_call_target="tpu_custom_call" | custom-call | tf_op jit(solution)/shard_map/pallas_call | solution.py:200
  232.9 7.5 %shard_map.493 = (f32[1,960,2048]{2,1,0:T(8,128)}, f32[1,4,2048]{2,1,0:T(4,128)}) custom-call(s32[1,2048]{1,0:T(1,128)} %sub.211.labels, bf16[32,1,64,512]{3,2,1,0:T(8,128)(2,1)} %bitcast.217, bf16[1,960,512]{2,1,0:T(8,128)(2,1)} %convert_bitcast_fusion.5.head), custom_call_target="tpu_custom_call" | custom-call | tf_op jit(solution)/shard_map/pallas_call | solution.py:434
  240.5 1.2 pad_maximum_fusion.3.refs_14_
  241.7 28.5 %shard_map.491 = (f32[4,960,2048]{2,1,0:T(8,128)}, f32[4,4,2048]{2,1,0:T(4,128)}) custom-call(s32[1,2048]{1,0:T(1,128)} %sub.211.labels, bf16[32,4,64,768]{3,2,1,0:T(8,128)(2,1)} %bitcast.234, bf16[4,960,768]{2,1,0:T(8,128)(2,1)} %all-gather.5.cloned.1.call-done.head), custom_call_target="tpu_custom_call" | custom-call | tf_op jit(solution)/shard_map/pallas_call | solution.py:434
  270.3 1.6 pad_maximum_fusion.5.stats
  271.9 19.2 %shard_map.494 = (f32[16,8,128]{2,1,0:T(8,128)}, f32[8,128]{1,0:T(8,128)}) custom-call(f32[5,4,2048]{2,1,0:T(4,128)} %pad_maximum_fusion.5.stats, f32[1,128]{1,0:T(1,128)} %fusion.46.counted_ref), custom_call_target="tpu_custom_call" | custom-call | tf_op jit(solution)/shard_map/pallas_call | solution.py:522
  291.1 0.8 copy-done.22
  292.0 17.7 %shard_map.495 = (f32[960,512]{1,0:T(8,128)S(1)}, bf16[960,512]{1,0:T(8,128)(2,1)S(1)}, bf16[2048,512]{1,0:T(8,128)(2,1)S(1)}, f32[1,256]{1,0:T(1,128)S(1)}) custom-call(f32[4,960,2048]{2,1,0:T(8,128)} %get-tuple-element.579.logits, f32[1,960,2048]{2,1,0:T(8,128)} %get-tuple-element.582.z, f32[16,8,128]{2,1,0:T(8,128)S(1)} %copy-done.22, ...), custom_call_target="tpu_custom_call" | custom-call | tf_op jit(solution)/shard_map/pallas_call | solution.py:585
  309.7 18.3 %shard_map.496 = (f32[64,512]{1,0:T(8,128)S(1)}, f32[960,128]{1,0:T(8,128)}) custom-call(bf16[16,2,64,512]{3,2,1,0:T(8,128)(2,1)S(1)} %bitcast.225, f32[960,512]{1,0:T(8,128)S(1)} %get-tuple-element.587.refs_1_, bf16[960,512]{1,0:T(8,128)(2,1)S(1)} %get-tuple-element.588.refs_2_), custom_call_target="tpu_custom_call" | custom-call | tf_op jit(solution)/shard_map/pallas_call | solution.py:768
  328.1 62.0 %shard_map.497 = (bf16[208,512]{1,0:T(8,128)(2,1)S(1)}, bf16[32,4,32,128]{3,2,1,0:T(8,128)(2,1)S(1)}, bf16[256,512]{1,0:T(8,128)(2,1)}) custom-call(s32[1,1]{1,0:T(1,128)} %bitcast.216.refs_0_, s32[1,64]{1,0:T(1,128)S(1)} %copy-done.24, s32[1,256]{1,0:T(1,128)S(1)} %get-tuple-element.694.refs_2_, f32[64,512]{1,0:T(8,128)S(1)} %get-tuple-element.590.refs_3_, ...), custom_call_target="tpu_custom_call" | custom-call | tf_op jit(solution)/shard_map/pallas_call | solution.py:1129
  390.1 0.8 while.29
  391.0 28.8 %shard_map.498 = (bf16[960,512]{1,0:T(8,128)(2,1)S(1)}, bf16[208,512]{1,0:T(8,128)(2,1)S(1)}, f32[32,16,128]{2,1,0:T(8,128)S(1)}) custom-call(f32[960,128]{1,0:T(8,128)} %get-tuple-element.592.head, s32[4,1024]{1,0:T(4,128)S(1)} %reshape_squeeze.4.wants, bf16[4,1024,128]{2,1,0:T(8,128)(2,1)S(1)} %bitcast.226, bf16[208,512]{1,0:T(8,128)(2,1)S(1)} %get-tuple-element.594.rest, ...), custom_call_target="tpu_custom_call" | custom-call | tf_op jit(solution)/shard_map/pallas_call | solution.py:848
  419.8 1.0 copy-done.19
  420.8 0.7 copy-done.20
  421.5 0.7 copy-done.21
  422.2 9.5 %shard_map.499 = (f32[1,1]{1,0:T(1,128)}, f32[1,1]{1,0:T(1,128)}, f32[8,128]{1,0:T(8,128)}, f32[960,512]{1,0:T(8,128)}, f32[8,512]{1,0:T(8,128)}, /*index=5*/f32...) custom-call(f32[32,16,128]{2,1,0:T(8,128)} %copy-done.20, ...), custom_call_target="tpu_custom_call" | custom-call | tf_op jit(solution)/shard_map/pallas_call | solution.py:270
  431.6 1.2 slice.199
  (176 shorter events, 13.1 us)
Async XLA Ops:
  7.2 4.9 %copy-start.37 = (f32[64,512]{1,0:T(8,128)S(1)}, f32[64,512]{1,0:T(8,128)}, u32[]{:S(2)}) copy-start(f32[64,512]{1,0:T(8,128)} %refs_5_.1) | copy-start | bytes 393220
  7.2 6.4 %copy-start.24 = (s32[1,64]{1,0:T(1,128)S(1)}, s32[1,64]{1,0:T(1,128)}, u32[]{:S(2)}) copy-start(s32[1,64]{1,0:T(1,128)} %refs_1_.2) | copy-start | bytes 772
  7.2 6.4 %copy-start.52 = (s32[1,256]{1,0:T(1,128)S(1)}, s32[1,256]{1,0:T(1,128)}, u32[]{:S(2)}) copy-start(s32[1,256]{1,0:T(1,128)} %param.36) | copy-start | bytes 3076
  7.2 35.2 %copy-start.25 = (f32[960,512]{1,0:T(8,128)S(1)}, f32[960,512]{1,0:T(8,128)}, u32[]{:S(2)}) copy-start(f32[960,512]{1,0:T(8,128)} %refs_0_.1) | copy-start | bytes 5898244
  7.2 152.6 %all-gather.5.cloned.1.call-start = ((), (), s32[]{:S(2)}) async-start(), calls=%async_computation.5 | async-start | bytes 7372800 | tf_op jit(solution)/shard_map/all_gather | solution.py:1334
  8.0 164.6 %all-gather.7.cloned.1.call-start = ((), (), s32[]{:S(2)}) async-start(), calls=%async_computation.6 | async-start | bytes 7028736 | tf_op jit(solution)/shard_map/all_gather | solution.py:1331
  12.1 0.7 copy-start.44
  12.8 228.9 %all-gather.9.cloned.1.call-start = ((), (), s32[]{:S(2)}) async-start(), calls=%async_computation.7 | async-start | bytes 12976128 | tf_op jit(solution)/shard_map/all_gather | solution.py:1352
  22.2 21.7 %copy-start.27 = (bf16[1,960,768]{2,1,0:T(8,128)(2,1)S(1)}, bf16[1,960,768]{2,1,0:T(8,128)(2,1)}, u32[]{:S(2)}) copy-start(bf16[1,960,768]{2,1,0:T(8,128)(2,1)} %param.61) | copy-start | bytes 4423684
  23.3 11.6 %copy-start.45 = (pred[1024]{0:T(1024)(128)(4,1)}, pred[1024]{0:T(1024)(128)(4,1)S(1)}, u32[]{:S(2)}) copy-start(pred[1024]{0:T(1024)(128)(4,1)S(1)} %not.18) | copy-start | bytes 3076
  41.5 2.1 copy-start.47
  41.5 2.1 copy-start.48
  42.5 1.1 copy-start.53
  42.5 1.2 copy-start.54
  43.6 63.5 %copy-start.50 = (s32[4,256,1]{1,0,2:T(4,128)S(1)}, s32[4,256,1]{1,0,2:T(4,128)}, u32[]{:S(2)}) copy-start(s32[4,256,1]{1,0,2:T(4,128)} %get-tuple-element.697) | copy-start | bytes 12292
  43.6 64.6 %copy-start.51 = (s32[4,64,1]{1,0,2:T(4,128)S(1)}, s32[4,64,1]{1,0,2:T(4,128)}, u32[]{:S(2)}) copy-start(s32[4,64,1]{1,0,2:T(4,128)} %slice_bitcast_fusion.7) | copy-start | bytes 3076
  43.9 67.0 %copy-start.46 = (pred[1024]{0:T(1024)(128)(4,1)S(1)}, pred[1024]{0:T(1024)(128)(4,1)}, u32[]{:S(2)}) copy-start(pred[1024]{0:T(1024)(128)(4,1)} %copy-done.45) | copy-start | bytes 3076
  104.1 1.8 copy-start.6
  120.1 50.0 %copy-start.26 = (f32[960,512]{1,0:T(8,128)S(1)}, f32[960,512]{1,0:T(8,128)}, u32[]{:S(2)}) copy-start(f32[960,512]{1,0:T(8,128)} %refs_0_.1) | copy-start | bytes 5898244
  171.2 2.3 copy-start.43
  179.5 0.8 copy-start.29
  179.5 1.0 copy-start.31
  179.5 10.7 %copy-start.7 = (bf16[32,16,512]{2,1,0:T(8,128)(2,1)}, bf16[32,16,512]{2,1,0:T(8,128)(2,1)S(1)}, u32[]{:S(2)}) copy-start(bf16[32,16,512]{2,1,0:T(8,128)(2,1)S(1)} %get-tuple-element.722) | copy-start | bytes 1572868
  180.5 5.1 %copy-start.11 = (bf16[256,1536]{1,0:T(8,128)(2,1)}, bf16[256,1536]{1,0:T(8,128)(2,1)S(1)}, u32[]{:S(2)}) copy-start(bf16[256,1536]{1,0:T(8,128)(2,1)S(1)} %convolution_convert_fusion.2.refs_6_) | copy-start | bytes 2359300
  181.6 4.0 copy-start.40
  190.2 8.9 %copy-start.1 = (bf16[32,64,512]{2,1,0:T(8,128)(2,1)}, bf16[32,64,512]{2,1,0:T(8,128)(2,1)S(1)}, u32[]{:S(2)}) copy-start(bf16[32,64,512]{2,1,0:T(8,128)(2,1)S(1)} %slice.236) | copy-start | bytes 6291460
  190.2 1.4 copy-start.33
  190.2 1.9 copy-start.34
  190.2 2.2 copy-start.35
  190.3 2.3 copy-start.36
  191.1 1.8 copy-start.16
  192.9 6.2 %copy-start.3 = (bf16[512,2048]{1,0:T(8,128)(2,1)}, bf16[512,2048]{1,0:T(8,128)(2,1)S(1)}, u32[]{:S(2)}) copy-start(bf16[512,2048]{1,0:T(8,128)(2,1)S(1)} %pad_maximum_fusion.2.refs_16_) | copy-start | bytes 6291460
  199.1 1.0 copy-start.14
  200.1 0.8 copy-start.9
  202.4 38.0 %copy-start.30 = (bf16[32,16,512]{2,1,0:T(8,128)(2,1)S(1)}, bf16[32,16,512]{2,1,0:T(8,128)(2,1)}, u32[]{:S(2)}) copy-start(bf16[32,16,512]{2,1,0:T(8,128)(2,1)} %copy-done.29) | copy-start | bytes 1572868
  202.4 38.0 %copy-start.32 = (bf16[32,16,512]{2,1,0:T(8,128)(2,1)S(1)}, bf16[32,16,512]{2,1,0:T(8,128)(2,1)}, u32[]{:S(2)}) copy-start(bf16[32,16,512]{2,1,0:T(8,128)(2,1)} %copy-done.31) | copy-start | bytes 1572868
  241.7 28.6 %copy-start.49 = (f32[1,4,2048]{2,1,0:T(4,128)S(1)}, f32[1,4,2048]{2,1,0:T(4,128)}, u32[]{:S(2)}) copy-start(f32[1,4,2048]{2,1,0:T(4,128)} %get-tuple-element.584) | copy-start | bytes 98308
  241.7 49.4 %copy-start = (bf16[16,2,64,512]{3,2,1,0:T(8,128)(2,1)S(1)}, bf16[16,2,64,512]{3,2,1,0:T(8,128)(2,1)}, u32[]{:S(2)}) copy-start(bf16[16,2,64,512]{3,2,1,0:T(8,128)(2,1)} %shard_map.492) | copy-start | bytes 6291460
  291.1 0.8 copy-start.22
  292.0 36.0 %copy-start.5 = (bf16[512,1536]{1,0:T(8,128)(2,1)S(1)}, bf16[512,1536]{1,0:T(8,128)(2,1)}, u32[]{:S(2)}) copy-start(bf16[512,1536]{1,0:T(8,128)(2,1)} %pad_maximum_fusion.3.refs_14_) | copy-start | bytes 4718596
  292.0 36.1 %copy-start.10 = (f32[256,512]{1,0:T(8,128)S(1)}, f32[256,512]{1,0:T(8,128)}, u32[]{:S(2)}) copy-start(f32[256,512]{1,0:T(8,128)} %copy-done.9) | copy-start | bytes 1572868
  292.0 36.1 %copy-start.12 = (bf16[256,1536]{1,0:T(8,128)(2,1)S(1)}, bf16[256,1536]{1,0:T(8,128)(2,1)}, u32[]{:S(2)}) copy-start(bf16[256,1536]{1,0:T(8,128)(2,1)} %copy-done.11) | copy-start | bytes 2359300
  292.0 36.1 %copy-start.13 = (f32[256,2048]{1,0:T(8,128)S(1)}, f32[256,2048]{1,0:T(8,128)}, u32[]{:S(2)}) copy-start(f32[256,2048]{1,0:T(8,128)} %get-tuple-element.756.refs_10_) | copy-start | bytes 6291460
  292.0 36.1 %copy-start.15 = (bf16[256,2048]{1,0:T(8,128)(2,1)S(1)}, bf16[256,2048]{1,0:T(8,128)(2,1)}, u32[]{:S(2)}) copy-start(bf16[256,2048]{1,0:T(8,128)(2,1)} %copy-done.14) | copy-start | bytes 3145732
  292.0 36.1 %copy-start.18 = (bf16[256,512]{1,0:T(8,128)(2,1)S(1)}, bf16[256,512]{1,0:T(8,128)(2,1)}, u32[]{:S(2)}) copy-start(bf16[256,512]{1,0:T(8,128)(2,1)} %copy.117.refs_7_) | copy-start | bytes 786436
  309.7 18.4 %copy-start.2 = (bf16[32,64,512]{2,1,0:T(8,128)(2,1)S(1)}, bf16[32,64,512]{2,1,0:T(8,128)(2,1)}, u32[]{:S(2)}) copy-start(bf16[32,64,512]{2,1,0:T(8,128)(2,1)} %copy-done.1) | copy-start | bytes 6291460
  309.7 18.4 %copy-start.4 = (bf16[512,2048]{1,0:T(8,128)(2,1)S(1)}, bf16[512,2048]{1,0:T(8,128)(2,1)}, u32[]{:S(2)}) copy-start(bf16[512,2048]{1,0:T(8,128)(2,1)} %copy-done.3) | copy-start | bytes 6291460
  309.7 18.4 %copy-start.8 = (bf16[32,16,512]{2,1,0:T(8,128)(2,1)S(1)}, bf16[32,16,512]{2,1,0:T(8,128)(2,1)}, u32[]{:S(2)}) copy-start(bf16[32,16,512]{2,1,0:T(8,128)(2,1)} %copy-done.7) | copy-start | bytes 1572868
  309.7 18.4 %copy-start.17 = (bf16[256,512]{1,0:T(8,128)(2,1)S(1)}, bf16[256,512]{1,0:T(8,128)(2,1)}, u32[]{:S(2)}) copy-start(bf16[256,512]{1,0:T(8,128)(2,1)} %copy-done.16) | copy-start | bytes 786436
  390.1 0.8 copy-start.23
  419.8 1.0 copy-start.19
  420.8 0.7 copy-start.20
  421.5 0.7 copy-start.21
Sparse Core Ops, SparseCore 0:
  9.7 65.8 all-gather.4
  77.9 58.2 all-gather.6
  168.5 72.3 all-gather.8

commit v7 on v6

--- a/solution.py
+++ b/solution.py
@@ -142,7 +142,7 @@
             pltpu.SemaphoreType.DMA,
         ],
         compiler_params=pltpu.CompilerParams(
-            collective_id=collective, has_side_effects=True, vmem_limit_bytes=40 * 2**20
+            collective_id=collective, has_side_effects=True, vmem_limit_bytes=WIDE
         ),
     )(notes, t_table, s_table)
 

time: 446 us -> 437 us (0.980)
  local copies, waits for them, and re-layouts: 33.2 us -> 27 us
    unnamed x110 -> x96, local copies, waits for them, and re-layouts: 9.2 us -> 7.41 us
  transfers between devices with their start and end apart: 3 -> 3, of which waited for: 0 -> 0; matrix products, arithmetic and copies ran while one was open for 14% -> 12% of each run, Pallas kernels for 35% -> 36%
where the time goes in v7:
time: 437 us; the launch traced here: 430 us
  Pallas kernels  338 us (77%)
  local copies, waits for them, and re-layouts  27 us (6%)
  other arithmetic  20.2 us (5%)
  between operations  19.5 us (4%)
  matrix products  14.4 us (3%)
  loops' own time  10.3 us (2%)
    pallas_call x1, Pallas kernels, backward(): pl.pallas_call(partial(finish_kernel, plan), out_shape=[jax.ShapeDtypeStr...  61.7 us
    pallas_call x1, Pallas kernels, route(): pl.pallas_call(route_kernel, out_shape=[jax.ShapeDtypeStruct(notes.shape,...  58.6 us
    pallas_call x1, Pallas kernels, teacher_rows(): pl.pallas_call(teacher_kernel, grid=(count,), out_shape=jax.ShapeDtypeStr...  40 us
    pallas_call x2, Pallas kernels, vocabulary_logits(): pl.pallas_call(logits_kernel, grid=(count, devices // block), out_shape=[...  36.2 us
    pallas_call x1, Pallas kernels, gather_plane(): pl.pallas_call(gather_kernel, out_shape=jax.ShapeDtypeStruct((16, 2, rows...  32.7 us
    pallas_call x1, Pallas kernels, sum_of_groups(): pl.pallas_call(group_sum_kernel, out_shape=[jax.ShapeDtypeStruct((head.sh...  29 us
    pallas_call x1, Pallas kernels, blend(): pl.pallas_call(blend_kernel, out_shape=[jax.ShapeDtypeStruct((16, 8, 128)...  18.9 us
    pallas_call x1, Pallas kernels, scatter_head(): pl.pallas_call(partial(scatter_sum_kernel, [(rows, width)], 'head'), out_...  18.4 us
  transfers between devices with their start and end apart: 3, of which 0 were waited for; matrix products, arithmetic and copies ran while one was open for 12% of the time, Pallas kernels for 36%

profile of v7, /device:TPU:1, one launch (start us, length us, event | category | flops | bytes accessed | tf_op | source)
XLA Modules:
  0.0 430.4 jit_solution(10831895913838499961)
XLA Ops:
  7.3 0.7 all-gather.5.cloned.1.call-update
  8.0 0.7 convert_bitcast_fusion.4
  8.7 0.7 convert_bitcast_fusion.3
  9.4 0.9 convert_bitcast_fusion.2
  10.4 0.8 constant_dynamic-update-slice_fusion.5
  11.1 0.9 convert_bitcast_fusion.1
  12.1 0.7 copy-done.43
  13.7 0.6 broadcast_in_dim.255.source
  14.3 7.2 %shard_map.487 = s32[4,8,128]{2,1,0:T(8,128)} custom-call(s32[4,8,128]{2,1,0:T(8,128)} %broadcast_in_dim.255.source), custom_call_target="tpu_custom_call" | custom-call | tf_op jit(solution)/shard_map/pallas_call | solution.py:166
  21.5 0.7 slice_bitcast_fusion.6
  22.7 1.2 convert_reduce_fusion
  23.9 0.6 fusion.61
  27.1 0.6 fusion.60
  29.7 0.7 slice_reduce_fusion.4
  30.4 0.6 select_reduce_fusion.5
  31.2 0.8 select_reduce_fusion.4
  32.7 0.8 stack.46.notes
  33.5 58.6 %shard_map.488 = (s32[32,8,128]{2,1,0:T(8,128)}, bf16[32,48,1024]{2,1,0:T(8,128)(2,1)}) custom-call(s32[32,8,128]{2,1,0:T(8,128)} %stack.46.notes, bf16[960,768]{1,0:T(8,128)(2,1)} %bitcast.236, bf16[960,512]{1,0:T(8,128)(2,1)S(1)} %convert_element_type.160.s_table.table), custom_call_target="tpu_custom_call" | custom-call | tf_op jit(solution)/shard_map/pallas_call | solution.py:129
  92.1 2.3 slice_reduce_fusion.1
  94.5 1.0 copy.109.slot
  95.5 0.8 copy.110.picks
  96.2 1.2 broadcast_in_dim.263
  97.5 9.4 %while.28 = (s32[]{:T(128)}, bf16[1024,768]{1,0:T(8,128)(2,1)}, bf16[256,512]{1,0:T(8,128)(2,1)S(1)}, s32[]{:T(128)}, s32[1024]{0:T(1024)S(1)}, /*index=5*/s32[1...) while((s32[]{:T(128)}, bf16[1024,768]{1,0:T(8,128)(2,1)}, ...), condition=%wide.region_12.13_spmd, body=%wide.region_9.12_spmd.sunk | while | flops 5663440896 | bytes 45958452 | solution.py:1283
  107.0 40.0 %shard_map.489.source = bf16[4,64,768]{2,1,0:T(8,128)(2,1)} custom-call(s32[1,4]{1,0:T(1,128)} %bitcast.294, s32[4,256,1]{2,1,0:T(8,128)} %copy.109.slot, s32[4,64,1]{2,1,0:T(8,128)} %copy.110.picks, bf16[1536,1024]{1,0:T(8,128)(2,1)} %bitcast.237, bf16[4,256,768]{2,1,0:T(8,128)(2,1)} %bitcast.30.extra, bf16[256,768]{1,0:T(8,128)(2,1)} %bitcast.260, ...), custom_call_target="tpu_custom_call" | custom-call | tf_op jit(solution)/shard_map/pallas_call | solution.py:355
  147.0 8.3 %shard_map.490 = bf16[4,64,768]{2,1,0:T(8,128)(2,1)} custom-call(bf16[4,64,768]{2,1,0:T(8,128)(2,1)} %shard_map.489.source), custom_call_target="tpu_custom_call" | custom-call | tf_op jit(solution)/shard_map/pallas_call | solution.py:166
  155.3 1.1 slice_reduce_fusion.2
  156.4 0.7 sub.211.labels
  157.4 1.0 slice_reduce_fusion
  159.0 1.1 convert_bitcast_fusion.5.head
  160.0 1.2 fusion.56
  161.4 0.9 convert_bitcast_fusion
  162.4 1.5 fusion.62
  164.2 4.1 fusion.55
  168.4 0.6 convolution_convert_fusion.2.refs_6_
  169.4 0.9 copy.112
  170.5 0.8 copy.114
  171.3 3.1 fusion.63
  174.4 1.9 convolution_convert_fusion.3
  176.4 0.9 copy.117.refs_7_
  177.2 1.8 slice.236
  179.9 0.5 copy-done.33
  180.5 0.5 copy-done.34
  181.7 6.1 %fusion.22 = (bf16[256,2048]{1,0:T(8,128)(2,1)S(1)}, f32[256,2048]{1,0:T(8,128)}) fusion(bf16[256,512]{1,0:T(8,128)(2,1)S(1)} %fusion.36.refs_9_, bf16[512,2048]{1,0:T(8,128)(2,1)S(1)} %pad_maximum_fusion.2.refs_16_), kind=kOutput, calls=%fused_computation.77 | convolution fusion | flops 570949632 | bytes 5505024 | tf_op jit(solution)/shard_map/blk,kn->bln/dot_general | solution.py:914
  187.9 0.8 fusion.65
  189.1 0.6 copy-done.8
  189.8 0.7 gather_fusion
  190.5 0.7 select_convert_fusion.source
  191.2 32.7 %shard_map.492 = bf16[16,2,64,512]{3,2,1,0:T(8,128)(2,1)} custom-call(bf16[64,512]{1,0:T(8,128)(2,1)} %select_convert_fusion.source), custom_call_target="tpu_custom_call" | custom-call | tf_op jit(solution)/shard_map/pallas_call | solution.py:200
  224.0 7.6 %shard_map.493 = (f32[1,960,2048]{2,1,0:T(8,128)}, f32[1,4,2048]{2,1,0:T(4,128)}) custom-call(s32[1,2048]{1,0:T(1,128)} %sub.211.labels, bf16[32,1,64,512]{3,2,1,0:T(8,128)(2,1)} %bitcast.217, bf16[1,960,512]{2,1,0:T(8,128)(2,1)} %convert_bitcast_fusion.5.head), custom_call_target="tpu_custom_call" | custom-call | tf_op jit(solution)/shard_map/pallas_call | solution.py:434
  231.6 1.2 pad_maximum_fusion.3.refs_14_
  232.8 28.6 %shard_map.491 = (f32[4,960,2048]{2,1,0:T(8,128)}, f32[4,4,2048]{2,1,0:T(4,128)}) custom-call(s32[1,2048]{1,0:T(1,128)} %sub.211.labels, bf16[32,4,64,768]{3,2,1,0:T(8,128)(2,1)} %bitcast.233, bf16[4,960,768]{2,1,0:T(8,128)(2,1)} %all-gather.5.cloned.1.call-done.head), custom_call_target="tpu_custom_call" | custom-call | tf_op jit(solution)/shard_map/pallas_call | solution.py:434
  261.4 1.6 pad_maximum_fusion.5.stats
  263.0 18.9 %shard_map.494 = (f32[16,8,128]{2,1,0:T(8,128)}, f32[8,128]{1,0:T(8,128)}) custom-call(f32[5,4,2048]{2,1,0:T(4,128)} %pad_maximum_fusion.5.stats, f32[1,128]{1,0:T(1,128)} %fusion.46.counted_ref), custom_call_target="tpu_custom_call" | custom-call | tf_op jit(solution)/shard_map/pallas_call | solution.py:522
  281.9 0.8 copy-done.21
  282.8 17.7 %shard_map.495 = (f32[960,512]{1,0:T(8,128)S(1)}, bf16[960,512]{1,0:T(8,128)(2,1)S(1)}, bf16[2048,512]{1,0:T(8,128)(2,1)S(1)}, f32[1,256]{1,0:T(1,128)S(1)}) custom-call(f32[4,960,2048]{2,1,0:T(8,128)} %get-tuple-element.579.logits, f32[1,960,2048]{2,1,0:T(8,128)} %get-tuple-element.582.z, f32[16,8,128]{2,1,0:T(8,128)S(1)} %copy-done.21, ...), custom_call_target="tpu_custom_call" | custom-call | tf_op jit(solution)/shard_map/pallas_call | solution.py:585
  300.5 18.4 %shard_map.496 = (f32[64,512]{1,0:T(8,128)S(1)}, f32[960,128]{1,0:T(8,128)}) custom-call(bf16[16,2,64,512]{3,2,1,0:T(8,128)(2,1)S(1)} %bitcast.224, f32[960,512]{1,0:T(8,128)S(1)} %get-tuple-element.587.refs_1_, bf16[960,512]{1,0:T(8,128)(2,1)S(1)} %get-tuple-element.588.refs_2_), custom_call_target="tpu_custom_call" | custom-call | tf_op jit(solution)/shard_map/pallas_call | solution.py:768
  319.0 61.7 %shard_map.497 = (bf16[208,512]{1,0:T(8,128)(2,1)S(1)}, bf16[32,4,32,128]{3,2,1,0:T(8,128)(2,1)S(1)}, bf16[256,512]{1,0:T(8,128)(2,1)}) custom-call(s32[1,1]{1,0:T(1,128)} %bitcast.216.refs_0_, s32[1,64]{1,0:T(1,128)S(1)} %copy-done.23, s32[1,256]{1,0:T(1,128)S(1)} %get-tuple-element.694.refs_2_, f32[64,512]{1,0:T(8,128)S(1)} %get-tuple-element.590.refs_3_, ...), custom_call_target="tpu_custom_call" | custom-call | tf_op jit(solution)/shard_map/pallas_call | solution.py:1129
  380.6 0.9 while.29
  381.6 29.0 %shard_map.498 = (bf16[960,512]{1,0:T(8,128)(2,1)S(1)}, bf16[208,512]{1,0:T(8,128)(2,1)S(1)}, f32[32,16,128]{2,1,0:T(8,128)S(1)}) custom-call(f32[960,128]{1,0:T(8,128)} %get-tuple-element.592.head, s32[4,1024]{1,0:T(4,128)S(1)} %reshape_squeeze.4.wants, bf16[4,1024,128]{2,1,0:T(8,128)(2,1)S(1)} %bitcast.225, bf16[208,512]{1,0:T(8,128)(2,1)S(1)} %get-tuple-element.594.rest, ...), custom_call_target="tpu_custom_call" | custom-call | tf_op jit(solution)/shard_map/pallas_call | solution.py:848
  410.6 1.0 copy-done.18
  411.5 0.7 copy-done.19
  412.3 0.7 copy-done.20
  412.9 9.5 %shard_map.499 = (f32[1,1]{1,0:T(1,128)}, f32[1,1]{1,0:T(1,128)}, f32[8,128]{1,0:T(8,128)}, f32[960,512]{1,0:T(8,128)}, f32[8,512]{1,0:T(8,128)}, /*index=5*/f32...) custom-call(f32[32,16,128]{2,1,0:T(8,128)} %copy-done.19, ...), custom_call_target="tpu_custom_call" | custom-call | tf_op jit(solution)/shard_map/pallas_call | solution.py:270
  422.4 1.2 slice.199
  (162 shorter events, 6.4 us)
Async XLA Ops:
  7.2 4.9 %copy-start.37 = (f32[64,512]{1,0:T(8,128)S(1)}, f32[64,512]{1,0:T(8,128)}, u32[]{:S(2)}) copy-start(f32[64,512]{1,0:T(8,128)} %refs_5_.1) | copy-start | bytes 393220
  7.2 6.4 %copy-start.23 = (s32[1,64]{1,0:T(1,128)S(1)}, s32[1,64]{1,0:T(1,128)}, u32[]{:S(2)}) copy-start(s32[1,64]{1,0:T(1,128)} %refs_1_.2) | copy-start | bytes 772
  7.2 6.4 %copy-start.45 = (s32[1,256]{1,0:T(1,128)S(1)}, s32[1,256]{1,0:T(1,128)}, u32[]{:S(2)}) copy-start(s32[1,256]{1,0:T(1,128)} %param.36) | copy-start | bytes 3076
  7.2 25.0 %copy-start.46 = (s32[1,64]{1,0:T(1,128)S(1)}, s32[1,64]{1,0:T(1,128)}, u32[]{:S(2)}) copy-start(s32[1,64]{1,0:T(1,128)} %param.39) | copy-start | bytes 772
  7.2 25.2 %copy-start.24 = (f32[960,512]{1,0:T(8,128)S(1)}, f32[960,512]{1,0:T(8,128)}, u32[]{:S(2)}) copy-start(f32[960,512]{1,0:T(8,128)} %refs_0_.1) | copy-start | bytes 5898244
  7.2 139.7 %all-gather.5.cloned.1.call-start = ((), (), s32[]{:S(2)}) async-start(), calls=%async_computation.5 | async-start | bytes 7372800 | tf_op jit(solution)/shard_map/all_gather | solution.py:1334
  8.0 153.4 %all-gather.7.cloned.1.call-start = ((), (), s32[]{:S(2)}) async-start(), calls=%async_computation.6 | async-start | bytes 7028736 | tf_op jit(solution)/shard_map/all_gather | solution.py:1331
  12.1 0.7 copy-start.43
  12.9 220.0 %all-gather.9.cloned.1.call-start = ((), (), s32[]{:S(2)}) async-start(), calls=%async_computation.7 | async-start | bytes 12976128 | tf_op jit(solution)/shard_map/all_gather | solution.py:1352
  106.9 40.0 %copy-start.28 = (bf16[960,512]{1,0:T(8,128)(2,1)}, bf16[960,512]{1,0:T(8,128)(2,1)S(1)}, u32[]{:S(2)}) copy-start(bf16[960,512]{1,0:T(8,128)(2,1)S(1)} %get-tuple-element.1110) | copy-start | bytes 2949124
  106.9 40.0 %copy-start.41 = (bf16[256,512]{1,0:T(8,128)(2,1)}, bf16[256,512]{1,0:T(8,128)(2,1)S(1)}, u32[]{:S(2)}) copy-start(bf16[256,512]{1,0:T(8,128)(2,1)S(1)} %get-tuple-element.581) | copy-start | bytes 786436
  106.9 52.0 %copy-start.25 = (f32[960,512]{1,0:T(8,128)S(1)}, f32[960,512]{1,0:T(8,128)}, u32[]{:S(2)}) copy-start(f32[960,512]{1,0:T(8,128)} %refs_0_.1) | copy-start | bytes 5898244
  160.0 2.3 copy-start.42
  168.4 0.8 copy-start.29
  168.4 1.0 copy-start.31
  168.4 10.8 %copy-start.6 = (bf16[32,16,512]{2,1,0:T(8,128)(2,1)}, bf16[32,16,512]{2,1,0:T(8,128)(2,1)S(1)}, u32[]{:S(2)}) copy-start(bf16[32,16,512]{2,1,0:T(8,128)(2,1)S(1)} %get-tuple-element.722) | copy-start | bytes 1572868
  169.3 5.1 %copy-start.10 = (bf16[256,1536]{1,0:T(8,128)(2,1)}, bf16[256,1536]{1,0:T(8,128)(2,1)S(1)}, u32[]{:S(2)}) copy-start(bf16[256,1536]{1,0:T(8,128)(2,1)S(1)} %convolution_convert_fusion.2.refs_6_) | copy-start | bytes 2359300
  170.5 4.0 copy-start.40
  179.1 8.8 %copy-start.1 = (bf16[32,64,512]{2,1,0:T(8,128)(2,1)}, bf16[32,64,512]{2,1,0:T(8,128)(2,1)S(1)}, u32[]{:S(2)}) copy-start(bf16[32,64,512]{2,1,0:T(8,128)(2,1)S(1)} %slice.236) | copy-start | bytes 6291460
  179.1 1.4 copy-start.33
  179.1 1.9 copy-start.34
  179.1 2.2 copy-start.35
  179.1 2.3 copy-start.36
  179.9 1.8 copy-start.15
  181.7 6.1 %copy-start.3 = (bf16[512,2048]{1,0:T(8,128)(2,1)}, bf16[512,2048]{1,0:T(8,128)(2,1)S(1)}, u32[]{:S(2)}) copy-start(bf16[512,2048]{1,0:T(8,128)(2,1)S(1)} %pad_maximum_fusion.2.refs_16_) | copy-start | bytes 6291460
  187.9 1.0 copy-start.13
  188.8 0.8 copy-start.8
  191.2 40.4 %copy-start.30 = (bf16[32,16,512]{2,1,0:T(8,128)(2,1)S(1)}, bf16[32,16,512]{2,1,0:T(8,128)(2,1)}, u32[]{:S(2)}) copy-start(bf16[32,16,512]{2,1,0:T(8,128)(2,1)} %copy-done.29) | copy-start | bytes 1572868
  191.2 40.4 %copy-start.32 = (bf16[32,16,512]{2,1,0:T(8,128)(2,1)S(1)}, bf16[32,16,512]{2,1,0:T(8,128)(2,1)}, u32[]{:S(2)}) copy-start(bf16[32,16,512]{2,1,0:T(8,128)(2,1)} %copy-done.31) | copy-start | bytes 1572868
  232.8 28.6 %copy-start.44 = (f32[1,4,2048]{2,1,0:T(4,128)S(1)}, f32[1,4,2048]{2,1,0:T(4,128)}, u32[]{:S(2)}) copy-start(f32[1,4,2048]{2,1,0:T(4,128)} %get-tuple-element.584) | copy-start | bytes 98308
  232.8 49.0 %copy-start = (bf16[16,2,64,512]{3,2,1,0:T(8,128)(2,1)S(1)}, bf16[16,2,64,512]{3,2,1,0:T(8,128)(2,1)}, u32[]{:S(2)}) copy-start(bf16[16,2,64,512]{3,2,1,0:T(8,128)(2,1)} %shard_map.492) | copy-start | bytes 6291460
  281.9 0.8 copy-start.21
  282.7 36.1 %copy-start.5 = (bf16[512,1536]{1,0:T(8,128)(2,1)S(1)}, bf16[512,1536]{1,0:T(8,128)(2,1)}, u32[]{:S(2)}) copy-start(bf16[512,1536]{1,0:T(8,128)(2,1)} %pad_maximum_fusion.3.refs_14_) | copy-start | bytes 4718596
  282.7 36.2 %copy-start.9 = (f32[256,512]{1,0:T(8,128)S(1)}, f32[256,512]{1,0:T(8,128)}, u32[]{:S(2)}) copy-start(f32[256,512]{1,0:T(8,128)} %copy-done.8) | copy-start | bytes 1572868
  282.7 36.2 %copy-start.11 = (bf16[256,1536]{1,0:T(8,128)(2,1)S(1)}, bf16[256,1536]{1,0:T(8,128)(2,1)}, u32[]{:S(2)}) copy-start(bf16[256,1536]{1,0:T(8,128)(2,1)} %copy-done.10) | copy-start | bytes 2359300
  282.7 36.2 %copy-start.12 = (f32[256,2048]{1,0:T(8,128)S(1)}, f32[256,2048]{1,0:T(8,128)}, u32[]{:S(2)}) copy-start(f32[256,2048]{1,0:T(8,128)} %get-tuple-element.756.refs_10_) | copy-start | bytes 6291460
  282.7 36.2 %copy-start.14 = (bf16[256,2048]{1,0:T(8,128)(2,1)S(1)}, bf16[256,2048]{1,0:T(8,128)(2,1)}, u32[]{:S(2)}) copy-start(bf16[256,2048]{1,0:T(8,128)(2,1)} %copy-done.13) | copy-start | bytes 3145732
  282.7 36.2 %copy-start.17 = (bf16[256,512]{1,0:T(8,128)(2,1)S(1)}, bf16[256,512]{1,0:T(8,128)(2,1)}, u32[]{:S(2)}) copy-start(bf16[256,512]{1,0:T(8,128)(2,1)} %copy.117.refs_7_) | copy-start | bytes 786436
  300.4 18.5 %copy-start.2 = (bf16[32,64,512]{2,1,0:T(8,128)(2,1)S(1)}, bf16[32,64,512]{2,1,0:T(8,128)(2,1)}, u32[]{:S(2)}) copy-start(bf16[32,64,512]{2,1,0:T(8,128)(2,1)} %copy-done.1) | copy-start | bytes 6291460
  300.4 18.5 %copy-start.4 = (bf16[512,2048]{1,0:T(8,128)(2,1)S(1)}, bf16[512,2048]{1,0:T(8,128)(2,1)}, u32[]{:S(2)}) copy-start(bf16[512,2048]{1,0:T(8,128)(2,1)} %copy-done.3) | copy-start | bytes 6291460
  300.4 18.5 %copy-start.7 = (bf16[32,16,512]{2,1,0:T(8,128)(2,1)S(1)}, bf16[32,16,512]{2,1,0:T(8,128)(2,1)}, u32[]{:S(2)}) copy-start(bf16[32,16,512]{2,1,0:T(8,128)(2,1)} %copy-done.6) | copy-start | bytes 1572868
  300.5 18.5 %copy-start.16 = (bf16[256,512]{1,0:T(8,128)(2,1)S(1)}, bf16[256,512]{1,0:T(8,128)(2,1)}, u32[]{:S(2)}) copy-start(bf16[256,512]{1,0:T(8,128)(2,1)} %copy-done.15) | copy-start | bytes 786436
  380.6 0.9 copy-start.22
  410.6 1.0 copy-start.18
  411.5 0.7 copy-start.19
  412.3 0.7 copy-start.20
Sparse Core Ops, SparseCore 0:
  9.7 65.8 all-gather.4
  77.9 50.7 all-gather.6
  155.4 74.8 all-gather.8
